TPU v7x, 32 devices: a whole 2x2x4 slice. The times are simulated.
32 devices in a mesh: dp: 8 (over y, x, core), tensor: 4 (over z).
Axes of the slice: x: 2, y: 2, z: 4, core: 2. Of those that a mesh axis runs over, the one named last changes fastest.
Arguments:
- tokens: bfloat16 [16384, 2048], P(('dp', 'tensor')), may hold values from -8 to 8
- segments: int32 [8, 2048], P('dp'), may hold values from 0 to 7, never falling along the last dimension, each value on 1 to 800 neighbouring positions
- norm_gain: float32 [2048], replicated, may hold values from 0.5 to 1.5
- norm_shift: float32 [2048], replicated, may hold values from -4 to 4
- qkv_weight: bfloat16 [3, 2048, 2048], P(None, 'dp', 'tensor'), may hold values from -1 to 1
- qkv_bias: bfloat16 [3, 2048], P(None, ('tensor', 'dp')), may hold values from -6 to 6
- dense_weight: bfloat16 [2048, 2048], P('tensor', 'dp'), may hold values from -0.5 to 0.5
- up_weight: bfloat16 [2048, 8192], P('dp', 'tensor'), may hold values from -1 to 1
- up_bias: bfloat16 [8192], P(('tensor', 'dp')), may hold values from -6 to 6
- down_weight: bfloat16 [8192, 2048], P('tensor', 'dp'), may hold values from -0.0625 to 0.0625
- out_bias: float32 [2048], replicated, may hold values from -6 to 6
- cotangent: bfloat16 [16384, 2048], P(('dp', 'tensor')), may hold values from -6 to 6
Outputs:
- output: bfloat16 [16384, 2048], P(('dp', 'tensor'))
- grad_tokens: bfloat16 [16384, 2048], P(('dp', 'tensor'))
- grad_norm_gain: float32 [2048], P(('dp', 'tensor'))
- grad_norm_shift: float32 [2048], P(('dp', 'tensor'))
- grad_qkv_weight: float32 [3, 2048, 2048], P(None, 'dp', 'tensor')
- grad_qkv_bias: float32 [3, 2048], P(None, ('tensor', 'dp'))
- grad_dense_weight: float32 [2048, 2048], P('tensor', 'dp')
- grad_up_weight: float32 [2048, 8192], P('dp', 'tensor')
- grad_up_bias: float32 [8192], P(('tensor', 'dp'))
- grad_down_weight: float32 [8192, 2048], P('tensor', 'dp')
- grad_out_bias: float32 [2048], P(('dp', 'tensor'))
- root_squares: float32 [3], replicated
Inputs may be any that keep to these rules, and one draw needn't show every extreme that they name: `segments`: within a sequence the numbers never fall; every number from 0 to 7 appears, each on 1 to 800 tokens, and one on exactly 800.
All inputs are finite; a program needn't handle non-finite values.
Results may differ from a plain program's by a relative error of at most 0.012.
The roundings to bfloat16 on the way count: a program that leaves them out, or rounds other values in their place, can miss the bound.
Values may be sent and summed in bfloat16 or wider, within the bound.
A program may use at most 640 MiB of HBM per device.

v0:
```python
import math

import jax
import jax.numpy as jnp
from jax import lax
from jax.sharding import PartitionSpec as P

HEAD_DIM = 64
ROT = 32


EPS = 1e-05
GELU_C = math.sqrt(2.0 / math.pi)


def positions_of(segs):
    count = segs.shape[-1]
    position = jnp.broadcast_to(jnp.arange(count, dtype=jnp.int32), segs.shape)
    first_flag = jnp.ones(segs.shape[:-1] + (1,), dtype=bool)
    change = jnp.concatenate([first_flag, segs[..., 1:] != segs[..., :-1]], axis=-1)
    seg_start = lax.cummax(
        jnp.where(change, position, jnp.zeros_like(position)), axis=segs.ndim - 1
    )
    return position - seg_start


def rotary_tables(segs):
    half_rot = ROT // 2
    frequency = jnp.exp(-math.log(10000.0) * (2.0 * jnp.arange(half_rot, dtype=jnp.float32) / ROT))
    angles = positions_of(segs).astype(jnp.float32)[..., None] * frequency
    return (jnp.cos(angles), jnp.sin(angles))


def rotate(values_in, cosines, sines, direction):
    half_rot = ROT // 2
    front_part = values_in[..., :half_rot]
    back_part = values_in[..., half_rot:ROT]
    cos_wide = cosines[..., None, :]
    sin_wide = sines[..., None, :]
    return jnp.concatenate(
        [
            front_part * cos_wide - direction * back_part * sin_wide,
            back_part * cos_wide + direction * front_part * sin_wide,
            values_in[..., ROT:],
        ],
        axis=-1,
    )


def gelu_value(u):
    tanh_value = jnp.tanh(GELU_C * (u + 0.044715 * u * u * u))
    return 0.5 * u * (1.0 + tanh_value)


def gelu_slope(u):
    tanh_value = jnp.tanh(GELU_C * (u + 0.044715 * u * u * u))
    return 0.5 * (1.0 + tanh_value) + 0.5 * u * (1.0 - tanh_value * tanh_value) * GELU_C * (
        1.0 + 3.0 * 0.044715 * u * u
    )


def contract_rows(left, right):
    return lax.dot_general(
        left, right, (((0,), (0,)), ((), ())), preferred_element_type=jnp.float32
    )


def contract_cols(left, right):
    return lax.dot_general(
        left, right, (((1,), (1,)), ((), ())), preferred_element_type=jnp.float32
    )


def masked_scores(query, keys, segments, seq_index, block_index, block):
    length = segments.shape[1]
    score_scale = 1.0 / math.sqrt(HEAD_DIM)
    query_seq = lax.dynamic_index_in_dim(query, seq_index, 0, keepdims=False)
    query_block = lax.dynamic_slice_in_dim(query_seq, block_index * block, block, 0)
    key_seq = lax.dynamic_index_in_dim(keys, seq_index, 0, keepdims=False)
    seg_row = lax.dynamic_index_in_dim(segments, seq_index, 0, keepdims=False)
    query_seg = lax.dynamic_slice_in_dim(seg_row, block_index * block, block, 0)
    query_pos = block_index * block + jnp.arange(block, dtype=jnp.int32)
    key_pos = jnp.arange(length, dtype=jnp.int32)
    allowed = (query_seg[:, None] == seg_row[None, :]) & (key_pos[None, :] <= query_pos[:, None])
    scores = (
        jnp.einsum("qhd,khd->hqk", query_block, key_seq, preferred_element_type=jnp.float32)
        * score_scale
    )
    return (jnp.where(allowed[None], scores, -jnp.inf), query_block, key_seq)


def attention_forward(query, keys, values, segments):
    seq_count, length, heads_dev, head_size = query.shape
    block = min(512, length)
    blocks = length // block

    def one_block(index_flat):
        seq_index = index_flat // blocks
        block_index = index_flat % blocks
        scores, query_block, key_seq = masked_scores(
            query, keys, segments, seq_index, block_index, block
        )
        row_top = jnp.max(scores, axis=-1, keepdims=True)
        exponent = jnp.exp(scores - row_top)
        row_total = jnp.sum(exponent, axis=-1, keepdims=True)
        prob_low = (exponent / row_total).astype(jnp.bfloat16)
        value_seq = lax.dynamic_index_in_dim(values, seq_index, 0, keepdims=False)
        block_out = jnp.einsum(
            "hqk,khd->qhd", prob_low, value_seq, preferred_element_type=jnp.float32
        )
        return (block_out, (row_top + jnp.log(row_total))[..., 0])

    block_outs, logsum = lax.map(one_block, jnp.arange(seq_count * blocks, dtype=jnp.int32))
    return (block_outs.reshape(seq_count * length, heads_dev * head_size), logsum)


def attention_backward(query, keys, values, segments, logsum, grad_out):
    seq_count, length, heads_dev, head_size = query.shape
    block = min(512, length)
    blocks = length // block
    score_scale = 1.0 / math.sqrt(HEAD_DIM)

    def per_seq(seq_index):
        value_seq = lax.dynamic_index_in_dim(values, seq_index, 0, keepdims=False)
        grad_seq = lax.dynamic_index_in_dim(grad_out, seq_index, 0, keepdims=False)

        def block_step(state, block_index):
            grad_key_acc, grad_value_acc = state
            scores, query_block, key_seq = masked_scores(
                query, keys, segments, seq_index, block_index, block
            )
            block_lse = lax.dynamic_index_in_dim(
                logsum, seq_index * blocks + block_index, 0, keepdims=False
            )
            attn_prob = jnp.exp(scores - block_lse[..., None])
            prob_low = attn_prob.astype(jnp.bfloat16)
            grad_block = lax.dynamic_slice_in_dim(grad_seq, block_index * block, block, 0)
            grad_value_acc = grad_value_acc + jnp.einsum(
                "hqk,qhd->khd", prob_low, grad_block, preferred_element_type=jnp.float32
            )
            grad_prob = jnp.einsum(
                "qhd,khd->hqk", grad_block, value_seq, preferred_element_type=jnp.float32
            )
            row_delta = jnp.sum(attn_prob * grad_prob, axis=-1, keepdims=True)
            grad_score = (attn_prob * (grad_prob - row_delta)).astype(jnp.bfloat16)
            grad_query_block = (
                jnp.einsum("hqk,khd->qhd", grad_score, key_seq, preferred_element_type=jnp.float32)
                * score_scale
            )
            grad_key_acc = (
                grad_key_acc
                + jnp.einsum(
                    "hqk,qhd->khd", grad_score, query_block, preferred_element_type=jnp.float32
                )
                * score_scale
            )
            return ((grad_key_acc, grad_value_acc), grad_query_block)

        zeros_seq = jnp.zeros((length, heads_dev, head_size), jnp.float32)
        (grad_key_seq, grad_value_seq), grad_query_blocks = lax.scan(
            block_step, (zeros_seq, zeros_seq), jnp.arange(blocks, dtype=jnp.int32)
        )
        return (
            grad_query_blocks.reshape(length, heads_dev, head_size),
            grad_key_seq,
            grad_value_seq,
        )

    return lax.map(per_seq, jnp.arange(seq_count, dtype=jnp.int32))


def body(
    tokens,
    segments,
    norm_gain,
    norm_shift,
    qkv_weight,
    qkv_bias,
    dense_weight,
    up_weight,
    up_bias,
    down_weight,
    out_bias,
    cotangent,
):
    row_count, model_width = tokens.shape
    seq_count, length = segments.shape
    all_rows = seq_count * length
    my_start = lax.axis_index("tensor") * row_count
    resid = tokens.astype(jnp.float32)
    row_mean = jnp.mean(resid, axis=-1, keepdims=True)
    centered = resid - row_mean
    inverse = lax.rsqrt(jnp.mean(centered * centered, axis=-1, keepdims=True) + EPS)
    normed = centered * inverse
    normed_mine = (normed * norm_gain + norm_shift).astype(jnp.bfloat16)
    normed_low = lax.all_gather(normed_mine, "tensor", axis=0, tiled=True)
    full_qkv, full_dense, full_up, full_down, full_qbias, full_ubias = (
        lax.all_gather(qkv_weight, "dp", axis=1, tiled=True),
        lax.all_gather(dense_weight, "dp", axis=1, tiled=True),
        lax.all_gather(up_weight, "dp", axis=0, tiled=True),
        lax.all_gather(down_weight, "dp", axis=1, tiled=True),
        lax.all_gather(qkv_bias, "dp", axis=1, tiled=True),
        lax.all_gather(up_bias, "dp", axis=0, tiled=True),
    )
    local_width = full_qkv.shape[2]
    heads_dev = local_width // HEAD_DIM
    projected = (
        jnp.einsum("td,cde->cte", normed_low, full_qkv, preferred_element_type=jnp.float32)
        + full_qbias.astype(jnp.float32)[:, None, :]
    )
    projected = projected.reshape(3, seq_count, length, heads_dev, HEAD_DIM)
    cosines, sines = rotary_tables(segments)
    query = rotate(projected[0], cosines, sines, 1.0).astype(jnp.bfloat16)
    keys = rotate(projected[1], cosines, sines, 1.0).astype(jnp.bfloat16)
    values = projected[2].astype(jnp.bfloat16)
    valid_rows = (segments != 0).astype(jnp.float32).reshape(all_rows, 1)
    context, logsum = attention_forward(query, keys, values, segments)
    context_low = (context * valid_rows).astype(jnp.bfloat16)
    attn_part = jnp.dot(context_low, full_dense, preferred_element_type=jnp.float32)
    every_up, every_down = (full_up, full_down)
    hidden_pre = jnp.dot(
        normed_low, full_up, preferred_element_type=jnp.float32
    ) + full_ubias.astype(jnp.float32)
    hidden_act = gelu_value(hidden_pre).astype(jnp.bfloat16)
    mlp_part = jnp.dot(hidden_act, full_down, preferred_element_type=jnp.float32)
    attn_mine, mlp_mine = (
        lax.psum_scatter(attn_part, "tensor", scatter_dimension=0, tiled=True),
        lax.psum_scatter(mlp_part, "tensor", scatter_dimension=0, tiled=True),
    )
    output = (resid + attn_mine + mlp_mine + out_bias).astype(jnp.bfloat16)
    valid_mine = lax.dynamic_slice_in_dim(valid_rows, my_start, row_count, 0)
    totals = lax.psum(
        (
            jnp.sum(valid_mine * resid * resid),
            jnp.sum(valid_mine * attn_mine * attn_mine),
            jnp.sum(valid_mine * mlp_mine * mlp_mine),
            jnp.sum(valid_mine) * model_width,
        ),
        ("dp", "tensor"),
    )
    root_squares = jnp.sqrt(jnp.stack([totals[0], totals[1], totals[2]]) / totals[3])
    grad_full = lax.all_gather(cotangent, "tensor", axis=0, tiled=True)
    grad_dense = contract_rows(context_low, grad_full)
    grad_context = contract_cols(grad_full, full_dense)
    grad_context_low = (
        grad_context.astype(jnp.bfloat16) * valid_rows.astype(jnp.bfloat16)
    ).reshape(seq_count, length, heads_dev, HEAD_DIM)
    grad_down = contract_rows(hidden_act, grad_full)
    grad_act = contract_cols(grad_full, every_down)
    grad_pre = (grad_act * gelu_slope(hidden_pre)).astype(jnp.bfloat16)
    grad_up = contract_rows(normed_low, grad_pre)
    grad_ubias = jnp.sum(grad_pre, axis=0, dtype=jnp.float32)
    mlp_normed = contract_cols(grad_pre, every_up)
    grad_query, grad_keys, grad_values = attention_backward(
        query, keys, values, segments, logsum, grad_context_low
    )
    grad_proj = jnp.stack(
        [
            rotate(grad_query, cosines, sines, -1.0),
            rotate(grad_keys, cosines, sines, -1.0),
            grad_values,
        ]
    )
    grad_proj = grad_proj.astype(jnp.bfloat16).reshape(3, all_rows, local_width)
    grad_qkv = jnp.einsum("td,cte->cde", normed_low, grad_proj, preferred_element_type=jnp.float32)
    grad_qbias = jnp.sum(grad_proj, axis=1, dtype=jnp.float32)
    grad_normed = jnp.einsum("cte,cde->td", grad_proj, full_qkv, preferred_element_type=jnp.float32)
    part_qkv, part_dense, part_up, part_down, part_qbias, part_ubias = (
        lax.psum_scatter(grad_qkv, "dp", scatter_dimension=1, tiled=True),
        lax.psum_scatter(grad_dense, "dp", scatter_dimension=1, tiled=True),
        lax.psum_scatter(grad_up, "dp", scatter_dimension=0, tiled=True),
        lax.psum_scatter(grad_down, "dp", scatter_dimension=1, tiled=True),
        lax.psum_scatter(grad_qbias, "dp", scatter_dimension=1, tiled=True),
        lax.psum_scatter(grad_ubias, "dp", scatter_dimension=0, tiled=True),
    )
    normed_term = grad_normed + mlp_normed
    grad_mine = lax.psum_scatter(normed_term, "tensor", scatter_dimension=0, tiled=True)
    scaled = grad_mine * norm_gain
    grad_tokens = (
        cotangent.astype(jnp.float32)
        + inverse
        * (
            scaled
            - jnp.mean(scaled, axis=-1, keepdims=True)
            - normed * jnp.mean(scaled * normed, axis=-1, keepdims=True)
        )
    ).astype(jnp.bfloat16)
    part_gain, part_shift, part_obias = (
        lax.psum_scatter(
            jnp.sum(grad_mine * normed, axis=0), ("dp", "tensor"), scatter_dimension=0, tiled=True
        ),
        lax.psum_scatter(
            jnp.sum(grad_mine, axis=0), ("dp", "tensor"), scatter_dimension=0, tiled=True
        ),
        lax.psum_scatter(
            jnp.sum(cotangent, axis=0, dtype=jnp.float32),
            ("dp", "tensor"),
            scatter_dimension=0,
            tiled=True,
        ),
    )
    return (
        output,
        grad_tokens,
        part_gain,
        part_shift,
        part_qkv,
        part_qbias,
        part_dense,
        part_up,
        part_ubias,
        part_down,
        part_obias,
        root_squares,
    )


def solution(mesh):
    placed = (
        P(("dp", "tensor"), None),
        P("dp", None),
        P(),
        P(),
        P(None, "dp", "tensor"),
        P(None, ("tensor", "dp")),
        P("tensor", "dp"),
        P("dp", "tensor"),
        P(("tensor", "dp")),
        P("tensor", "dp"),
        P(),
        P(("dp", "tensor"), None),
    )
    return jax.shard_map(
        body,
        mesh=mesh,
        in_specs=placed,
        out_specs=(
            P(("dp", "tensor"), None),
            P(("dp", "tensor"), None),
            P(("dp", "tensor")),
            P(("dp", "tensor")),
            P(None, "dp", "tensor"),
            P(None, ("tensor", "dp")),
            P("tensor", "dp"),
            P("dp", "tensor"),
            P(("tensor", "dp")),
            P("tensor", "dp"),
            P(("dp", "tensor")),
            P(),
        ),
        check_vma=False,
    )
```

profile of v0, /device:TPU:0, one launch (start us, length us, event | category | flops | bytes accessed | tf_op | source)
XLA Modules:
  0.0 2402.5 jit_solution(15305269189243383809)
XLA Ops:
  31.1 28.9 %all-gather.11.cloned.1.call-done = bf16[3,2048,512]{1,2,0:T(8,128)(2,1)} async-done(((bf16[3,256,512]{1,2,0:T(8,128)(2,1)}), bf16[3,2048,512]{1,2,0:T(8,128)(2,1)}) %all-gather.11.cloned.1.call-update) | async-done | bytes 6291472 | tf_op jit(solution)/shard_map/all_gather | solution.py:198
  59.9 151.8 %all-gather.9.cloned.1.call-done = bf16[2048,2048]{1,0:T(8,128)(2,1)} async-done(((bf16[512,2048]{1,0:T(8,128)(2,1)}), bf16[2048,2048]{1,0:T(8,128)(2,1)}) %all-gather.9.cloned.1.call-update) | async-done | bytes 8388624 | tf_op jit(solution)/shard_map/all_gather | solution.py:196
  237.4 295.6 %while.43 = (s32[]{:T(128)}, f32[4,512,8,64]{1,0,3,2:T(4,128)}, f32[4,8,512]{2,1,0:T(8,128)S(1)}, s32[4]{0:T(128)S(1)}, s32[1,2048]{1,0:T(1,128)S(1)}, /*index=5...) while((s32[]{:T(128)}, f32[4,512,8,64]{1,0,3,2:T(4,128)}, ...), condition=%wide.region_7.8_spmd, body=%wide.region_4.7_spmd.sunk | while | flops 2251289088 | bytes 114968888 | solution.py:113
  545.4 544.2 %while.44 = (s32[]{:T(128)}, f32[2048,8,64]{0,2,1:T(8,128)}, f32[2048,8,64]{0,2,1:T(8,128)}, f32[4,512,8,64]{1,0,3,2:T(4,128)}, s32[4]{0:T(128)S(1)}, /*index=5*...) while((s32[]{:T(128)}, f32[2048,8,64]{0,2,1:T(8,128)}, ...), condition=%wide.region_12.13_spmd.clone, body=%wide.region_10.12_spmd.clone.sunk | while | flops 5452853760 | bytes 284264704 | solution.py:160
  578.5 24.5 %multiply_reduce_fusion.3 = (f32[8,512]{1,0:T(8,128)S(1)}, f32[8,512,2048]{2,1,0:T(8,128)}) fusion(f32[8,512,2048]{2,1,0:T(8,128)} %fusion.137, f32[8,512]{1,0:T(8,128)S(1)} %dynamic-slice_bitcast_fusion.2, bf16[1,2048,8,64]{1,3,2,0:T(8,128)(2,1)S(1)} %get-tuple-element.696, bf16[1,2048,8,64]{1,3,2,0:T(8,128)(2,1)} %get-tuple-element.694, ...), kind=kOutput, calls=%fused_computation.21.clone.1 | convolution fusion | flops 1115680768 | bytes 70811648 | tf_op jit(solution)/shard_map/while/body/eval_jaxpr/while/body/eval_jaxpr/qhd,khd->hqk/dot_general | solution.py:86
  603.0 27.4 %multiply_convert_fusion.8 = bf16[8,512,2048]{2,1,0:T(8,128)(2,1)} fusion(f32[8,512,2048]{2,1,0:T(8,128)} %get-tuple-element.613, f32[8,512,2048]{2,1,0:T(8,128)} %fusion.137, f32[8,512]{1,0:T(8,128)S(1)} %get-tuple-element.614), kind=kLoop, calls=%fused_computation.20.clone.1 | loop fusion | flops 25165824 | bytes 83902464 | tf_op jit(solution)/shard_map/while/body/eval_jaxpr/while/body/eval_jaxpr/convert_element_type | solution.py:145
  709.9 24.5 %multiply_reduce_fusion.3 = (f32[8,512]{1,0:T(8,128)S(1)}, f32[8,512,2048]{2,1,0:T(8,128)}) fusion(f32[8,512,2048]{2,1,0:T(8,128)} %fusion.137, f32[8,512]{1,0:T(8,128)S(1)} %dynamic-slice_bitcast_fusion.2, bf16[1,2048,8,64]{1,3,2,0:T(8,128)(2,1)S(1)} %get-tuple-element.696, bf16[1,2048,8,64]{1,3,2,0:T(8,128)(2,1)} %get-tuple-element.694, ...), kind=kOutput, calls=%fused_computation.21.clone.1 | convolution fusion | flops 1115680768 | bytes 70811648 | tf_op jit(solution)/shard_map/while/body/eval_jaxpr/while/body/eval_jaxpr/qhd,khd->hqk/dot_general | solution.py:86
  734.4 27.4 %multiply_convert_fusion.8 = bf16[8,512,2048]{2,1,0:T(8,128)(2,1)} fusion(f32[8,512,2048]{2,1,0:T(8,128)} %get-tuple-element.613, f32[8,512,2048]{2,1,0:T(8,128)} %fusion.137, f32[8,512]{1,0:T(8,128)S(1)} %get-tuple-element.614), kind=kLoop, calls=%fused_computation.20.clone.1 | loop fusion | flops 25165824 | bytes 83902464 | tf_op jit(solution)/shard_map/while/body/eval_jaxpr/while/body/eval_jaxpr/convert_element_type | solution.py:145
  843.6 24.5 %multiply_reduce_fusion.3 = (f32[8,512]{1,0:T(8,128)S(1)}, f32[8,512,2048]{2,1,0:T(8,128)}) fusion(f32[8,512,2048]{2,1,0:T(8,128)} %fusion.137, f32[8,512]{1,0:T(8,128)S(1)} %dynamic-slice_bitcast_fusion.2, bf16[1,2048,8,64]{1,3,2,0:T(8,128)(2,1)S(1)} %get-tuple-element.696, bf16[1,2048,8,64]{1,3,2,0:T(8,128)(2,1)} %get-tuple-element.694, ...), kind=kOutput, calls=%fused_computation.21.clone.1 | convolution fusion | flops 1115680768 | bytes 70811648 | tf_op jit(solution)/shard_map/while/body/eval_jaxpr/while/body/eval_jaxpr/qhd,khd->hqk/dot_general | solution.py:86
  868.1 27.4 %multiply_convert_fusion.8 = bf16[8,512,2048]{2,1,0:T(8,128)(2,1)} fusion(f32[8,512,2048]{2,1,0:T(8,128)} %get-tuple-element.613, f32[8,512,2048]{2,1,0:T(8,128)} %fusion.137, f32[8,512]{1,0:T(8,128)S(1)} %get-tuple-element.614), kind=kLoop, calls=%fused_computation.20.clone.1 | loop fusion | flops 25165824 | bytes 83902464 | tf_op jit(solution)/shard_map/while/body/eval_jaxpr/while/body/eval_jaxpr/convert_element_type | solution.py:145
  977.3 24.5 %multiply_reduce_fusion.3 = (f32[8,512]{1,0:T(8,128)S(1)}, f32[8,512,2048]{2,1,0:T(8,128)}) fusion(f32[8,512,2048]{2,1,0:T(8,128)} %fusion.137, f32[8,512]{1,0:T(8,128)S(1)} %dynamic-slice_bitcast_fusion.2, bf16[1,2048,8,64]{1,3,2,0:T(8,128)(2,1)S(1)} %get-tuple-element.696, bf16[1,2048,8,64]{1,3,2,0:T(8,128)(2,1)} %get-tuple-element.694, ...), kind=kOutput, calls=%fused_computation.21.clone.1 | convolution fusion | flops 1115680768 | bytes 70811648 | tf_op jit(solution)/shard_map/while/body/eval_jaxpr/while/body/eval_jaxpr/qhd,khd->hqk/dot_general | solution.py:86
  1001.9 27.4 %multiply_convert_fusion.8 = bf16[8,512,2048]{2,1,0:T(8,128)(2,1)} fusion(f32[8,512,2048]{2,1,0:T(8,128)} %get-tuple-element.613, f32[8,512,2048]{2,1,0:T(8,128)} %fusion.137, f32[8,512]{1,0:T(8,128)S(1)} %get-tuple-element.614), kind=kLoop, calls=%fused_computation.20.clone.1 | loop fusion | flops 25165824 | bytes 83902464 | tf_op jit(solution)/shard_map/while/body/eval_jaxpr/while/body/eval_jaxpr/convert_element_type | solution.py:145
  1186.2 24.2 %fusion.87 = f32[2048,2048]{1,0:T(8,128)} fusion(bf16[2048,2048]{1,0:T(8,128)(2,1)} %all-gather.9.cloned.1.call-done, bf16[2048,2048]{1,0:T(8,128)(2,1)} %all-gather.15.cloned.1.call-done), kind=kOutput, calls=%fused_computation.146 | convolution fusion | flops 17179869184 | bytes 33554432 | tf_op jit(solution)/shard_map/dot_general | solution.py:221
  1210.4 35.3 %convert_reduce_fusion = (f32[2048]{0:T(1024)}, bf16[2048,2048]{1,0:T(8,128)(2,1)}) fusion(f32[2048,2048]{1,0:T(8,128)} %fusion.87, f32[2048]{0:T(1024)S(1)} %bitcast.202, bf16[2048,2048]{1,0:T(8,128)(2,1)} %all-gather.19.cloned.1.call-done, bf16[2048,2048]{1,0:T(8,128)(2,1)} %all-gather.17.cloned.1.call-done), kind=kOutput, calls=%fused_computation.58 | convolution fusion | flops 17272141824 | bytes 41959424 | tf_op jit(solution)/shard_map/dot_general | solution.py:69
  1245.8 26.9 %bitcast_add_fusion.2 = f32[2048,2048]{1,0:T(8,128)} fusion(f32[2048,2048,1]{1,0,2:T(8,128)} %fusion.82, bf16[2048,2048]{1,0:T(8,128)(2,1)} %get-tuple-element.488, bf16[2048,2048]{1,0:T(8,128)(2,1)} %all-gather.15.cloned.1.call-done), kind=kOutput, calls=%fused_computation.57 | convolution fusion | flops 17184063488 | bytes 50331648 | tf_op jit(solution)/shard_map/dot_general | solution.py:69
  1272.7 26.4 %fusion.84 = f32[2048,2048]{1,0:T(8,128)} fusion(bf16[2048,2048]{1,0:T(8,128)(2,1)} %all-gather.17.cloned.1.call-done, f32[2048,2048]{1,0:T(8,128)} %fusion.87, f32[2048]{0:T(1024)S(1)} %bitcast.203), kind=kOutput, calls=%fused_computation.143 | convolution fusion | flops 17221812224 | bytes 41951232 | tf_op jit(solution)/shard_map/dot_general | solution.py:225
  1311.0 24.8 %fusion.88 = f32[2048,2048]{1,0:T(8,128)} fusion(bf16[2048,2048]{1,0:T(8,128)(2,1)} %all-gather.9.cloned.1.call-done, bf16[2048,2048]{1,0:T(8,128)(2,1)} %get-tuple-element.488), kind=kOutput, calls=%fused_computation.147 | convolution fusion | flops 17179869184 | bytes 33554432 | tf_op jit(solution)/shard_map/dot_general | solution.py:63
  1335.8 27.1 %fusion.83 = f32[2048,2048]{1,0:T(8,128)} fusion(bf16[2048,2048]{1,0:T(8,128)(2,1)} %all-gather.19.cloned.1.call-done, f32[2048,2048]{1,0:T(8,128)} %fusion.87, f32[2048]{0:T(1024)S(1)} %bitcast.204), kind=kOutput, calls=%fused_computation.142 | convolution fusion | flops 17221812224 | bytes 41951232 | tf_op jit(solution)/shard_map/dot_general | solution.py:63
  1384.7 146.8 %reduce-scatter.11.cloned.1.call-done = f32[512,2048]{1,0:T(8,128)} async-done(((f32[2048,2048]{1,0:T(8,128)}), f32[512,2048]{1,0:T(8,128)}) %reduce-scatter.11.cloned.1.call-update) | async-done | bytes 4194320 | tf_op jit(solution)/shard_map/reduce_scatter | solution.py:227
  1531.5 283.3 %reduce-scatter.15.cloned.1.call-done = f32[512,2048]{1,0:T(8,128)} async-done(((f32[2048,2048]{1,0:T(8,128)}), f32[512,2048]{1,0:T(8,128)}) %reduce-scatter.15.cloned.1.call-update) | async-done | bytes 4194320 | tf_op jit(solution)/shard_map/reduce_scatter | solution.py:277
  1814.8 283.5 %reduce-scatter.13.cloned.1.call-done = f32[512,2048]{1,0:T(8,128)} async-done(((f32[2048,2048]{1,0:T(8,128)}), f32[512,2048]{1,0:T(8,128)}) %reduce-scatter.13.cloned.1.call-update) | async-done | bytes 4194320 | tf_op jit(solution)/shard_map/reduce_scatter | solution.py:228
  2110.6 41.9 %all-reduce.4 = (f32[2048]{0:T(1024)S(1)}, f32[2048]{0:T(1024)S(1)}, f32[2048]{0:T(1024)S(1)}, f32[1]{0:T(128)}, f32[1]{0:T(128)}, /*index=5*/f32[1]{0:T(128)}, f32[]{:T(128)}) all-reduce(f32[2048]{0:T(1024)S(1)} %get-tuple-element.409, f32[2048]{0:T(1024)S(1)} %get-tuple-element.412, ...), channel_id=5, replica_groups=mesh['dp'=8,'tensor'=4] {'dp','tensor'}, use_global_device_ids=true, to_apply=%region_17.18.clone | all-reduce | flops 6148 | bytes 49184
  2157.4 118.0 %reduce-scatter.21.cloned.1.call-done = f32[256,2048]{1,0:T(8,128)} async-done(((f32[2048,2048]{1,0:T(8,128)}), f32[256,2048]{1,0:T(8,128)}) %reduce-scatter.21.cloned.1.call-update) | async-done | bytes 2097168 | tf_op jit(solution)/shard_map/reduce_scatter | solution.py:271
  2275.3 120.4 %reduce-scatter.23.cloned.1.call-done = f32[2048,256]{1,0:T(8,128)} async-done(((f32[2048,2048]{1,0:T(8,128)}), f32[2048,256]{1,0:T(8,128)}) %reduce-scatter.23.cloned.1.call-update) | async-done | bytes 2097168 | tf_op jit(solution)/shard_map/reduce_scatter | solution.py:272
  (246 shorter events, 809.1 us)
Async XLA Ops:
  7.2 52.7 %all-gather.11.cloned.1.call-start = ((), (), s32[]{:S(2)}) async-start(), calls=%async_computation.9 | async-start | bytes 7077888 | tf_op jit(solution)/shard_map/all_gather | solution.py:198
  9.7 202.0 %all-gather.9.cloned.1.call-start = ((), (), s32[]{:S(2)}) async-start(), calls=%async_computation.8 | async-start | bytes 10485760 | tf_op jit(solution)/shard_map/all_gather | solution.py:196
  15.2 517.7 %all-gather.13.cloned.1.call-start = ((), (), s32[]{:S(2)}) async-start(), calls=%async_computation.10 | async-start | bytes 2359296 | tf_op jit(solution)/shard_map/all_gather | solution.py:199
  16.0 517.0 %all-gather.19.cloned.1.call-start = ((), (), s32[]{:S(2)}) async-start(), calls=%async_computation.15 | async-start | bytes 10485760 | tf_op jit(solution)/shard_map/all_gather | solution.py:242
  16.5 1169.7 %all-gather.15.cloned.1.call-start = ((), (), s32[]{:S(2)}) async-start(), calls=%async_computation.12 | async-start | bytes 9437184 | tf_op jit(solution)/shard_map/all_gather | solution.py:200
  17.1 1193.3 %all-gather.17.cloned.1.call-start = ((), (), s32[]{:S(2)}) async-start(), calls=%async_computation.13 | async-start | bytes 9437184 | tf_op jit(solution)/shard_map/all_gather | solution.py:201
  17.7 1348.4 %reduce-scatter.25.cloned.1.call-start = ((), (), s32[]{:S(2)}) async-start(), calls=%async_computation.21 | async-start | bytes 294912
  17.9 193.8 %copy-start.15 = (f32[1,2048]{1,0:T(1,128)}, f32[1,2048]{1,0:T(1,128)S(1)}, u32[]{:S(2)}) copy-start(f32[1,2048]{1,0:T(1,128)S(1)} %compare_convert_fusion) | copy-start | bytes 24580
  31.0 201.5 %copy-start.8 = (f32[2048,16]{0,1:T(8,128)}, f32[2048,16]{0,1:T(8,128)S(1)}, u32[]{:S(2)}) copy-start(f32[2048,16]{0,1:T(8,128)S(1)} %get-tuple-element.486) | copy-start | bytes 393220
  237.4 295.6 %copy-start.23 = (bf16[2048]{0:T(1024)(128)(2,1)S(1)}, bf16[2048]{0:T(1024)(128)(2,1)}, u32[]{:S(2)}) copy-start(bf16[2048]{0:T(1024)(128)(2,1)} %convert_element_type.133) | copy-start | bytes 12292
  1089.6 9.7 copy-start.9
  1089.6 9.7 copy-start.10
  1119.3 262.3 %reduce-scatter.17.cloned.1.call-start = ((), (), s32[]{:S(2)}) async-start(), calls=%async_computation.17 | async-start | bytes 14155776 | tf_op jit(solution)/shard_map/reduce_scatter | solution.py:269
  1139.3 392.2 %reduce-scatter.11.cloned.1.call-start = ((), (), s32[]{:S(2)}) async-start(), calls=%async_computation.11 | async-start | bytes 20971520 | tf_op jit(solution)/shard_map/reduce_scatter | solution.py:227
  1154.3 660.5 %reduce-scatter.15.cloned.1.call-start = ((), (), s32[]{:S(2)}) async-start(), calls=%async_computation.16 | async-start | bytes 20971520 | tf_op jit(solution)/shard_map/reduce_scatter | solution.py:277
  1272.6 825.7 %reduce-scatter.13.cloned.1.call-start = ((), (), s32[]{:S(2)}) async-start(), calls=%async_computation.14 | async-start | bytes 20971520 | tf_op jit(solution)/shard_map/reduce_scatter | solution.py:228
  1299.1 858.3 %reduce-scatter.19.cloned.1.call-start = ((), (), s32[]{:S(2)}) async-start(), calls=%async_computation.18 | async-start | bytes 4718592 | tf_op jit(solution)/shard_map/reduce_scatter | solution.py:270
  1311.0 964.4 %reduce-scatter.21.cloned.1.call-start = ((), (), s32[]{:S(2)}) async-start(), calls=%async_computation.19 | async-start | bytes 18874368 | tf_op jit(solution)/shard_map/reduce_scatter | solution.py:271
  1335.8 1059.9 %reduce-scatter.23.cloned.1.call-start = ((), (), s32[]{:S(2)}) async-start(), calls=%async_computation.20 | async-start | bytes 18874368 | tf_op jit(solution)/shard_map/reduce_scatter | solution.py:272
  1363.0 735.3 %copy-start.12 = (f32[2048]{0:T(1024)S(1)}, f32[2048]{0:T(1024)}, u32[]{:S(2)}) copy-start(f32[2048]{0:T(1024)} %param.18) | copy-start | bytes 24580
  1363.0 735.3 %copy-start.14 = (f32[512]{0:T(512)S(1)}, f32[512]{0:T(512)}, u32[]{:S(2)}) copy-start(f32[512]{0:T(512)} %copy-done.13) | copy-start | bytes 6148
  1363.0 735.3 %copy-start.19 = (f32[512]{0:T(512)S(1)}, f32[512]{0:T(512)}, u32[]{:S(2)}) copy-start(f32[512]{0:T(512)} %copy-done.18) | copy-start | bytes 6148
  1363.0 735.3 %copy-start.20 = (f32[2048]{0:T(1024)S(1)}, f32[2048]{0:T(1024)}, u32[]{:S(2)}) copy-start(f32[2048]{0:T(1024)} %param.26) | copy-start | bytes 24580
  1363.0 735.3 %copy-start.2 = (bf16[512,2048]{1,0:T(8,128)(2,1)S(1)}, bf16[512,2048]{1,0:T(8,128)(2,1)}, u32[]{:S(2)}) copy-start(bf16[512,2048]{1,0:T(8,128)(2,1)} %param.16) | copy-start | bytes 6291460
  (18 other events, 70.9 us)
Sparse Core Ops, SparseCore 0:
  10.5 49.3 all-gather.10
  62.0 149.6 all-gather.8
  213.6 26.4 all-gather.12
  241.5 149.6 all-gather.18
  392.9 52.6 all-gather.14
  447.3 55.9 all-gather.16
  1119.5 32.8 reduce-scatter.24
  1156.3 92.3 reduce-scatter.16
  1251.2 280.2 reduce-scatter.10
  1533.7 281.0 reduce-scatter.14
  1817.2 281.0 reduce-scatter.12
  2102.1 52.6 reduce-scatter.18
  2159.4 115.9 reduce-scatter.20
  2279.8 115.9 reduce-scatter.22
where the time goes:
time: 2410 us; the launch traced here: 2400 us
  waiting for transfers between devices  1140 us (47%)
  matrix products  697 us (29%)
  local copies, waits for them, and re-layouts  232 us (10%)
  other arithmetic  216 us (9%)
  blocking collectives  74.8 us (3%)
  loops' own time  30.5 us (1%)
    reduce_scatter x1, waiting for transfers between devices, body(): lax.psum_scatter(mlp_part, 'tensor', scatter_dimension=0, tiled=True)  284 us
    reduce_scatter x1, waiting for transfers between devices, body(): lax.psum_scatter(normed_term, 'tensor', scatter_dimension=0, tiled=True)  283 us
    dynamic_update_slice x16, local copies, waits for them, and re-layouts, attention_forward(): lax.map(one_block, jnp.arange(seq_count * blocks, dtype=jnp.int32))  182 us
    dot_general x8, matrix products, masked_scores(): jnp.einsum('qhd,khd->hqk', query_block, key_seq, preferred_element_type=j...  161 us
    all_gather x1, waiting for transfers between devices, body(): normed_low = lax.all_gather(normed_mine, 'tensor', axis=0, tiled=True)  152 us
    reduce_scatter x1, waiting for transfers between devices, body(): lax.psum_scatter(attn_part, 'tensor', scatter_dimension=0, tiled=True)  147 us
    reduce_scatter x1, waiting for transfers between devices, body(): lax.psum_scatter(grad_down, 'dp', scatter_dimension=1, tiled=True)  120 us
    reduce_scatter x1, waiting for transfers between devices, body(): lax.psum_scatter(grad_up, 'dp', scatter_dimension=0, tiled=True)  118 us
  transfers between devices with their start and end apart: 14, of which 7 were waited for; matrix products, arithmetic and copies ran while one was open for 47% of the time, Pallas kernels for 0%

commit v1 on v0

v1 whole, which is shorter than its diff:
```python
import functools
import math

import jax
import jax.numpy as jnp
from jax import lax
from jax.experimental import pallas as pl
from jax.experimental.pallas import tpu as pltpu
from jax.sharding import PartitionSpec as P

HEAD_DIM = 64
ROT = 32
PAIR = 2 * HEAD_DIM
BLOCK = 256

EPS = 1e-05
GELU_C = math.sqrt(2.0 / math.pi)


def segment_starts(segs):
    return jnp.sum((segs[:, None, :] < segs[:, :, None]).astype(jnp.int32), axis=-1)


def rotary_wide(starts):
    length = starts.shape[0]
    half_rot = ROT // 2
    frequency = jnp.exp(-math.log(10000.0) * (2.0 * jnp.arange(half_rot, dtype=jnp.float32) / ROT))
    position = jnp.arange(length, dtype=jnp.int32) - starts
    angles = position.astype(jnp.float32)[:, None] * frequency
    cosines, sines = jnp.cos(angles), jnp.sin(angles)
    ones = jnp.ones((length, HEAD_DIM - ROT), jnp.float32)
    cos_head = jnp.concatenate([cosines, cosines, ones], axis=-1)
    sin_head = jnp.concatenate([-sines, sines, 0.0 * ones], axis=-1)
    return (jnp.concatenate([cos_head, cos_head], -1), jnp.concatenate([sin_head, sin_head], -1))


def turn(x, cos_wide, sin_wide):
    lane = lax.broadcasted_iota(jnp.int32, x.shape, 1) % HEAD_DIM
    half_rot = ROT // 2
    partner = jnp.where(
        lane < half_rot, pltpu.roll(x, PAIR - half_rot, 1), pltpu.roll(x, half_rot, 1)
    )
    return x * cos_wide + partner * sin_wide


def first_half(shape):
    return lax.broadcasted_iota(jnp.int32, shape, len(shape) - 1) < HEAD_DIM


def halves(x):
    front = first_half(x.shape)
    zero = jnp.zeros_like(x)
    return (jnp.where(front, x, zero), jnp.where(front, zero, x))


def nt(left, right):
    return lax.dot_general(
        left, right, (((1,), (1,)), ((), ())), preferred_element_type=jnp.float32
    )


def nn(left, right):
    return lax.dot_general(
        left, right, (((1,), (0,)), ((), ())), preferred_element_type=jnp.float32
    )


def tn(left, right):
    return lax.dot_general(
        left, right, (((0,), (0,)), ((), ())), preferred_element_type=jnp.float32
    )


def attend_kernel(
    low_ref, xq_ref, xk_ref, xv_ref, bias_ref, cos_ref, sin_ref, start_ref, valid_ref,
    q_ref, k_ref, v_ref, ctx_ref, lse_ref, km, vm, s_scr,
):
    length = q_ref.shape[0]
    blocks = length // BLOCK
    scale = 1.0 / math.sqrt(HEAD_DIM)

    def project(i, _):
        rows = pl.ds(pl.multiple_of(i * BLOCK, BLOCK), BLOCK)
        cw, sw = cos_ref[rows, :], sin_ref[rows, :]
        q = turn(xq_ref[0, rows, :] + bias_ref[0], cw, sw).astype(jnp.bfloat16)
        q_ref[rows, :] = q * jnp.bfloat16(scale)
        k = turn(xk_ref[0, rows, :] + bias_ref[1], cw, sw).astype(jnp.bfloat16)
        k_ref[rows, :] = k
        v = (xv_ref[0, rows, :] + bias_ref[2]).astype(jnp.bfloat16)
        v_ref[rows, :] = v
        km[0, rows, :], km[1, rows, :] = halves(k)
        vm[0, rows, :], vm[1, rows, :] = halves(v)
        return 0

    lax.fori_loop(0, blocks, project, 0)

    def query_block(i, _):
        rows = pl.ds(pl.multiple_of(i * BLOCK, BLOCK), BLOCK)
        q = q_ref[rows, :]
        start = start_ref[rows, :][:, :1]
        low = low_ref[i]
        qpos = i * BLOCK + lax.broadcasted_iota(jnp.int32, (BLOCK, BLOCK), 0)

        def top(j, tops):
            cols = pl.ds(pl.multiple_of(j * BLOCK, BLOCK), BLOCK)
            kpos = j * BLOCK + lax.broadcasted_iota(jnp.int32, (BLOCK, BLOCK), 1)
            allowed = (kpos >= start) & (kpos <= qpos)
            out = []
            for h in range(2):
                s = jnp.where(allowed, nt(q, km[h, cols, :]), -jnp.inf)
                s_scr[h, j] = s
                out.append(jnp.maximum(tops[h], jnp.max(s, axis=-1, keepdims=True)))
            return tuple(out)

        floor = jnp.full((BLOCK, 1), -jnp.inf, jnp.float32)
        tops = lax.fori_loop(low, i + 1, top, (floor, floor))

        def weigh(j, state):
            sum_0, sum_1, acc = state
            cols = pl.ds(pl.multiple_of(j * BLOCK, BLOCK), BLOCK)
            sums = [sum_0, sum_1]
            for h in range(2):
                e = jnp.exp(s_scr[h, j] - tops[h])
                sums[h] = sums[h] + jnp.sum(e, axis=-1, keepdims=True)
                acc = acc + nn(e.astype(jnp.bfloat16), vm[h, cols, :])
            return (sums[0], sums[1], acc)

        none = jnp.zeros((BLOCK, 1), jnp.float32)
        sum_0, sum_1, acc = lax.fori_loop(
            low, i + 1, weigh, (none, none, jnp.zeros((BLOCK, PAIR), jnp.float32))
        )
        front = first_half((BLOCK, PAIR))
        out = acc / jnp.where(front, sum_0, sum_1)
        ctx_ref[rows, :] = (out * valid_ref[rows, :]).astype(jnp.bfloat16)
        lse = jnp.where(front, tops[0] + jnp.log(sum_0), tops[1] + jnp.log(sum_1))
        lse_t = lse.T
        lse_ref[0, 0:1, rows] = lse_t[0:1, :]
        lse_ref[0, 1:2, rows] = lse_t[HEAD_DIM : HEAD_DIM + 1, :]
        return 0

    lax.fori_loop(0, blocks, query_block, 0)


def attention_forward(projected, bias, cos_wide, sin_wide, starts, valid_wide, lows):
    _, length, width = projected.shape
    pairs = width // PAIR
    blocks = length // BLOCK
    start_wide = jnp.broadcast_to(starts[:, None], (length, PAIR))
    part = lambda c: pl.BlockSpec((1, length, PAIR), lambda p, low, c=c: (c, 0, p))
    table = pl.BlockSpec((length, PAIR), lambda p, low: (0, 0))
    flat = pl.BlockSpec((length, PAIR), lambda p, low: (0, p))
    flat_shape = jax.ShapeDtypeStruct((length, width), jnp.bfloat16)
    return pl.pallas_call(
        attend_kernel,
        grid_spec=pltpu.PrefetchScalarGridSpec(
            num_scalar_prefetch=1,
            grid=(pairs,),
            in_specs=[
                part(0), part(1), part(2),
                pl.BlockSpec((3, 1, PAIR), lambda p, low: (0, 0, p)),
                table, table, table, table,
            ],
            out_specs=[flat, flat, flat, flat,
                       pl.BlockSpec((1, 2, length), lambda p, low: (p, 0, 0))],
            scratch_shapes=[
                pltpu.VMEM((2, length, PAIR), jnp.bfloat16),
                pltpu.VMEM((2, length, PAIR), jnp.bfloat16),
                pltpu.VMEM((2, blocks, BLOCK, BLOCK), jnp.float32),
            ],
        ),
        out_shape=[flat_shape] * 4 + [jax.ShapeDtypeStruct((pairs, 2, length), jnp.float32)],
        compiler_params=pltpu.CompilerParams(vmem_limit_bytes=48 * 2**20),
        name="attend",
    )(lows, projected, projected, projected, bias[:, None, :], cos_wide, sin_wide, start_wide, valid_wide)


def attend_back_kernel(
    low_ref, q_ref, k_ref, v_ref, do_ref, lse_ref, cos_ref, sin_ref, start_ref,
    grad_ref, sums_ref, qm, km, vm, dom, p_scr, dp_scr, dk_acc, dv_acc,
):
    length = q_ref.shape[0]
    blocks = length // BLOCK
    scale = 1.0 / math.sqrt(HEAD_DIM)

    def split(i, _):
        rows = pl.ds(pl.multiple_of(i * BLOCK, BLOCK), BLOCK)
        qm[0, rows, :], qm[1, rows, :] = halves(q_ref[rows, :])
        km[0, rows, :], km[1, rows, :] = halves(k_ref[rows, :])
        vm[0, rows, :], vm[1, rows, :] = halves(v_ref[rows, :])
        dom[0, rows, :], dom[1, rows, :] = halves(do_ref[rows, :])
        dk_acc[rows, :] = jnp.zeros((BLOCK, PAIR), jnp.float32)
        dv_acc[rows, :] = jnp.zeros((BLOCK, PAIR), jnp.float32)
        return 0

    lax.fori_loop(0, blocks, split, 0)

    def query_block(i, total):
        rows = pl.ds(pl.multiple_of(i * BLOCK, BLOCK), BLOCK)
        q = q_ref[rows, :]
        do = do_ref[rows, :]
        start = start_ref[:, rows]
        low = low_ref[i]
        qpos = i * BLOCK + lax.broadcasted_iota(jnp.int32, (BLOCK, BLOCK), 1)
        lse = [lse_ref[0, h : h + 1, rows] for h in range(2)]

        def weigh(j, deltas):
            cols = pl.ds(pl.multiple_of(j * BLOCK, BLOCK), BLOCK)
            kpos = j * BLOCK + lax.broadcasted_iota(jnp.int32, (BLOCK, BLOCK), 0)
            allowed = (kpos >= start) & (kpos <= qpos)
            out = []
            for h in range(2):
                s = nt(km[h, cols, :], q)
                p = jnp.where(allowed, jnp.exp(s - lse[h]), 0.0)
                dp = nt(vm[h, cols, :], do)
                p_scr[h, j] = p
                dp_scr[h, j] = dp
                out.append(deltas[h] + jnp.sum(p * dp, axis=0, keepdims=True))
            return tuple(out)

        none = jnp.zeros((1, BLOCK), jnp.float32)
        deltas = lax.fori_loop(low, i + 1, weigh, (none, none))

        def gather(j, dq):
            cols = pl.ds(pl.multiple_of(j * BLOCK, BLOCK), BLOCK)
            dk = dk_acc[cols, :]
            dv = dv_acc[cols, :]
            for h in range(2):
                p = p_scr[h, j]
                ds = (p * (dp_scr[h, j] - deltas[h])).astype(jnp.bfloat16)
                dv = dv + nn(p.astype(jnp.bfloat16), dom[h, rows, :])
                dk = dk + nn(ds, qm[h, rows, :])
                dq = dq + tn(ds, km[h, cols, :])
            dk_acc[cols, :] = dk
            dv_acc[cols, :] = dv
            return dq

        dq = lax.fori_loop(low, i + 1, gather, jnp.zeros((BLOCK, PAIR), jnp.float32))
        dq = turn(dq * scale, cos_ref[rows, :], -sin_ref[rows, :]).astype(jnp.bfloat16)
        grad_ref[0, rows, :] = dq
        return total + jnp.sum(dq.astype(jnp.float32), axis=0, keepdims=True)

    none = jnp.zeros((1, PAIR), jnp.float32)
    sums_ref[0] = lax.fori_loop(0, blocks, query_block, none)

    def finish(i, totals):
        rows = pl.ds(pl.multiple_of(i * BLOCK, BLOCK), BLOCK)
        dk = turn(dk_acc[rows, :], cos_ref[rows, :], -sin_ref[rows, :]).astype(jnp.bfloat16)
        dv = dv_acc[rows, :].astype(jnp.bfloat16)
        grad_ref[1, rows, :] = dk
        grad_ref[2, rows, :] = dv
        return (
            totals[0] + jnp.sum(dk.astype(jnp.float32), axis=0, keepdims=True),
            totals[1] + jnp.sum(dv.astype(jnp.float32), axis=0, keepdims=True),
        )

    sums_ref[1], sums_ref[2] = lax.fori_loop(0, blocks, finish, (none, none))


def attention_backward(q, k, v, do, lse, cos_wide, sin_wide, starts, lows):
    length, width = q.shape
    pairs = width // PAIR
    blocks = length // BLOCK
    flat = pl.BlockSpec((length, PAIR), lambda p, low: (0, p))
    table = pl.BlockSpec((length, PAIR), lambda p, low: (0, 0))
    grad, sums = pl.pallas_call(
        attend_back_kernel,
        grid_spec=pltpu.PrefetchScalarGridSpec(
            num_scalar_prefetch=1,
            grid=(pairs,),
            in_specs=[
                flat, flat, flat, flat,
                pl.BlockSpec((1, 2, length), lambda p, low: (p, 0, 0)),
                table, table,
                pl.BlockSpec((1, length), lambda p, low: (0, 0)),
            ],
            out_specs=[
                pl.BlockSpec((3, length, PAIR), lambda p, low: (0, 0, p)),
                pl.BlockSpec((3, 1, PAIR), lambda p, low: (0, 0, p)),
            ],
            scratch_shapes=[pltpu.VMEM((2, length, PAIR), jnp.bfloat16)] * 4
            + [pltpu.VMEM((2, blocks, BLOCK, BLOCK), jnp.float32)] * 2
            + [pltpu.VMEM((length, PAIR), jnp.float32)] * 2,
        ),
        out_shape=[
            jax.ShapeDtypeStruct((3, length, width), jnp.bfloat16),
            jax.ShapeDtypeStruct((3, 1, width), jnp.float32),
        ],
        compiler_params=pltpu.CompilerParams(vmem_limit_bytes=48 * 2**20),
        name="attend_back",
    )(lows, q, k, v, do, lse, cos_wide, sin_wide, starts[None, :])
    return (grad, sums[:, 0, :])


def gelu_value(u):
    tanh_value = jnp.tanh(GELU_C * (u + 0.044715 * u * u * u))
    return 0.5 * u * (1.0 + tanh_value)


def gelu_slope(u):
    tanh_value = jnp.tanh(GELU_C * (u + 0.044715 * u * u * u))
    return 0.5 * (1.0 + tanh_value) + 0.5 * u * (1.0 - tanh_value * tanh_value) * GELU_C * (
        1.0 + 3.0 * 0.044715 * u * u
    )


def contract_rows(left, right):
    return lax.dot_general(
        left, right, (((0,), (0,)), ((), ())), preferred_element_type=jnp.float32
    )


def contract_cols(left, right):
    return lax.dot_general(
        left, right, (((1,), (1,)), ((), ())), preferred_element_type=jnp.float32
    )


def scatter_low(part, axis, dim):
    return lax.psum_scatter(
        part.astype(jnp.bfloat16), axis, scatter_dimension=dim, tiled=True
    ).astype(jnp.float32)


def body(
    tokens,
    segments,
    norm_gain,
    norm_shift,
    qkv_weight,
    qkv_bias,
    dense_weight,
    up_weight,
    up_bias,
    down_weight,
    out_bias,
    cotangent,
):
    row_count, model_width = tokens.shape
    seq_count, length = segments.shape
    all_rows = seq_count * length
    my_start = lax.axis_index("tensor") * row_count
    resid = tokens.astype(jnp.float32)
    row_mean = jnp.mean(resid, axis=-1, keepdims=True)
    centered = resid - row_mean
    inverse = lax.rsqrt(jnp.mean(centered * centered, axis=-1, keepdims=True) + EPS)
    normed = centered * inverse
    normed_mine = (normed * norm_gain + norm_shift).astype(jnp.bfloat16)
    normed_low = lax.all_gather(normed_mine, "tensor", axis=0, tiled=True)
    full_qkv, full_dense, full_up, full_down, full_qbias, full_ubias = (
        lax.all_gather(qkv_weight, "dp", axis=1, tiled=True),
        lax.all_gather(dense_weight, "dp", axis=1, tiled=True),
        lax.all_gather(up_weight, "dp", axis=0, tiled=True),
        lax.all_gather(down_weight, "dp", axis=1, tiled=True),
        lax.all_gather(qkv_bias, "dp", axis=1, tiled=True),
        lax.all_gather(up_bias, "dp", axis=0, tiled=True),
    )
    starts = segment_starts(segments)[0]
    cos_wide, sin_wide = rotary_wide(starts)
    valid_rows = (segments != 0).astype(jnp.float32).reshape(all_rows, 1)
    valid_wide = jnp.broadcast_to(valid_rows, (length, PAIR))
    lows = starts[::BLOCK] // BLOCK
    projected = jnp.einsum(
        "td,cde->cte", normed_low, full_qkv, preferred_element_type=jnp.float32
    )
    query, keys, values, context_low, logsum = attention_forward(
        projected, full_qbias.astype(jnp.float32), cos_wide, sin_wide, starts, valid_wide, lows
    )
    attn_part = jnp.dot(context_low, full_dense, preferred_element_type=jnp.float32)
    every_up, every_down = (full_up, full_down)
    hidden_pre = jnp.dot(
        normed_low, full_up, preferred_element_type=jnp.float32
    ) + full_ubias.astype(jnp.float32)
    hidden_act = gelu_value(hidden_pre).astype(jnp.bfloat16)
    mlp_part = jnp.dot(hidden_act, full_down, preferred_element_type=jnp.float32)
    attn_mine, mlp_mine = (
        scatter_low(attn_part, "tensor", 0),
        scatter_low(mlp_part, "tensor", 0),
    )
    output = (resid + attn_mine + mlp_mine + out_bias).astype(jnp.bfloat16)
    valid_mine = lax.dynamic_slice_in_dim(valid_rows, my_start, row_count, 0)
    totals = lax.psum(
        (
            jnp.sum(valid_mine * resid * resid),
            jnp.sum(valid_mine * attn_mine * attn_mine),
            jnp.sum(valid_mine * mlp_mine * mlp_mine),
            jnp.sum(valid_mine) * model_width,
        ),
        ("dp", "tensor"),
    )
    root_squares = jnp.sqrt(jnp.stack([totals[0], totals[1], totals[2]]) / totals[3])
    grad_full = lax.all_gather(cotangent, "tensor", axis=0, tiled=True)
    grad_dense = contract_rows(context_low, grad_full)
    grad_context = contract_cols(grad_full, full_dense)
    grad_context_low = grad_context.astype(jnp.bfloat16) * valid_rows.astype(jnp.bfloat16)
    grad_down = contract_rows(hidden_act, grad_full)
    grad_act = contract_cols(grad_full, every_down)
    grad_pre = (grad_act * gelu_slope(hidden_pre)).astype(jnp.bfloat16)
    grad_up = contract_rows(normed_low, grad_pre)
    grad_ubias = jnp.sum(grad_pre, axis=0, dtype=jnp.float32)
    mlp_normed = contract_cols(grad_pre, every_up)
    grad_proj, grad_qbias = attention_backward(
        query, keys, values, grad_context_low, logsum, cos_wide, sin_wide, starts, lows
    )
    grad_qkv = jnp.einsum("td,cte->cde", normed_low, grad_proj, preferred_element_type=jnp.float32)
    grad_normed = jnp.einsum("cte,cde->td", grad_proj, full_qkv, preferred_element_type=jnp.float32)
    part_qkv, part_dense, part_up, part_down, part_qbias, part_ubias = (
        scatter_low(grad_qkv, "dp", 1),
        scatter_low(grad_dense, "dp", 1),
        scatter_low(grad_up, "dp", 0),
        scatter_low(grad_down, "dp", 1),
        lax.psum_scatter(grad_qbias, "dp", scatter_dimension=1, tiled=True),
        lax.psum_scatter(grad_ubias, "dp", scatter_dimension=0, tiled=True),
    )
    normed_term = grad_normed + mlp_normed
    grad_mine = scatter_low(normed_term, "tensor", 0)
    scaled = grad_mine * norm_gain
    grad_tokens = (
        cotangent.astype(jnp.float32)
        + inverse
        * (
            scaled
            - jnp.mean(scaled, axis=-1, keepdims=True)
            - normed * jnp.mean(scaled * normed, axis=-1, keepdims=True)
        )
    ).astype(jnp.bfloat16)
    part_gain, part_shift, part_obias = (
        lax.psum_scatter(
            jnp.sum(grad_mine * normed, axis=0), ("dp", "tensor"), scatter_dimension=0, tiled=True
        ),
        lax.psum_scatter(
            jnp.sum(grad_mine, axis=0), ("dp", "tensor"), scatter_dimension=0, tiled=True
        ),
        lax.psum_scatter(
            jnp.sum(cotangent, axis=0, dtype=jnp.float32),
            ("dp", "tensor"),
            scatter_dimension=0,
            tiled=True,
        ),
    )
    return (
        output,
        grad_tokens,
        part_gain,
        part_shift,
        part_qkv,
        part_qbias,
        part_dense,
        part_up,
        part_ubias,
        part_down,
        part_obias,
        root_squares,
    )


def solution(mesh):
    placed = (
        P(("dp", "tensor"), None),
        P("dp", None),
        P(),
        P(),
        P(None, "dp", "tensor"),
        P(None, ("tensor", "dp")),
        P("tensor", "dp"),
        P("dp", "tensor"),
        P(("tensor", "dp")),
        P("tensor", "dp"),
        P(),
        P(("dp", "tensor"), None),
    )
    return jax.shard_map(
        body,
        mesh=mesh,
        in_specs=placed,
        out_specs=(
            P(("dp", "tensor"), None),
            P(("dp", "tensor"), None),
            P(("dp", "tensor")),
            P(("dp", "tensor")),
            P(None, "dp", "tensor"),
            P(None, ("tensor", "dp")),
            P("tensor", "dp"),
            P("dp", "tensor"),
            P(("tensor", "dp")),
            P("tensor", "dp"),
            P(("dp", "tensor")),
            P(),
        ),
        check_vma=False,
    )
```

time: 2410 us -> 1310 us (0.54)
  matrix products: 697 us -> 251 us
  waiting for transfers between devices: 1140 us -> 775 us
  local copies, waits for them, and re-layouts: 232 us -> 21.4 us
  other arithmetic: 216 us -> 38.6 us
  Pallas kernels: 0 us -> 126 us
  loops' own time: 30.5 us -> 0 us
    dot_general x28 -> x0, matrix products: 443 us -> none  [the longest x8 161 us: masked_scores(): jnp.einsum('qhd,khd->hqk', query_block, key_seq, preferred_element_type=j...]
    reduce_scatter x7, waiting for transfers between devices: 952 us -> 517 us  [scatter_low(): lax.psum_scatter(part.astype(jnp.bfloat16), axis, scatter_dimension=dim,...]
    dynamic_update_slice x16 -> x0, local copies, waits for them, and re-layouts: 182 us -> none  [attention_forward(): lax.map(one_block, jnp.arange(seq_count * blocks, dtype=jnp.int32))]
    pallas_call x0 -> x2, Pallas kernels: none -> 126 us  [the longest x1 67.2 us: attention_backward(): pl.pallas_call(attend_back_kernel, grid_spec=pltpu.PrefetchScalarGridSpec...]
    convert_element_type x6 -> x4, other arithmetic: 110 us -> 7.27 us  [the longest x3 7.27 us: scatter_low(): return lax.psum_scatter(part.astype(jnp.bfloat16), axis, scatter_dimensio...]
    all_gather x1, waiting for transfers between devices: 0.01 us -> 100 us  [body(): grad_full = lax.all_gather(cotangent, 'tensor', axis=0, tiled=True)]
    reduce_sum x6 -> x2, other arithmetic: 73.3 us -> 9.97 us  [the longest x1 8.17 us: body(): jnp.sum(valid_mine * attn_mine * attn_mine)]
    another operation x2 -> x0, loops' own time: 30.5 us -> none  [the longest x1 22.3 us: per_seq(): lax.scan(block_step, (zeros_seq, zeros_seq), jnp.arange(blocks, dtype=jnp...]
  transfers between devices with their start and end apart: 14 -> 14, of which waited for: 7 -> 8; matrix products, arithmetic and copies ran while one was open for 47% -> 22% of each run, Pallas kernels for 0% -> 10%
where the time goes in v1:
time: 1310 us
  waiting for transfers between devices  775 us (59%)
  matrix products  251 us (19%)
  Pallas kernels  126 us (10%)
  blocking collectives  77.7 us (6%)
  other arithmetic  38.6 us (3%)
  local copies, waits for them, and re-layouts  21.4 us (2%)
  between operations  15.8 us (1%)
    reduce_scatter x7, waiting for transfers between devices, scatter_low(): lax.psum_scatter(part.astype(jnp.bfloat16), axis, scatter_dimension=dim,...  517 us
    all_gather x1, waiting for transfers between devices, body(): normed_low = lax.all_gather(normed_mine, 'tensor', axis=0, tiled=True)  152 us
    all_gather x1, waiting for transfers between devices, body(): grad_full = lax.all_gather(cotangent, 'tensor', axis=0, tiled=True)  100 us
    dot_general x3, matrix products, contract_cols(): lax.dot_general(left, right, (((1,), (1,)), ((), ())), preferred_element_...  70.5 us
    pallas_call x1, Pallas kernels, attention_backward(): pl.pallas_call(attend_back_kernel, grid_spec=pltpu.PrefetchScalarGridSpec...  67.2 us
    dot_general x3, matrix products, contract_rows(): lax.dot_general(left, right, (((0,), (0,)), ((), ())), preferred_element_...  61 us
    pallas_call x1, Pallas kernels, attention_forward(): pl.pallas_call(attend_kernel, grid_spec=pltpu.PrefetchScalarGridSpec(num_...  59.1 us
    unnamed x2, blocking collectives  58.3 us
  transfers between devices with their start and end apart: 14, of which 8 were waited for; matrix products, arithmetic and copies ran while one was open for 22% of the time, Pallas kernels for 10%

profile of v1, /device:TPU:0, one launch (start us, length us, event | category | flops | bytes accessed | tf_op | source)
XLA Modules:
  0.0 1306.7 jit_solution(759644740409612437)
XLA Ops:
  19.2 10.4 all-gather.1
  31.5 9.1 all-gather
  58.2 151.8 %all-gather.9.cloned.1.call-done = bf16[2048,2048]{1,0:T(8,128)(2,1)} async-done(((bf16[512,2048]{1,0:T(8,128)(2,1)}), bf16[2048,2048]{1,0:T(8,128)(2,1)}) %all-gather.9.cloned.1.call-update) | async-done | bytes 8388624 | tf_op jit(solution)/shard_map/all_gather | solution.py:348
  210.0 19.2 %fusion.15.xq_ref.xk_ref.xv_ref = f32[3,2048,512]{2,1,0:T(8,128)} fusion(bf16[3,2048,512]{2,1,0:T(8,128)(2,1)} %all-gather.11.cloned.1.call-done, bf16[2048,2048]{1,0:T(8,128)(2,1)} %all-gather.9.cloned.1.call-done), kind=kOutput, calls=%fused_computation.36 | convolution fusion | flops 12884901888 | bytes 27262976 | tf_op jit(solution)/shard_map/td,cde->cte/dot_general | solution.py:362
  229.9 59.1 %attend.1 = (bf16[2048,512]{1,0:T(8,128)(2,1)}, bf16[2048,512]{1,0:T(8,128)(2,1)}, bf16[2048,512]{1,0:T(8,128)(2,1)}, bf16[2048,512]{1,0:T(8,128)(2,1)}, f32[4,2,2048]{2,1,0:T(2,128)S(1)}) custom-call(s32[8]{0:T(128)S(1)} %and_select_fusion.low_ref, f32[3,2048,512]{2,1,0:T(8,128)} %fusion.15.xq_ref.xk_ref.xv_ref, ...), custom_call_target="tpu_custom_call" | custom-call | tf_op jit(solution)/shard_map/attend/pallas_call | solution.py:153
  289.1 100.4 %all-gather.19.cloned.1.call-done = bf16[2048,2048]{1,0:T(8,128)(2,1)} async-done(((bf16[512,2048]{1,0:T(8,128)(2,1)}), bf16[2048,2048]{1,0:T(8,128)(2,1)}) %all-gather.19.cloned.1.call-update) | async-done | bytes 8388624 | tf_op jit(solution)/shard_map/all_gather | solution.py:391
  389.5 10.0 fusion.37.do_ref
  399.5 67.2 %attend_back.1 = (bf16[3,2048,512]{2,1,0:T(8,128)(2,1)}, f32[3,1,512]{2,1,0:T(1,128)S(1)}) custom-call(s32[8]{0:T(128)S(1)} %and_select_fusion.low_ref, bf16[2048,512]{1,0:T(8,128)(2,1)S(1)} %copy-done, bf16[2048,512]{1,0:T(8,128)(2,1)} %get-tuple-element.21.k_ref, bf16[2048,512]{1,0:T(8,128)(2,1)} %get-tuple-element.22.v_ref, ...), custom_call_target="tpu_custom_call" | custom-call | tf_op jit(solution)/shard_map/attend_back/pallas_call | solution.py:265
  467.9 9.9 convolution_convert_fusion.4
  477.9 19.2 %convert_bitcast_fusion = bf16[3,2048,512]{1,2,0:T(8,128)(2,1)} fusion(bf16[3,2048,512]{2,1,0:T(8,128)(2,1)} %get-tuple-element.24, bf16[2048,2048]{1,0:T(8,128)(2,1)} %all-gather.9.cloned.1.call-done), kind=kOutput, calls=%fused_computation.29 | convolution fusion | flops 12888047616 | bytes 20971520 | tf_op jit(solution)/shard_map/td,cte->cde/dot_general | solution.py:404
  497.5 24.6 %fusion.41 = f32[2048,2048]{1,0:T(8,128)} fusion(bf16[2048,2048]{1,0:T(8,128)(2,1)} %all-gather.9.cloned.1.call-done, bf16[2048,2048]{1,0:T(8,128)(2,1)} %all-gather.15.cloned.1.call-done), kind=kOutput, calls=%fused_computation.79 | convolution fusion | flops 17179869184 | bytes 33554432 | tf_op jit(solution)/shard_map/dot_general | solution.py:370
  522.2 35.0 %convert_reduce_fusion = (f32[2048]{0:T(1024)}, bf16[2048,2048]{1,0:T(8,128)(2,1)}) fusion(f32[2048,2048]{1,0:T(8,128)} %fusion.41, f32[2048]{0:T(1024)S(1)} %bitcast.63, bf16[2048,2048]{1,0:T(8,128)(2,1)} %all-gather.19.cloned.1.call-done, bf16[2048,2048]{1,0:T(8,128)(2,1)} %all-gather.17.cloned.1.call-done), kind=kOutput, calls=%fused_computation.11 | convolution fusion | flops 17272141824 | bytes 41959424 | tf_op jit(solution)/shard_map/dot_general | solution.py:313
  557.2 24.0 %convolution_convert_fusion.1 = bf16[2048,2048]{1,0:T(8,128)(2,1)} fusion(bf16[2048,2048]{1,0:T(8,128)(2,1)} %all-gather.9.cloned.1.call-done, bf16[2048,2048]{1,0:T(8,128)(2,1)} %get-tuple-element.102), kind=kOutput, calls=%fused_computation.24 | convolution fusion | flops 17184063488 | bytes 25165824 | tf_op jit(solution)/shard_map/dot_general | solution.py:307
  581.2 27.1 %convolution_convert_fusion = bf16[2048,2048]{1,0:T(8,128)(2,1)} fusion(bf16[2048,2048]{1,0:T(8,128)(2,1)} %all-gather.19.cloned.1.call-done, f32[2048,2048]{1,0:T(8,128)} %fusion.41, f32[2048]{0:T(1024)S(1)} %bitcast.64), kind=kOutput, calls=%fused_computation.23 | convolution fusion | flops 17226006528 | bytes 33562624 | tf_op jit(solution)/shard_map/dot_general | solution.py:307
  609.9 8.4 convolution_convert_fusion.3
  618.4 19.9 %fusion.42 = f32[2048,2048,1]{1,0,2:T(8,128)} fusion(bf16[3,2048,512]{2,1,0:T(8,128)(2,1)} %get-tuple-element.24, bf16[3,2048,512]{2,1,0:T(8,128)(2,1)} %all-gather.11.cloned.1.call-done), kind=kOutput, calls=%fused_computation.80 | convolution fusion | flops 12884901888 | bytes 29360128 | tf_op jit(solution)/shard_map/cte,cde->td/dot_general | solution.py:405
  638.2 25.5 %fusion.7 = bf16[2048,2048]{1,0:T(8,128)(2,1)} fusion(f32[2048,2048,1]{1,0,2:T(8,128)} %fusion.42, bf16[2048,2048]{1,0:T(8,128)(2,1)} %get-tuple-element.102, bf16[2048,2048]{1,0:T(8,128)(2,1)} %all-gather.15.cloned.1.call-done), kind=kOutput, calls=%fused_computation.10 | convolution fusion | flops 17188257792 | bytes 41943040 | tf_op jit(solution)/shard_map/dot_general | solution.py:313
  663.8 28.4 %convolution_convert_fusion.2 = bf16[2048,2048]{1,0:T(8,128)(2,1)} fusion(bf16[2048,2048]{1,0:T(8,128)(2,1)} %all-gather.17.cloned.1.call-done, f32[2048,2048]{1,0:T(8,128)} %fusion.41, f32[2048]{0:T(1024)S(1)} %bitcast.65), kind=kOutput, calls=%fused_computation.25 | convolution fusion | flops 17226006528 | bytes 33562624 | tf_op jit(solution)/shard_map/dot_general | solution.py:374
  697.4 16.5 %all-reduce.2 = f32[2048]{0:T(1024)S(1)} all-reduce(f32[2048]{0:T(1024)S(1)} %copy-done.11), channel_id=11, replica_groups=mesh['dp'=8,'tensor'=4] {'dp'}, use_global_device_ids=true, to_apply=%region_17.18.clone | all-reduce | flops 2048 | bytes 16384
  727.4 72.0 %reduce-scatter.23.cloned.1.call-done = bf16[2048,256]{1,0:T(8,128)(2,1)} async-done(((bf16[2048,2048]{1,0:T(8,128)(2,1)}), bf16[2048,256]{1,0:T(8,128)(2,1)}) %reduce-scatter.23.cloned.1.call-update) | async-done | bytes 1048592 | tf_op jit(solution)/shard_map/reduce_scatter | solution.py:319
  802.1 144.1 %reduce-scatter.11.cloned.1.call-done = bf16[512,2048]{1,0:T(8,128)(2,1)} async-done(((bf16[2048,2048]{1,0:T(8,128)(2,1)}), bf16[512,2048]{1,0:T(8,128)(2,1)}) %reduce-scatter.11.cloned.1.call-update) | async-done | bytes 2097168 | tf_op jit(solution)/shard_map/reduce_scatter | solution.py:319
  946.2 147.7 %reduce-scatter.15.cloned.1.call-done = bf16[512,2048]{1,0:T(8,128)(2,1)} async-done(((bf16[2048,2048]{1,0:T(8,128)(2,1)}), bf16[512,2048]{1,0:T(8,128)(2,1)}) %reduce-scatter.15.cloned.1.call-update) | async-done | bytes 2097168 | tf_op jit(solution)/shard_map/reduce_scatter | solution.py:319
  1093.9 147.6 %reduce-scatter.13.cloned.1.call-done = bf16[512,2048]{1,0:T(8,128)(2,1)} async-done(((bf16[2048,2048]{1,0:T(8,128)(2,1)}), bf16[512,2048]{1,0:T(8,128)(2,1)}) %reduce-scatter.13.cloned.1.call-update) | async-done | bytes 2097168 | tf_op jit(solution)/shard_map/reduce_scatter | solution.py:319
  1253.2 41.8 %all-reduce.4 = (f32[2048]{0:T(1024)S(1)}, f32[2048]{0:T(1024)S(1)}, f32[2048]{0:T(1024)S(1)}, f32[1]{0:T(128)}, f32[1]{0:T(128)}, /*index=5*/f32[1]{0:T(128)}, f32[]{:T(128)}) all-reduce(f32[2048]{0:T(1024)S(1)} %get-tuple-element.95, f32[2048]{0:T(1024)S(1)} %get-tuple-element.91, ...), channel_id=5, replica_groups=mesh['dp'=8,'tensor'=4] {'dp','tensor'}, use_global_device_ids=true, to_apply=%region_9.10.clone | all-reduce | flops 6148 | bytes 49184
  (110 shorter events, 72.1 us)
Async XLA Ops:
  7.2 12.0 copy-start.15
  7.2 22.3 %copy-start.10 = (s32[1,2048]{1,0:T(1,128)S(1)}, s32[1,2048]{1,0:T(1,128)}, u32[]{:S(2)}) copy-start(s32[1,2048]{1,0:T(1,128)} %param.13) | copy-start | bytes 24580
  7.2 24.3 %copy-start.13 = (bf16[3,64]{1,0:T(4,128)(2,1)S(1)}, bf16[3,64]{1,0:T(4,128)(2,1)}, u32[]{:S(2)}) copy-start(bf16[3,64]{1,0:T(4,128)(2,1)} %param.17) | copy-start | bytes 1156
  7.2 51.0 %all-gather.11.cloned.1.call-start = ((), (), s32[]{:S(2)}) async-start(), calls=%async_computation.9 | async-start | bytes 7077888 | tf_op jit(solution)/shard_map/all_gather | solution.py:350
  7.9 202.1 %all-gather.9.cloned.1.call-start = ((), (), s32[]{:S(2)}) async-start(), calls=%async_computation.8 | async-start | bytes 10485760 | tf_op jit(solution)/shard_map/all_gather | solution.py:348
  16.6 272.4 %all-gather.13.cloned.1.call-start = ((), (), s32[]{:S(2)}) async-start(), calls=%async_computation.10 | async-start | bytes 2359296 | tf_op jit(solution)/shard_map/all_gather | solution.py:351
  17.3 372.2 %all-gather.19.cloned.1.call-start = ((), (), s32[]{:S(2)}) async-start(), calls=%async_computation.15 | async-start | bytes 10485760 | tf_op jit(solution)/shard_map/all_gather | solution.py:391
  17.9 479.6 %all-gather.15.cloned.1.call-start = ((), (), s32[]{:S(2)}) async-start(), calls=%async_computation.12 | async-start | bytes 9437184 | tf_op jit(solution)/shard_map/all_gather | solution.py:352
  18.5 503.7 %all-gather.17.cloned.1.call-start = ((), (), s32[]{:S(2)}) async-start(), calls=%async_computation.13 | async-start | bytes 9437184 | tf_op jit(solution)/shard_map/all_gather | solution.py:353
  19.1 676.9 %reduce-scatter.25.cloned.1.call-start = ((), (), s32[]{:S(2)}) async-start(), calls=%async_computation.21 | async-start | bytes 294912
  31.5 197.8 %copy-start.4 = (f32[1,2048]{1,0:T(1,128)}, f32[1,2048]{1,0:T(1,128)S(1)}, u32[]{:S(2)}) copy-start(f32[1,2048]{1,0:T(1,128)S(1)} %compare_convert_fusion) | copy-start | bytes 24580
  389.5 10.0 copy-start
  467.6 246.9 %reduce-scatter.19.cloned.1.call-start = ((), (), s32[]{:S(2)}) async-start(), calls=%async_computation.18 | async-start | bytes 2359296 | tf_op jit(solution)/shard_map/reduce_scatter | solution.py:319
  477.8 238.5 %reduce-scatter.17.cloned.1.call-start = ((), (), s32[]{:S(2)}) async-start(), calls=%async_computation.17 | async-start | bytes 7077888 | tf_op jit(solution)/shard_map/reduce_scatter | solution.py:319
  497.1 227.5 %reduce-scatter.21.cloned.1.call-start = ((), (), s32[]{:S(2)}) async-start(), calls=%async_computation.19 | async-start | bytes 9437184 | tf_op jit(solution)/shard_map/reduce_scatter | solution.py:319
  581.2 218.2 %reduce-scatter.23.cloned.1.call-start = ((), (), s32[]{:S(2)}) async-start(), calls=%async_computation.20 | async-start | bytes 9437184 | tf_op jit(solution)/shard_map/reduce_scatter | solution.py:319
  608.3 337.8 %reduce-scatter.11.cloned.1.call-start = ((), (), s32[]{:S(2)}) async-start(), calls=%async_computation.11 | async-start | bytes 10485760 | tf_op jit(solution)/shard_map/reduce_scatter | solution.py:319
  618.3 475.6 %reduce-scatter.15.cloned.1.call-start = ((), (), s32[]{:S(2)}) async-start(), calls=%async_computation.16 | async-start | bytes 10485760 | tf_op jit(solution)/shard_map/reduce_scatter | solution.py:319
  663.7 577.7 %reduce-scatter.13.cloned.1.call-start = ((), (), s32[]{:S(2)}) async-start(), calls=%async_computation.14 | async-start | bytes 10485760 | tf_op jit(solution)/shard_map/reduce_scatter | solution.py:319
  692.2 549.3 %copy-start.1 = (bf16[512,2048]{1,0:T(8,128)(2,1)S(1)}, bf16[512,2048]{1,0:T(8,128)(2,1)}, u32[]{:S(2)}) copy-start(bf16[512,2048]{1,0:T(8,128)(2,1)} %param.12) | copy-start | bytes 6291460
  692.2 549.3 %copy-start.5 = (f32[2048]{0:T(1024)S(1)}, f32[2048]{0:T(1024)}, u32[]{:S(2)}) copy-start(f32[2048]{0:T(1024)} %param.14) | copy-start | bytes 24580
  692.2 549.3 %copy-start.7 = (f32[512]{0:T(512)S(1)}, f32[512]{0:T(512)}, u32[]{:S(2)}) copy-start(f32[512]{0:T(512)} %copy-done.6) | copy-start | bytes 6148
  692.2 549.3 %copy-start.9 = (f32[512]{0:T(512)S(1)}, f32[512]{0:T(512)}, u32[]{:S(2)}) copy-start(f32[512]{0:T(512)} %copy-done.8) | copy-start | bytes 6148
  692.2 549.3 %copy-start.12 = (f32[2048]{0:T(1024)S(1)}, f32[2048]{0:T(1024)}, u32[]{:S(2)}) copy-start(f32[2048]{0:T(1024)} %param.22) | copy-start | bytes 24580
  (7 other events, 26.8 us)
Sparse Core Ops, SparseCore 0:
  9.9 48.2 all-gather.10
  60.4 149.6 all-gather.8
  211.9 26.4 all-gather.12
  239.8 149.6 all-gather.18
  391.2 52.5 all-gather.14
  445.6 55.9 all-gather.16
  505.2 33.6 reduce-scatter.24
  543.1 41.2 reduce-scatter.18
  587.7 61.7 reduce-scatter.16
  653.2 71.3 reduce-scatter.20
  728.1 71.2 reduce-scatter.22
  801.7 144.4 reduce-scatter.10
  948.7 145.1 reduce-scatter.14
  1096.2 145.1 reduce-scatter.12

commit v2 on v1

v2 whole, which is shorter than its diff:
```python
import functools
import math

import jax
import jax.numpy as jnp
from jax import lax
from jax.experimental import pallas as pl
from jax.experimental.pallas import tpu as pltpu
from jax.sharding import PartitionSpec as P

HEAD_DIM = 64
ROT = 32
PAIR = 2 * HEAD_DIM
BLOCK = 256
MOST = 5

EPS = 1e-05
GELU_C = math.sqrt(2.0 / math.pi)


def segment_starts(segs):
    return jnp.sum((segs[:, None, :] < segs[:, :, None]).astype(jnp.int32), axis=-1)


def rotary_wide(starts):
    length = starts.shape[0]
    half_rot = ROT // 2
    frequency = jnp.exp(-math.log(10000.0) * (2.0 * jnp.arange(half_rot, dtype=jnp.float32) / ROT))
    position = jnp.arange(length, dtype=jnp.int32) - starts
    angles = position.astype(jnp.float32)[:, None] * frequency
    cosines, sines = jnp.cos(angles), jnp.sin(angles)
    ones = jnp.ones((length, HEAD_DIM - ROT), jnp.float32)
    cos_head = jnp.concatenate([cosines, cosines, ones], axis=-1)
    sin_head = jnp.concatenate([-sines, sines, 0.0 * ones], axis=-1)
    return (jnp.concatenate([cos_head, cos_head], -1), jnp.concatenate([sin_head, sin_head], -1))


def turn(x, cos_wide, sin_wide):
    lane = lax.broadcasted_iota(jnp.int32, x.shape, 1) % HEAD_DIM
    half_rot = ROT // 2
    partner = jnp.where(
        lane < half_rot, pltpu.roll(x, PAIR - half_rot, 1), pltpu.roll(x, half_rot, 1)
    )
    return x * cos_wide + partner * sin_wide


def first_half(shape):
    return lax.broadcasted_iota(jnp.int32, shape, len(shape) - 1) < HEAD_DIM


def halves(x):
    front = first_half(x.shape)
    zero = jnp.zeros_like(x)
    return (jnp.where(front, x, zero), jnp.where(front, zero, x))


def nt(left, right):
    return lax.dot_general(
        left, right, (((1,), (1,)), ((), ())), preferred_element_type=jnp.float32
    )


def nn(left, right):
    return lax.dot_general(
        left, right, (((1,), (0,)), ((), ())), preferred_element_type=jnp.float32
    )


def tn(left, right):
    return lax.dot_general(
        left, right, (((0,), (0,)), ((), ())), preferred_element_type=jnp.float32
    )


def attend_kernel(
    low_ref, place_ref, parts, bias_ref, cos_ref, sin_ref, start_ref, valid_ref,
    q_ref, k_ref, v_ref, ctx_ref, lse_ref, km, vm,
):
    length = q_ref.shape[0]
    blocks = length // BLOCK
    scale = 1.0 / math.sqrt(HEAD_DIM)

    per = length // len(parts) // BLOCK

    def project(i, slot):
        rows = pl.ds(pl.multiple_of(place_ref[slot * per + i] * BLOCK, BLOCK), BLOCK)
        here = pl.ds(i * BLOCK, BLOCK)
        part = parts[slot]
        cw, sw = cos_ref[rows, :], sin_ref[rows, :]
        q = turn(part[0, here, :] + bias_ref[0], cw, sw).astype(jnp.bfloat16)
        q_ref[rows, :] = q * jnp.bfloat16(scale)
        k = turn(part[1, here, :] + bias_ref[1], cw, sw).astype(jnp.bfloat16)
        k_ref[rows, :] = k
        v = (part[2, here, :] + bias_ref[2]).astype(jnp.bfloat16)
        v_ref[rows, :] = v
        km[0, rows, :], km[1, rows, :] = halves(k)
        vm[0, rows, :], vm[1, rows, :] = halves(v)

    for slot in range(len(parts)):
        for i in range(per):
            project(i, slot)

    def query_block(i, count):
        rows = pl.ds(pl.multiple_of(i * BLOCK, BLOCK), BLOCK)
        base = pl.multiple_of((i + 1 - count) * BLOCK, BLOCK)
        cols = pl.ds(base, count * BLOCK)
        shape = (BLOCK, count * BLOCK)
        q = q_ref[rows, :]
        start = start_ref[rows, :][:, :1] - base
        kpos = lax.broadcasted_iota(jnp.int32, shape, 1)
        qpos = lax.broadcasted_iota(jnp.int32, shape, 0) + (count - 1) * BLOCK
        allowed = (kpos >= start) & (kpos <= qpos)
        there = pl.ds(pl.multiple_of(place_ref[i] * BLOCK, BLOCK), BLOCK)
        acc = jnp.zeros((BLOCK, PAIR), jnp.float32)
        tops, sums = [], []
        for h in range(2):
            s = jnp.where(allowed, nt(q, km[h, cols, :]), -jnp.inf)
            top = jnp.max(s, axis=-1, keepdims=True)
            e = jnp.exp(s - top)
            tops.append(top)
            sums.append(jnp.sum(e, axis=-1, keepdims=True))
            acc = acc + nn(e.astype(jnp.bfloat16), vm[h, cols, :])
        front = first_half((BLOCK, PAIR))
        out = acc / jnp.where(front, sums[0], sums[1])
        ctx_ref[there, :] = (out * valid_ref[rows, :]).astype(jnp.bfloat16)
        lse = jnp.where(front, tops[0] + jnp.log(sums[0]), tops[1] + jnp.log(sums[1]))
        lse_t = lse.T
        lse_ref[0, 0:1, rows] = lse_t[0:1, :]
        lse_ref[0, 1:2, rows] = lse_t[HEAD_DIM : HEAD_DIM + 1, :]

    def step(i, _):
        for count in range(1, MOST + 1):
            pl.when(i + 1 - low_ref[i] == count)(functools.partial(query_block, i, count))
        return 0

    lax.fori_loop(0, blocks, step, 0)


def attention_forward(projected, bias, tables, first, count, held=None):
    cos_wide, sin_wide, starts, valid_wide, lows, places = tables
    width = projected[0].shape[2]
    length = starts.shape[0]
    blocks = length // BLOCK
    ways = len(projected)
    start_wide = jnp.broadcast_to(starts[:, None], (length, PAIR))
    part = pl.BlockSpec((3, length // ways, PAIR), lambda p, low, place: (0, 0, p + first))
    table = pl.BlockSpec((length, PAIR), lambda p, low, place: (0, 0))
    flat = pl.BlockSpec((length, PAIR), lambda p, low, place: (0, p + first))
    flat_shape = jax.ShapeDtypeStruct((length, width), jnp.bfloat16)
    held = tuple(held or ())

    def kernel(*refs):
        rest = refs[2 + ways :]
        attend_kernel(*refs[:2], refs[2 : 2 + ways], *rest[:5], *rest[5 + len(held) :])

    return pl.pallas_call(
        kernel,
        grid_spec=pltpu.PrefetchScalarGridSpec(
            num_scalar_prefetch=2,
            grid=(count,),
            in_specs=[
                *[part] * ways,
                pl.BlockSpec((3, 1, PAIR), lambda p, low, place: (0, 0, p + first)),
                table, table, table, table,
            ] + [pl.BlockSpec(memory_space=pl.ANY)] * len(held),
            out_specs=[flat, flat, flat, flat,
                       pl.BlockSpec((1, 2, length), lambda p, low, place: (p + first, 0, 0))],
            scratch_shapes=[
                pltpu.VMEM((2, length, PAIR), jnp.bfloat16),
                pltpu.VMEM((2, length, PAIR), jnp.bfloat16),
            ],
        ),
        out_shape=[flat_shape] * 4
        + [jax.ShapeDtypeStruct((width // PAIR, 2, length), jnp.float32)],
        input_output_aliases={7 + ways + i: i for i in range(len(held))},
        compiler_params=pltpu.CompilerParams(vmem_limit_bytes=48 * 2**20),
        name="attend",
    )(lows, places, *projected, bias[:, None, :], cos_wide, sin_wide,
      start_wide, valid_wide, *held)


def attend_back_kernel(
    low_ref, place_ref, dos, q_ref, k_ref, v_ref, lse_ref, cos_ref, sin_ref, start_ref, valid_ref,
    grad_ref, sums_ref, qm, km, vm, dom, do_scr, dk_acc, dv_acc,
):
    length = q_ref.shape[0]
    blocks = length // BLOCK
    scale = 1.0 / math.sqrt(HEAD_DIM)

    def split(i, _):
        rows = pl.ds(pl.multiple_of(i * BLOCK, BLOCK), BLOCK)
        qm[0, rows, :], qm[1, rows, :] = halves(q_ref[rows, :])
        km[0, rows, :], km[1, rows, :] = halves(k_ref[rows, :])
        vm[0, rows, :], vm[1, rows, :] = halves(v_ref[rows, :])
        dk_acc[rows, :] = jnp.zeros((BLOCK, PAIR), jnp.float32)
        dv_acc[rows, :] = jnp.zeros((BLOCK, PAIR), jnp.float32)
        return 0

    lax.fori_loop(0, blocks, split, 0)

    per = length // len(dos) // BLOCK
    for slot in range(len(dos)):
        for i in range(per):
            rows = pl.ds(pl.multiple_of(place_ref[slot * per + i] * BLOCK, BLOCK), BLOCK)
            do = dos[slot][i * BLOCK : (i + 1) * BLOCK, :].astype(jnp.float32)
            do = (do * valid_ref[rows, :]).astype(jnp.bfloat16)
            do_scr[rows, :] = do
            dom[0, rows, :], dom[1, rows, :] = halves(do)

    def query_block(i, count):
        rows = pl.ds(pl.multiple_of(i * BLOCK, BLOCK), BLOCK)
        base = pl.multiple_of((i + 1 - count) * BLOCK, BLOCK)
        cols = pl.ds(base, count * BLOCK)
        shape = (count * BLOCK, BLOCK)
        q = q_ref[rows, :]
        do = do_scr[rows, :]
        start = start_ref[:, rows] - base
        kpos = lax.broadcasted_iota(jnp.int32, shape, 0)
        qpos = lax.broadcasted_iota(jnp.int32, shape, 1) + (count - 1) * BLOCK
        allowed = (kpos >= start) & (kpos <= qpos)
        dk = dk_acc[cols, :]
        dv = dv_acc[cols, :]
        dq = jnp.zeros((BLOCK, PAIR), jnp.float32)
        for h in range(2):
            s = nt(km[h, cols, :], q)
            p = jnp.where(allowed, jnp.exp(s - lse_ref[0, h : h + 1, rows]), 0.0)
            dp = nt(vm[h, cols, :], do)
            delta = jnp.sum(p * dp, axis=0, keepdims=True)
            dv = dv + nn(p.astype(jnp.bfloat16), dom[h, rows, :])
            ds = (p * (dp - delta)).astype(jnp.bfloat16)
            dk = dk + nn(ds, qm[h, rows, :])
            dq = dq + tn(ds, km[h, cols, :])
        dk_acc[cols, :] = dk
        dv_acc[cols, :] = dv
        dq = turn(dq * scale, cos_ref[rows, :], -sin_ref[rows, :]).astype(jnp.bfloat16)
        there = pl.ds(pl.multiple_of(place_ref[i] * BLOCK, BLOCK), BLOCK)
        grad_ref[0, there, :] = dq
        sums_ref[0] += jnp.sum(dq.astype(jnp.float32), axis=0, keepdims=True)

    none = jnp.zeros((1, PAIR), jnp.float32)
    sums_ref[0] = none

    def step(i, _):
        for count in range(1, MOST + 1):
            pl.when(i + 1 - low_ref[i] == count)(functools.partial(query_block, i, count))
        return 0

    lax.fori_loop(0, blocks, step, 0)

    def finish(i, totals):
        rows = pl.ds(pl.multiple_of(i * BLOCK, BLOCK), BLOCK)
        dk = turn(dk_acc[rows, :], cos_ref[rows, :], -sin_ref[rows, :]).astype(jnp.bfloat16)
        dv = dv_acc[rows, :].astype(jnp.bfloat16)
        there = pl.ds(pl.multiple_of(place_ref[i] * BLOCK, BLOCK), BLOCK)
        grad_ref[1, there, :] = dk
        grad_ref[2, there, :] = dv
        return (
            totals[0] + jnp.sum(dk.astype(jnp.float32), axis=0, keepdims=True),
            totals[1] + jnp.sum(dv.astype(jnp.float32), axis=0, keepdims=True),
        )

    sums_ref[1], sums_ref[2] = lax.fori_loop(0, blocks, finish, (none, none))


def attention_backward(q, k, v, do, lse, tables, first, count, held=None):
    cos_wide, sin_wide, starts, valid_wide, lows, places = tables
    length, width = q.shape
    blocks = length // BLOCK
    flat = pl.BlockSpec((length, PAIR), lambda p, low, place: (0, p + first))
    table = pl.BlockSpec((length, PAIR), lambda p, low, place: (0, 0))
    held = tuple(held or ())
    ways = len(do)

    def kernel(*refs):
        rest = refs[2 + ways :]
        attend_back_kernel(*refs[:2], refs[2 : 2 + ways], *rest[:8], *rest[8 + len(held) :])

    return pl.pallas_call(
        kernel,
        grid_spec=pltpu.PrefetchScalarGridSpec(
            num_scalar_prefetch=2,
            grid=(count,),
            in_specs=[
                *[pl.BlockSpec((length // ways, PAIR), lambda p, low, place: (0, p + first))] * ways,
                flat, flat, flat,
                pl.BlockSpec((1, 2, length), lambda p, low, place: (p + first, 0, 0)),
                table, table,
                pl.BlockSpec((1, length), lambda p, low, place: (0, 0)),
                table,
            ] + [pl.BlockSpec(memory_space=pl.ANY)] * len(held),
            out_specs=[
                pl.BlockSpec((3, length, PAIR), lambda p, low, place: (0, 0, p + first)),
                pl.BlockSpec((3, 1, PAIR), lambda p, low, place: (0, 0, p + first)),
            ],
            scratch_shapes=[pltpu.VMEM((2, length, PAIR), jnp.bfloat16)] * 4
            + [pltpu.VMEM((length, PAIR), jnp.bfloat16)]
            + [pltpu.VMEM((length, PAIR), jnp.float32)] * 2,
        ),
        out_shape=[
            jax.ShapeDtypeStruct((3, length, width), jnp.bfloat16),
            jax.ShapeDtypeStruct((3, 1, width), jnp.float32),
        ],
        input_output_aliases={10 + ways + i: i for i in range(len(held))},
        compiler_params=pltpu.CompilerParams(vmem_limit_bytes=48 * 2**20),
        name="attend_back",
    )(lows, places, *do, q, k, v, lse, cos_wide, sin_wide, starts[None, :], valid_wide, *held)


def gelu_and_slope(u):
    tanh_value = jnp.tanh(GELU_C * (u + 0.044715 * u * u * u))
    value = 0.5 * u * (1.0 + tanh_value)
    slope = 0.5 * (1.0 + tanh_value) + 0.5 * u * (1.0 - tanh_value * tanh_value) * GELU_C * (
        1.0 + 3.0 * 0.044715 * u * u
    )
    return (value, slope)


def contract_rows(left, right):
    return lax.dot_general(
        left, right, (((0,), (0,)), ((), ())), preferred_element_type=jnp.float32
    )


def contract_cols(left, right):
    return lax.dot_general(
        left, right, (((1,), (1,)), ((), ())), preferred_element_type=jnp.float32
    )


def shift(x, pairs):
    return lax.ppermute(x, "tensor", pairs)


class LineGather:
    def __init__(self, x):
        self.up, self.down = [x], [x]

    def step(self):
        n, k = lax.axis_size("tensor"), len(self.up)
        self.up.append(shift(self.up[-1], [(i, i + 1) for i in range(k - 1, n - 1)]))
        self.down.append(shift(self.down[-1], [(i, i - 1) for i in range(1, n - k + 1)]))

    def block(self, k):
        n, me = lax.axis_size("tensor"), lax.axis_index("tensor")
        return jnp.where(me >= k, self.up[k], self.down[n - k]) if k else self.up[0]


class RingScatter:
    def __init__(self, parts, rows):
        self.parts, self.rows, self.k, self.up, self.down = list(parts), rows, 0, None, None

    def next(self):
        place = self.k * self.rows
        for part in self.parts:
            if place < part.shape[0]:
                return part[place : place + self.rows]
            place -= part.shape[0]

    def step(self):
        n, mine = lax.axis_size("tensor"), self.next()
        if self.k:
            mine = (mine.astype(jnp.float32) + self.up.astype(jnp.float32)).astype(jnp.bfloat16)
        self.up = shift(mine, [(i, (i + 1) % n) for i in range(n)])
        self.k += 1

    def total(self):
        return self.next().astype(jnp.float32) + self.up.astype(jnp.float32)


class LineScatter:
    def __init__(self, parts):
        self.parts, self.k, self.up, self.down = parts, 1, None, None

    def step(self):
        n, k = lax.axis_size("tensor"), self.k
        mine_up, mine_down = self.parts[k], self.parts[n - k]
        if k > 1:
            mine_up = mine_up.astype(jnp.float32) + self.up.astype(jnp.float32)
            mine_down = mine_down.astype(jnp.float32) + self.down.astype(jnp.float32)
        self.up = shift(mine_up.astype(jnp.bfloat16), [(i, i + 1) for i in range(k)])
        self.down = shift(mine_down.astype(jnp.bfloat16), [(i, i - 1) for i in range(n - k, n)])
        self.k = k + 1

    def total(self):
        return sum(x.astype(jnp.float32) for x in (self.parts[0], self.up, self.down))


def together(*moves, after=()):
    state = [
        (m.up[-1], m.down[-1]) if isinstance(m, LineGather) else (m.parts, m.up, m.down)
        for m in moves
    ]
    state, after = lax.optimization_barrier((state, after))
    for m, kept in zip(moves, state):
        if isinstance(m, LineGather):
            m.up[-1], m.down[-1] = kept
        else:
            m.parts, m.up, m.down = kept
    return after


def blocks_of(whole, n):
    rows = whole.shape[0] // n
    return [whole[k * rows : (k + 1) * rows] for k in range(n)]


def scatter_low(part, axis, dim):
    return lax.psum_scatter(
        part.astype(jnp.bfloat16), axis, scatter_dimension=dim, tiled=True
    ).astype(jnp.float32)


def body(
    tokens,
    segments,
    norm_gain,
    norm_shift,
    qkv_weight,
    qkv_bias,
    dense_weight,
    up_weight,
    up_bias,
    down_weight,
    out_bias,
    cotangent,
):
    row_count, model_width = tokens.shape
    length = segments.shape[1]
    ways, copies = lax.axis_size("tensor"), lax.axis_size("dp")
    me = lax.axis_index("tensor")
    low = jnp.bfloat16
    resid = tokens.astype(jnp.float32)
    row_mean = jnp.mean(resid, axis=-1, keepdims=True)
    centered = resid - row_mean
    inverse = lax.rsqrt(jnp.mean(centered * centered, axis=-1, keepdims=True) + EPS)
    normed = centered * inverse
    normed_mine = (normed * norm_gain + norm_shift).astype(low)
    full_qkv = lax.all_gather(qkv_weight, "dp", axis=1, tiled=True)
    normed_mine, up_weight, down_weight, dense_weight = lax.optimization_barrier(
        (normed_mine, up_weight, down_weight, dense_weight)
    )
    full_up = lax.all_gather(up_weight, "dp", axis=0, tiled=True)
    full_down = lax.all_gather(down_weight, "dp", axis=1, tiled=True)
    full_dense = lax.all_gather(dense_weight, "dp", axis=1, tiled=True)
    around = [(i, (i + 1) % ways) for i in range(ways)]
    ring = [normed_mine, shift(normed_mine, around)]

    biases = jnp.concatenate([qkv_bias.reshape(-1), up_bias])
    biases = lax.all_gather(biases, "dp", axis=0).astype(jnp.float32)
    third = qkv_bias.shape[1]
    full_qbias = biases[:, : 3 * third].reshape(copies, 3, third)
    full_qbias = full_qbias.transpose(1, 0, 2).reshape(3, copies * third)
    full_ubias = biases[:, 3 * third :].reshape(-1)

    starts = segment_starts(segments)[0]
    cos_wide, sin_wide = rotary_wide(starts)
    valid_rows = (segments != 0).astype(jnp.float32).reshape(length, 1)
    valid_wide = jnp.broadcast_to(valid_rows, (length, PAIR))
    lows = starts[::BLOCK] // BLOCK
    chunk = jnp.arange(length // BLOCK, dtype=jnp.int32)
    per = row_count // BLOCK
    places = (me - 1 - chunk // per) % ways * per + chunk % per

    tables = (cos_wide, sin_wide, starts, valid_wide, lows, places)
    valid_mine = lax.dynamic_slice_in_dim(valid_rows, me * row_count, row_count, 0)
    cot_columns = jnp.sum(cotangent, axis=0, dtype=jnp.float32)
    resid_square = jnp.sum(valid_mine * resid * resid)
    fixed = lax.optimization_barrier
    ring[1], cot_mine, tables, full_qbias, full_ubias, cot_columns, resid_square = fixed(
        (ring[1], cotangent, tables, full_qbias, full_ubias, cot_columns, resid_square)
    )
    pairs = full_qkv.shape[2] // PAIR
    half = max(1, pairs // 2)
    projected, slopes, hidden_act, mlp_parts = ([None] * ways for _ in range(4))
    grad_context, grad_pre, pre_sums = ([None] * ways for _ in range(3))

    def turned(blocks):
        return [*blocks[1:], blocks[0]]

    def project(k):
        projected[k] = jnp.einsum(
            "td,cde->cte", ring[k], full_qkv, preferred_element_type=jnp.float32
        )

    def widen(k):
        pre = jnp.dot(ring[k], full_up, preferred_element_type=jnp.float32) + full_ubias
        value, slopes[k] = gelu_and_slope(pre)
        hidden_act[k] = value.astype(low)

    def narrow(k):
        mlp_parts[k] = jnp.dot(
            hidden_act[k], full_down, preferred_element_type=jnp.float32
        ).astype(low)

    def back(k):
        block = cot.block(k)
        grad_context[k] = contract_cols(block, full_dense).astype(low)
        grad_act = contract_cols(block, full_down)
        grad_pre[k] = (grad_act * slopes[k]).astype(low)
        pre_sums[k] = jnp.sum(grad_pre[k], axis=0, dtype=jnp.float32)

    for k in range(2, ways):
        coming = shift(ring[k - 1], around)
        if k == 2:
            project(0)
            project(1)
        if k == ways - 1:
            for j in range(ways - 1):
                if projected[j] is None:
                    project(j)
                widen(j)
        coming, ring, projected, slopes, hidden_act, cot_mine = fixed(
            (coming, ring, projected, slopes, hidden_act, cot_mine)
        )
        ring.append(coming)

    cot = LineGather(cot_mine)
    cot.step()
    project(ways - 1)
    widen(ways - 1)
    for k in range(ways):
        narrow(k)
    ring, projected, slopes, hidden_act, mlp_parts = together(
        cot, after=(ring, projected, slopes, hidden_act, mlp_parts)
    )

    mlp = LineScatter(mlp_parts)
    while len(cot.up) < ways - 1:
        cot.step()
        mlp.step()
    attended = attention_forward(turned(projected), full_qbias, tables, 0, pairs)
    query, keys, values, context_low, logsum = attended
    mix = lambda rows: jnp.dot(rows, full_dense, preferred_element_type=jnp.float32).astype(low)
    attn_parts = [mix(context_low[:row_count]), mix(context_low[row_count:])]
    ring, attended, attn_parts, slopes, hidden_act = together(
        cot, mlp, after=(ring, attended, attn_parts, slopes, hidden_act)
    )
    query, keys, values, context_low, logsum = attended

    cot.step()
    mlp.step()
    for k in [0, *range(2, ways - 1)]:
        back(k)
    acts = jnp.concatenate(turned(hidden_act), axis=0)
    grad_context, grad_pre, acts, slopes, pre_sums = together(
        cot, mlp, after=(grad_context, grad_pre, acts, slopes, pre_sums)
    )

    while mlp.k < ways:
        mlp.step()
    for k in sorted({1, ways - 1}):
        back(k)
    grad_full = jnp.concatenate(turned([cot.block(k) for k in range(ways)]), axis=0)
    grad_context, grad_pre, pre_sums, attn_parts, grad_full, acts = together(
        mlp, after=(grad_context, grad_pre, pre_sums, attn_parts, grad_full, acts)
    )

    attn = RingScatter(attn_parts, row_count)
    attn.step()
    grads = attention_backward(query, keys, values, turned(grad_context), logsum, tables, 0, half)
    grad_down = contract_rows(acts, grad_full).astype(low)
    normed_low = jnp.concatenate(turned(ring), axis=0)
    pre_full = jnp.concatenate(turned(grad_pre), axis=0)
    grads, grad_context, grad_down, grad_full, context_low, normed_low, pre_full, pre_sums = together(
        attn,
        mlp,
        after=(grads, grad_context, grad_down, grad_full, context_low, normed_low, pre_full, pre_sums),
    )
    part_down = scatter_low(grad_down, "dp", 1)

    while attn.k < ways - 2:
        attn.step()
    if pairs > half:
        grads = attention_backward(
            query, keys, values, turned(grad_context), logsum, tables, half, pairs - half, held=grads
        )
    grad_up = contract_rows(normed_low, pre_full).astype(low)
    grads, grad_up, pre_full, pre_sums, normed_low, grad_full, context_low = together(
        attn, mlp, after=(grads, grad_up, pre_full, pre_sums, normed_low, grad_full, context_low)
    )
    part_up = scatter_low(grad_up, "dp", 0)
    grad_proj, grad_qbias = grads[0], grads[1][:, 0, :]

    def return_normed(low_block, high_block):
        rows = slice(low_block * row_count, high_block * row_count)
        part = contract_cols(pre_full[rows], full_up) + jnp.einsum(
            "cte,cde->td", grad_proj[:, rows], full_qkv, preferred_element_type=jnp.float32
        )
        return part.astype(low)

    attn.step()
    grad_qkv = jnp.einsum(
        "td,cte->cde", normed_low, grad_proj, preferred_element_type=jnp.float32
    ).astype(low)
    grad_parts = [return_normed(0, ways // 2)]
    grad_parts, grad_qkv, pre_full, pre_sums, grad_proj, grad_full, context_low, part_down = together(
        attn,
        mlp,
        after=(grad_parts, grad_qkv, pre_full, pre_sums, grad_proj, grad_full, context_low, part_down),
    )
    part_qkv = scatter_low(grad_qkv, "dp", 1)

    last = RingScatter(grad_parts, row_count)
    last.step()
    grad_dense = contract_rows(context_low, grad_full).astype(low)
    last.parts.append(return_normed(ways // 2, ways))
    grad_dense, pre_sums, part_up = together(last, attn, mlp, after=(grad_dense, pre_sums, part_up))
    part_dense = scatter_low(grad_dense, "dp", 1)
    while last.k < ways - 2:
        last.step()
    attn_mine, mlp_mine = attn.total(), mlp.total()
    grad_ubias = sum(pre_sums)
    attn_mine, mlp_mine, grad_ubias, part_qkv = together(
        last, after=(attn_mine, mlp_mine, grad_ubias, part_qkv)
    )
    last.step()
    output = (resid + attn_mine + mlp_mine + out_bias).astype(low)
    attn_square = jnp.sum(valid_mine * attn_mine * attn_mine)
    mlp_square = jnp.sum(valid_mine * mlp_mine * mlp_mine)
    output, attn_square, mlp_square, part_dense = together(
        last, after=(output, attn_square, mlp_square, part_dense)
    )
    grad_mine = last.total()
    scaled = grad_mine * norm_gain
    grad_tokens = (
        cotangent.astype(jnp.float32)
        + inverse
        * (
            scaled
            - jnp.mean(scaled, axis=-1, keepdims=True)
            - normed * jnp.mean(scaled * normed, axis=-1, keepdims=True)
        )
    ).astype(low)

    totals = jnp.stack(
        [resid_square, attn_square, mlp_square, jnp.sum(valid_mine) * model_width]
    )
    columns = jnp.stack(
        [
            jnp.sum(grad_mine * normed, axis=0),
            jnp.sum(grad_mine, axis=0),
            cot_columns,
        ]
    )
    peers = copies * ways
    share = model_width // peers
    columns = columns.reshape(3, peers, share).transpose(1, 0, 2).reshape(peers, 3 * share)
    own_bias = jnp.concatenate(
        [
            grad_qbias.reshape(3, copies, third).transpose(1, 0, 2).reshape(copies, 3 * third),
            grad_ubias.reshape(copies, -1),
        ],
        axis=1,
    )
    same = (jnp.arange(ways) == me).astype(jnp.float32)[None, :, None]
    own_bias = (own_bias[:, None, :] * same).reshape(peers, -1)
    small = jnp.concatenate(
        [columns, own_bias, jnp.broadcast_to(totals, (peers, 4))], axis=1
    )
    small = jnp.sum(lax.all_to_all(small, ("dp", "tensor"), 0, 0, tiled=True), axis=0)
    part_gain, part_shift, part_obias = small[: 3 * share].reshape(3, share)
    part_qbias = small[3 * share : 3 * share + 3 * third].reshape(3, third)
    part_ubias = small[3 * share + 3 * third : -4]
    root_squares = jnp.sqrt(small[-4:-1] / small[-1])
    return (
        output,
        grad_tokens,
        part_gain,
        part_shift,
        part_qkv,
        part_qbias,
        part_dense,
        part_up,
        part_ubias,
        part_down,
        part_obias,
        root_squares,
    )


def solution(mesh):
    placed = (
        P(("dp", "tensor"), None),
        P("dp", None),
        P(),
        P(),
        P(None, "dp", "tensor"),
        P(None, ("tensor", "dp")),
        P("tensor", "dp"),
        P("dp", "tensor"),
        P(("tensor", "dp")),
        P("tensor", "dp"),
        P(),
        P(("dp", "tensor"), None),
    )
    return jax.shard_map(
        body,
        mesh=mesh,
        in_specs=placed,
        out_specs=(
            P(("dp", "tensor"), None),
            P(("dp", "tensor"), None),
            P(("dp", "tensor")),
            P(("dp", "tensor")),
            P(None, "dp", "tensor"),
            P(None, ("tensor", "dp")),
            P("tensor", "dp"),
            P("dp", "tensor"),
            P(("tensor", "dp")),
            P("tensor", "dp"),
            P(("dp", "tensor")),
            P(),
        ),
        check_vma=False,
    )
```

time: 1310 us -> 769 us (0.59)
  waiting for transfers between devices: 775 us -> 151 us
  other arithmetic: 38.6 us -> 109 us
  blocking collectives: 77.7 us -> 14.8 us
  starting transfers between devices: 1.18 us -> 53.6 us
  matrix products: 251 us -> 288 us
  Pallas kernels: 126 us -> 99.5 us
    reduce_scatter x7 -> x4, waiting for transfers between devices: 517 us -> 77.5 us  [scatter_low(): lax.psum_scatter(part.astype(jnp.bfloat16), axis, scatter_dimension=dim,...]
    all_gather x6 -> x4, waiting for transfers between devices: 254 us -> 0.02 us  [the longest x1 0.02 us: body(): full_qkv = lax.all_gather(qkv_weight, 'dp', axis=1, tiled=True)]
    ppermute x0 -> x21, waiting for transfers between devices: none -> 69.1 us  [shift(): return lax.ppermute(x, 'tensor', pairs)]
    ppermute x0 -> x21, starting transfers between devices: none -> 48.7 us  [shift(): return lax.ppermute(x, 'tensor', pairs)]
    unnamed x2 -> x1, blocking collectives: 58.3 us -> 14.8 us
    convert_element_type x4 -> x11, other arithmetic: 3.78 us -> 37.7 us  [the longest x4 16.4 us: step(): (mine.astype(jnp.float32) + self.up.astype(jnp.float32)).astype(jnp.bfloa...]
    dot_general x5 -> x16, matrix products: 100 us -> 130 us  [the longest x4 43 us: widen(): jnp.dot(ring[k], full_up, preferred_element_type=jnp.float32) + full_ubias]
    pallas_call x2 -> x3, Pallas kernels: 126 us -> 99.5 us  [the longest x2 61.9 us: attention_backward(): pl.pallas_call(kernel, grid_spec=pltpu.PrefetchScalarGridSpec(num_scalar_...]
  transfers between devices with their start and end apart: 14 -> 30, of which waited for: 8 -> 10; matrix products, arithmetic and copies ran while one was open for 22% -> 53% of each run, Pallas kernels for 10% -> 13%
where the time goes in v2:
time: 769 us; the launch traced here: 760 us
  matrix products  288 us (37%)
  waiting for transfers between devices  151 us (20%)
  other arithmetic  109 us (14%)
  Pallas kernels  99.5 us (13%)
  starting transfers between devices  53.6 us (7%)
  local copies, waits for them, and re-layouts  27.5 us (4%)
  between operations  16.5 us (2%)
  blocking collectives  14.8 us (2%)
    dot_general x10, matrix products, contract_cols(): lax.dot_general(left, right, (((1,), (1,)), ((), ())), preferred_element_...  88.6 us
    reduce_scatter x4, waiting for transfers between devices, scatter_low(): lax.psum_scatter(part.astype(jnp.bfloat16), axis, scatter_dimension=dim,...  77.5 us
    ppermute x21, waiting for transfers between devices, shift(): return lax.ppermute(x, 'tensor', pairs)  69.1 us
    pallas_call x2, Pallas kernels, attention_backward(): pl.pallas_call(kernel, grid_spec=pltpu.PrefetchScalarGridSpec(num_scalar_...  61.9 us
    dot_general x3, matrix products, contract_rows(): lax.dot_general(left, right, (((0,), (0,)), ((), ())), preferred_element_...  53.7 us
    ppermute x21, starting transfers between devices, shift(): return lax.ppermute(x, 'tensor', pairs)  48.7 us
    dot_general x4, matrix products, widen(): jnp.dot(ring[k], full_up, preferred_element_type=jnp.float32) + full_ubias  43 us
    pallas_call x1, Pallas kernels, attention_forward(): pl.pallas_call(kernel, grid_spec=pltpu.PrefetchScalarGridSpec(num_scalar_...  37.6 us
  transfers between devices with their start and end apart: 30, of which 10 were waited for; matrix products, arithmetic and copies ran while one was open for 53% of the time, Pallas kernels for 13%

profile of v2, /device:TPU:0, one launch (start us, length us, event | category | flops | bytes accessed | tf_op | source)
XLA Modules:
  0.0 759.7 jit_solution(3045520702015316467)
XLA Ops:
  23.1 14.8 %all-reduce = bf16[3584]{0:T(1024)(128)(2,1)S(1)} all-reduce(bf16[3584]{0:T(1024)(128)(2,1)S(1)} %dynamic-update-slice), channel_id=2, replica_groups=mesh['dp'=8,'tensor'=4] {'dp'}, use_global_device_ids=true, to_apply=%add | all-reduce | flops 3584 | bytes 14336
  56.3 11.3 %collective-permute-done = bf16[512,2048]{1,0:T(8,128)(2,1)} collective-permute-done((bf16[512,2048]{1,0:T(8,128)(2,1)}, bf16[512,2048]{1,0:T(8,128)(2,1)}, u32[]{:S(2)}, u32[]{:S(2)}) %collective-permute-start) | collective-permute-done | bytes 2097184 | tf_op jit(solution)/shard_map/ppermute | solution.py:331
  82.2 34.7 %collective-permute-done.1 = bf16[512,2048]{1,0:T(8,128)(2,1)} collective-permute-done((bf16[512,2048]{1,0:T(8,128)(2,1)}, bf16[512,2048]{1,0:T(8,128)(2,1)}, u32[]{:S(2)}, u32[]{:S(2)}) %collective-permute-start.1) | collective-permute-done | bytes 2097184 | tf_op jit(solution)/shard_map/ppermute | solution.py:331
  139.9 16.4 %multiply_convert_fusion.5 = (bf16[512,2048]{1,0:T(8,128)(2,1)}, f32[512,2048]{1,0:T(8,128)}, f32[512,2048]{1,0:T(8,128)}, bf16[512,2048]{1,0:T(8,128)(2,1)}, f32[512,2048]{1,0:T(8,128)}, /*index=5*/bf16[512,2048]{1,0:T(8,128)(2,1)}) fusion(f32[2048]{0:T(1024)S(1)} %bitcast.125, f32[512,2048]{1,0:T(8,128)} %fusion.93, f32[512,2048]{1,0:T(8,128)S(1)} %fusion.92, ...), kind=kOutput, calls=%fused_computation.98 | convolution fusion | flops 4357881856 | bytes 37756928 | tf_op jit(solution)/shard_map/dot_general | solution.py:486
  169.4 10.9 %multiply_convert_fusion.4 = (bf16[512,2048]{1,0:T(8,128)(2,1)}, f32[512,2048]{1,0:T(8,128)}) fusion(f32[2048]{0:T(1024)S(1)} %bitcast.126, bf16[512,2048]{1,0:T(8,128)(2,1)} %collective-permute-done.2, bf16[2048,2048]{1,0:T(8,128)(2,1)S(1)} %copy-done.45), kind=kOutput, calls=%fused_computation.97 | convolution fusion | flops 4315938816 | bytes 16785408 | tf_op jit(solution)/shard_map/dot_general | solution.py:486
  180.3 10.2 %convolution_convert_fusion.5 = bf16[512,2048]{1,0:T(8,128)(2,1)} fusion(bf16[512,2048]{1,0:T(8,128)(2,1)} %get-tuple-element.292, bf16[2048,2048]{1,0:T(8,128)(2,1)} %all-gather.10.cloned.1.call-done), kind=kOutput, calls=%fused_computation.110 | convolution fusion | flops 4296015872 | bytes 12582912 | tf_op jit(solution)/shard_map/dot_general | solution.py:491
  231.4 37.6 %attend.1 = (bf16[2048,512]{1,0:T(8,128)(2,1)}, bf16[2048,512]{1,0:T(8,128)(2,1)}, bf16[2048,512]{1,0:T(8,128)(2,1)}, bf16[2048,512]{1,0:T(8,128)(2,1)}, f32[4,2,2048]{2,1,0:T(2,128)S(1)}) custom-call(s32[8]{0:T(128)S(1)} %get-tuple-element.255.refs_0_, s32[8]{0:T(128)S(1)} %get-tuple-element.256.refs_1_, f32[3,512,512]{2,1,0:T(8,128)} %fusion.74.refs_2_, ...), custom_call_target="tpu_custom_call" | custom-call | tf_op jit(solution)/shard_map/attend/pallas_call | solution.py:156
  298.5 10.5 %convert_reduce_fusion.5 = (f32[2048]{0:T(1024)}, bf16[512,2048]{1,0:T(8,128)(2,1)}) fusion(f32[512,2048]{1,0:T(8,128)} %get-tuple-element.289, bf16[512,2048]{1,0:T(8,128)(2,1)S(1)} %broadcast_select_fusion.2, bf16[2048,2048]{1,0:T(8,128)(2,1)} %all-gather.10.cloned.1.call-done), kind=kOutput, calls=%fused_computation.93 | convolution fusion | flops 4299159552 | bytes 16785408 | tf_op jit(solution)/shard_map/dot_general | solution.py:325
  317.9 11.7 %convert_reduce_fusion.6 = (f32[2048]{0:T(1024)}, bf16[512,2048]{1,0:T(8,128)(2,1)}) fusion(f32[512,2048]{1,0:T(8,128)} %get-tuple-element.288, bf16[512,2048]{1,0:T(8,128)(2,1)} %param.23, bf16[2048,2048]{1,0:T(8,128)(2,1)} %all-gather.10.cloned.1.call-done), kind=kOutput, calls=%fused_computation.94 | convolution fusion | flops 4299159552 | bytes 16785408 | tf_op jit(solution)/shard_map/dot_general | solution.py:325
  344.0 11.2 %collective-permute-start.13 = (bf16[512,2048]{1,0:T(8,128)(2,1)}, bf16[512,2048]{1,0:T(8,128)(2,1)}, u32[]{:S(2)}, u32[]{:S(2)}) collective-permute-start(bf16[512,2048]{1,0:T(8,128)(2,1)} %add_convert_fusion.5), channel_id=1, source_target_pairs={{0,1},{1,2},{2,3},{4,5},{5,6},{6,7},{8,9},{9,10},{10,11},{12,13},{... | collective-permute-start | bytes 6291464 | tf_op jit(solution)/shard_map/ppermute | solution.py:331
  361.7 14.7 %convert_reduce_fusion.3 = (f32[2048]{0:T(1024)}, bf16[512,2048]{1,0:T(8,128)(2,1)}) fusion(f32[512,2048]{1,0:T(8,128)} %get-tuple-element.308, bf16[512,2048]{1,0:T(8,128)(2,1)} %copy-done.12, bf16[2048,2048]{1,0:T(8,128)(2,1)} %all-gather.10.cloned.1.call-done), kind=kOutput, calls=%fused_computation.87 | convolution fusion | flops 4299159552 | bytes 16785408 | tf_op jit(solution)/shard_map/dot_general | solution.py:325
  382.4 10.0 %convert_reduce_fusion.4 = (f32[2048]{0:T(1024)S(1)}, bf16[512,2048]{1,0:T(8,128)(2,1)}) fusion(f32[512,2048]{1,0:T(8,128)} %get-tuple-element.306, bf16[512,2048]{1,0:T(8,128)(2,1)S(1)} %broadcast_select_fusion.1, bf16[2048,2048]{1,0:T(8,128)(2,1)} %all-gather.10.cloned.1.call-done), kind=kOutput, calls=%fused_computation.88 | convolution fusion | flops 4299159552 | bytes 16785408 | tf_op jit(solution)/shard_map/dot_general | solution.py:325
  399.6 22.1 %convolution_convert_fusion.1 = bf16[2048,2048]{1,0:T(8,128)(2,1)} fusion(bf16[2048,2048]{1,0:T(8,128)(2,1)} %pad_maximum_fusion, bf16[2048,2048]{1,0:T(8,128)(2,1)S(1)} %pad_maximum_fusion.1), kind=kOutput, calls=%fused_computation.17 | convolution fusion | flops 17184063488 | bytes 25165824 | tf_op jit(solution)/shard_map/dot_general | solution.py:319
  425.8 31.1 %attend_back.2 = (bf16[3,2048,512]{2,1,0:T(8,128)(2,1)}, f32[3,1,512]{2,1,0:T(1,128)S(1)}) custom-call(s32[8]{0:T(128)S(1)} %get-tuple-element.255.refs_0_, s32[8]{0:T(128)S(1)} %get-tuple-element.256.refs_1_, bf16[512,512]{1,0:T(8,128)(2,1)S(1)} %copy-done.6, bf16[512,512]{1,0:T(8,128)(2,1)S(1)} %copy-done.2, bf16[512,512]{1,0:T(8,128)(2,1)S(1)} %copy-done.4, ...), custom_call_target="tpu_custom_call" | custom-call | tf_op jit(solution)/shard_map/attend_back/pallas_call | solution.py:278
  467.8 30.8 %attend_back.3 = (bf16[3,2048,512]{2,1,0:T(8,128)(2,1)}, f32[3,1,512]{2,1,0:T(1,128)S(1)}) custom-call(s32[8]{0:T(128)S(1)} %get-tuple-element.255.refs_0_, s32[8]{0:T(128)S(1)} %get-tuple-element.256.refs_1_, bf16[512,512]{1,0:T(8,128)(2,1)S(1)} %copy-done.7, bf16[512,512]{1,0:T(8,128)(2,1)S(1)} %copy-done.3, ...), custom_call_target="tpu_custom_call", output_to_operand_aliasing={{0}: (14, {}), {1}: (15, {})} | custom-call | tf_op jit(solution)/shard_map/attend_back/pallas_call | solution.py:278
  498.6 21.4 %convolution_convert_fusion = bf16[2048,2048]{1,0:T(8,128)(2,1)} fusion(bf16[2048,2048]{1,0:T(8,128)(2,1)S(1)} %bitcast.114, bf16[2048,2048]{1,0:T(8,128)(2,1)} %pad_maximum_fusion.3), kind=kOutput, calls=%fused_computation.16 | convolution fusion | flops 17184063488 | bytes 25165824 | tf_op jit(solution)/shard_map/dot_general | solution.py:319
  524.2 12.7 %fusion.61 = f32[1024,2048,1]{1,0,2:T(8,128)} fusion(bf16[3,2048,512]{2,1,0:T(8,128)(2,1)} %all-gather.6.cloned.1.call-done, bf16[3,2048,512]{2,1,0:T(8,128)(2,1)} %get-tuple-element.382), kind=kOutput, calls=%fused_computation.106 | convolution fusion | flops 6442450944 | bytes 17825792 | tf_op jit(solution)/shard_map/cte,cde->td/dot_general | solution.py:586
  536.9 15.8 %convert_bitcast_fusion = bf16[3,2048,512]{1,2,0:T(8,128)(2,1)} fusion(bf16[3,2048,512]{2,1,0:T(8,128)(2,1)S(1)} %bitcast.118, bf16[2048,2048]{1,0:T(8,128)(2,1)S(1)} %bitcast.116), kind=kOutput, calls=%fused_computation.21 | convolution fusion | flops 12888047616 | bytes 20971520 | tf_op jit(solution)/shard_map/td,cte->cde/dot_general | solution.py:592
  552.8 15.3 %fusion.3 = bf16[1024,2048]{1,0:T(8,128)(2,1)} fusion(f32[1024,2048,1]{1,0,2:T(8,128)} %fusion.61, bf16[2048,2048]{1,0:T(8,128)(2,1)} %all-gather.8.cloned.1.call-done, bf16[2048,2048]{1,0:T(8,128)(2,1)} %pad_maximum_fusion.3), kind=kOutput, calls=%fused_computation.10 | convolution fusion | flops 8594128896 | bytes 25165824 | tf_op jit(solution)/shard_map/dot_general | solution.py:325
  575.6 10.2 %convolution_convert_fusion.3 = bf16[512,2048]{1,0:T(8,128)(2,1)} fusion(bf16[2048,512]{1,0:T(8,128)(2,1)} %get-tuple-element.388, bf16[2048,2048]{1,0:T(8,128)(2,1)} %copy-done.11), kind=kOutput, calls=%fused_computation.108 | convolution fusion | flops 4296015872 | bytes 12582912 | tf_op jit(solution)/shard_map/dot_general | solution.py:319
  585.9 9.9 %fusion.59 = f32[1024,2048,1]{1,0,2:T(8,128)S(1)} fusion(bf16[3,2048,512]{2,1,0:T(8,128)(2,1)} %all-gather.6.cloned.1.call-done, bf16[3,2048,512]{2,1,0:T(8,128)(2,1)} %get-tuple-element.382), kind=kOutput, calls=%fused_computation.104 | convolution fusion | flops 6442450944 | bytes 17825792 | tf_op jit(solution)/shard_map/cte,cde->td/dot_general | solution.py:586
  595.7 14.0 %fusion = bf16[1024,2048]{1,0:T(8,128)(2,1)} fusion(f32[1024,2048,1]{1,0,2:T(8,128)S(1)} %fusion.59, bf16[2048,2048]{1,0:T(8,128)(2,1)} %all-gather.8.cloned.1.call-done, bf16[2048,2048]{1,0:T(8,128)(2,1)} %pad_maximum_fusion.3), kind=kOutput, calls=%fused_computation.6 | convolution fusion | flops 8594128896 | bytes 25165824 | tf_op jit(solution)/shard_map/dot_general | solution.py:325
  631.4 41.5 %reduce-scatter.9.cloned.1.call-done = bf16[3,256,512]{1,2,0:T(8,128)(2,1)} async-done(((bf16[3,2048,512]{1,2,0:T(8,128)(2,1)}), bf16[3,256,512]{1,2,0:T(8,128)(2,1)}) %reduce-scatter.9.cloned.1.call-update) | async-done | bytes 786448 | tf_op jit(solution)/shard_map/reduce_scatter | solution.py:408
  682.6 35.9 %reduce-scatter.11.cloned.1.call-done = bf16[512,256]{1,0:T(8,128)(2,1)} async-done(((bf16[512,2048]{1,0:T(8,128)(2,1)}), bf16[512,256]{1,0:T(8,128)(2,1)}) %reduce-scatter.11.cloned.1.call-update) | async-done | bytes 262160 | tf_op jit(solution)/shard_map/reduce_scatter | solution.py:408
  (294 shorter events, 288.5 us)
Async XLA Ops:
  7.2 60.9 %all-gather.6.cloned.1.call-start = ((), (), s32[]{:S(2)}) async-start(), calls=%async_computation.5 | async-start | bytes 7077888 | tf_op jit(solution)/shard_map/all_gather | solution.py:438
  7.9 116.2 %all-gather.8.cloned.1.call-start = ((), (), s32[]{:S(2)}) async-start(), calls=%async_computation.6 | async-start | bytes 9437184 | tf_op jit(solution)/shard_map/all_gather | solution.py:442
  15.8 164.5 %all-gather.10.cloned.1.call-start = ((), (), s32[]{:S(2)}) async-start(), calls=%async_computation.7 | async-start | bytes 9437184 | tf_op jit(solution)/shard_map/all_gather | solution.py:443
  16.5 210.3 %all-gather.12.cloned.1.call-start = ((), (), s32[]{:S(2)}) async-start(), calls=%async_computation.8 | async-start | bytes 2359296 | tf_op jit(solution)/shard_map/all_gather | solution.py:444
  16.5 51.0 %collective-permute-start = (bf16[512,2048]{1,0:T(8,128)(2,1)}, bf16[512,2048]{1,0:T(8,128)(2,1)}, u32[]{:S(2)}, u32[]{:S(2)}) collective-permute-start(bf16[512,2048]{1,0:T(8,128)(2,1)} %fusion.13), channel_id=1, source_target_pairs={{0,1},{1,2},{2,3},{3,0},{4,5},{5,6},{6,7},{7,4},{8,9},{9,10},{10,1... | collective-permute-start | bytes 6291464 | tf_op jit(solution)/shard_map/ppermute | solution.py:331
  67.9 49.0 %collective-permute-start.1 = (bf16[512,2048]{1,0:T(8,128)(2,1)}, bf16[512,2048]{1,0:T(8,128)(2,1)}, u32[]{:S(2)}, u32[]{:S(2)}) collective-permute-start(bf16[512,2048]{1,0:T(8,128)(2,1)} %collective-permute-done), channel_id=1, source_target_pairs={{0,1},{1,2},{2,3},{3,0},{4,5},{5,6},{6,7},{7,4},{8,9},{9,10},{10,1... | collective-permute-start | bytes 6291464 | tf_op jit(solution)/shard_map/ppermute | solution.py:331
  68.0 500.1 %reduce-scatter.5.cloned.1.call-start = ((), (), s32[]{:S(2)}) async-start(), calls=%async_computation.9 | async-start | bytes 9437184 | tf_op jit(solution)/shard_map/reduce_scatter | solution.py:408
  116.9 48.5 %collective-permute-start.2 = (bf16[512,2048]{1,0:T(8,128)(2,1)}, bf16[512,2048]{1,0:T(8,128)(2,1)}, u32[]{:S(2)}, u32[]{:S(2)}) collective-permute-start(bf16[512,2048]{1,0:T(8,128)(2,1)} %collective-permute-done.1), channel_id=1, source_target_pairs={{0,1},{1,2},{2,3},{3,0},{4,5},{5,6},{6,7},{7,4},{8,9},{9,10},{10,1... | collective-permute-start | bytes 6291464 | tf_op jit(solution)/shard_map/ppermute | solution.py:331
  165.4 49.5 %collective-permute-start.3 = (bf16[512,2048]{1,0:T(8,128)(2,1)}, bf16[512,2048]{1,0:T(8,128)(2,1)}, u32[]{:S(2)}, u32[]{:S(2)}) collective-permute-start(bf16[512,2048]{1,0:T(8,128)(2,1)} %param.23), channel_id=1, source_target_pairs={{0,1},{1,2},{2,3},{4,5},{5,6},{6,7},{8,9},{9,10},{10,11},{12,13},{... | collective-permute-start | bytes 6291464 | tf_op jit(solution)/shard_map/ppermute | solution.py:331
  215.2 63.1 %collective-permute-start.5 = (bf16[512,2048]{1,0:T(8,128)(2,1)}, bf16[512,2048]{1,0:T(8,128)(2,1)}, u32[]{:S(2)}, u32[]{:S(2)}) collective-permute-start(bf16[512,2048]{1,0:T(8,128)(2,1)} %collective-permute-done.3), channel_id=1, source_target_pairs={{1,2},{2,3},{5,6},{6,7},{9,10},{10,11},{13,14},{14,15},{17,18},{18... | collective-permute-start | bytes 6291464 | tf_op jit(solution)/shard_map/ppermute | solution.py:331
  217.1 61.1 %collective-permute-start.6 = (bf16[512,2048]{1,0:T(8,128)(2,1)}, bf16[512,2048]{1,0:T(8,128)(2,1)}, u32[]{:S(2)}, u32[]{:S(2)}) collective-permute-start(bf16[512,2048]{1,0:T(8,128)(2,1)} %collective-permute-done.4), channel_id=1, source_target_pairs={{1,0},{2,1},{5,4},{6,5},{9,8},{10,9},{13,12},{14,13},{17,16},{18,1... | collective-permute-start | bytes 6291464 | tf_op jit(solution)/shard_map/ppermute | solution.py:331
  218.4 59.8 %collective-permute-start.7 = (bf16[512,2048]{1,0:T(8,128)(2,1)}, bf16[512,2048]{1,0:T(8,128)(2,1)}, u32[]{:S(2)}, u32[]{:S(2)}) collective-permute-start(bf16[512,2048]{1,0:T(8,128)(2,1)} %convolution_convert_fusion.7), channel_id=1, source_target_pairs={{0,1},{4,5},{8,9},{12,13},{16,17},{20,21},{24,25},{28,29}} | collective-permute-start | bytes 6291464 | tf_op jit(solution)/shard_map/ppermute | solution.py:331
  224.8 53.4 %collective-permute-start.8 = (bf16[512,2048]{1,0:T(8,128)(2,1)}, bf16[512,2048]{1,0:T(8,128)(2,1)}, u32[]{:S(2)}, u32[]{:S(2)}) collective-permute-start(bf16[512,2048]{1,0:T(8,128)(2,1)} %convolution_convert_fusion.5), channel_id=1, source_target_pairs={{3,2},{7,6},{11,10},{15,14},{19,18},{23,22},{27,26},{31,30}} | collective-permute-start | bytes 6291464 | tf_op jit(solution)/shard_map/ppermute | solution.py:331
  278.2 57.1 %collective-permute-start.10 = (bf16[512,2048]{1,0:T(8,128)(2,1)}, bf16[512,2048]{1,0:T(8,128)(2,1)S(1)}, u32[]{:S(2)}, u32[]{:S(2)}) collective-permute-start(bf16[512,2048]{1,0:T(8,128)(2,1)} %collective-permute-done.6), channel_id=1, source_target_pairs={{1,0},{5,4},{9,8},{13,12},{17,16},{21,20},{25,24},{29,28}} | collective-permute-start | bytes 6291464 | tf_op jit(solution)/shard_map/ppermute | solution.py:331
  280.1 55.2 %collective-permute-start.9 = (bf16[512,2048]{1,0:T(8,128)(2,1)}, bf16[512,2048]{1,0:T(8,128)(2,1)S(1)}, u32[]{:S(2)}, u32[]{:S(2)}) collective-permute-start(bf16[512,2048]{1,0:T(8,128)(2,1)} %collective-permute-done.5), channel_id=1, source_target_pairs={{2,3},{6,7},{10,11},{14,15},{18,19},{22,23},{26,27},{30,31}} | collective-permute-start | bytes 6291464 | tf_op jit(solution)/shard_map/ppermute | solution.py:331
  339.1 53.3 %collective-permute-start.14 = (bf16[512,2048]{1,0:T(8,128)(2,1)}, bf16[512,2048]{1,0:T(8,128)(2,1)}, u32[]{:S(2)}, u32[]{:S(2)}) collective-permute-start(bf16[512,2048]{1,0:T(8,128)(2,1)} %add_convert_fusion.4), channel_id=1, source_target_pairs={{1,0},{2,1},{3,2},{5,4},{6,5},{7,6},{9,8},{10,9},{11,10},{13,12},{... | collective-permute-start | bytes 6291464 | tf_op jit(solution)/shard_map/ppermute | solution.py:331
  344.0 53.0 %collective-permute-start.13 = (bf16[512,2048]{1,0:T(8,128)(2,1)}, bf16[512,2048]{1,0:T(8,128)(2,1)}, u32[]{:S(2)}, u32[]{:S(2)}) collective-permute-start(bf16[512,2048]{1,0:T(8,128)(2,1)} %add_convert_fusion.5), channel_id=1, source_target_pairs={{0,1},{1,2},{2,3},{4,5},{5,6},{6,7},{8,9},{9,10},{10,11},{12,13},{... | collective-permute-start | bytes 6291464 | tf_op jit(solution)/shard_map/ppermute | solution.py:331
  397.1 64.0 %collective-permute-start.15 = (bf16[512,2048]{1,0:T(8,128)(2,1)}, bf16[512,2048]{1,0:T(8,128)(2,1)}, u32[]{:S(2)}, u32[]{:S(2)}) collective-permute-start(bf16[512,2048]{1,0:T(8,128)(2,1)} %convolution_convert_fusion.4), channel_id=1, source_target_pairs={{0,1},{1,2},{2,3},{3,0},{4,5},{5,6},{6,7},{7,4},{8,9},{9,10},{10,1... | collective-permute-start | bytes 6291464 | tf_op jit(solution)/shard_map/ppermute | solution.py:331
  461.1 148.7 %reduce-scatter.7.cloned.1.call-start = ((), (), s32[]{:S(2)}) async-start(), calls=%async_computation.10 | async-start | bytes 9437184 | tf_op jit(solution)/shard_map/reduce_scatter | solution.py:408
  465.8 54.2 %collective-permute-start.16 = (bf16[512,2048]{1,0:T(8,128)(2,1)}, bf16[512,2048]{1,0:T(8,128)(2,1)}, u32[]{:S(2)}, u32[]{:S(2)}) collective-permute-start(bf16[512,2048]{1,0:T(8,128)(2,1)} %add_convert_fusion.3), channel_id=1, source_target_pairs={{0,1},{1,2},{2,3},{3,0},{4,5},{5,6},{6,7},{7,4},{8,9},{9,10},{10,1... | collective-permute-start | bytes 6291464 | tf_op jit(solution)/shard_map/ppermute | solution.py:331
  520.0 153.0 %reduce-scatter.9.cloned.1.call-start = ((), (), s32[]{:S(2)}) async-start(), calls=%async_computation.11 | async-start | bytes 7077888 | tf_op jit(solution)/shard_map/reduce_scatter | solution.py:408
  570.8 147.6 %reduce-scatter.11.cloned.1.call-start = ((), (), s32[]{:S(2)}) async-start(), calls=%async_computation.12 | async-start | bytes 2359296 | tf_op jit(solution)/shard_map/reduce_scatter | solution.py:408
  619.9 55.5 %collective-permute-start.19 = (bf16[512,2048]{1,0:T(8,128)(2,1)}, bf16[512,2048]{1,0:T(8,128)(2,1)}, u32[]{:S(2)}, u32[]{:S(2)}) collective-permute-start(bf16[512,2048]{1,0:T(8,128)(2,1)} %add_convert_fusion.1), channel_id=1, source_target_pairs={{0,1},{1,2},{2,3},{3,0},{4,5},{5,6},{6,7},{7,4},{8,9},{9,10},{10,1... | collective-permute-start | bytes 6291464 | tf_op jit(solution)/shard_map/ppermute | solution.py:331
  680.0 49.6 %collective-permute-start.20 = (bf16[512,2048]{1,0:T(8,128)(2,1)}, bf16[512,2048]{1,0:T(8,128)(2,1)}, u32[]{:S(2)}, u32[]{:S(2)}) collective-permute-start(bf16[512,2048]{1,0:T(8,128)(2,1)} %add_convert_fusion), channel_id=1, source_target_pairs={{0,1},{1,2},{2,3},{3,0},{4,5},{5,6},{6,7},{7,4},{8,9},{9,10},{10,1... | collective-permute-start | bytes 6291464 | tf_op jit(solution)/shard_map/ppermute | solution.py:331
  (68 other events, 1106.9 us)
Sparse Core Ops, SparseCore 0:
  9.9 48.4 all-gather.5
  60.3 54.3 all-gather.7
  116.6 55.9 all-gather.9
  174.3 28.1 all-gather.11
  461.2 71.5 reduce-scatter.4
  536.5 71.2 reduce-scatter.6
  611.2 61.7 reduce-scatter.8
  677.2 41.2 reduce-scatter.10

commit v3 on v2

--- a/solution.py
+++ b/solution.py
@@ -87,11 +87,12 @@
         here = pl.ds(i * BLOCK, BLOCK)
         part = parts[slot]
         cw, sw = cos_ref[rows, :], sin_ref[rows, :]
-        q = turn(part[0, here, :] + bias_ref[0], cw, sw).astype(jnp.bfloat16)
+        x = part[here, :] + bias_ref[...]
+        q = turn(x[:, :PAIR], cw, sw).astype(jnp.bfloat16)
         q_ref[rows, :] = q * jnp.bfloat16(scale)
-        k = turn(part[1, here, :] + bias_ref[1], cw, sw).astype(jnp.bfloat16)
+        k = turn(x[:, PAIR : 2 * PAIR], cw, sw).astype(jnp.bfloat16)
         k_ref[rows, :] = k
-        v = (part[2, here, :] + bias_ref[2]).astype(jnp.bfloat16)
+        v = x[:, 2 * PAIR :].astype(jnp.bfloat16)
         v_ref[rows, :] = v
         km[0, rows, :], km[1, rows, :] = halves(k)
         vm[0, rows, :], vm[1, rows, :] = halves(v)
@@ -138,12 +139,12 @@
 
 def attention_forward(projected, bias, tables, first, count, held=None):
     cos_wide, sin_wide, starts, valid_wide, lows, places = tables
-    width = projected[0].shape[2]
+    width = projected[0].shape[1] // 3
     length = starts.shape[0]
     blocks = length // BLOCK
     ways = len(projected)
     start_wide = jnp.broadcast_to(starts[:, None], (length, PAIR))
-    part = pl.BlockSpec((3, length // ways, PAIR), lambda p, low, place: (0, 0, p + first))
+    part = pl.BlockSpec((length // ways, 3 * PAIR), lambda p, low, place: (0, p + first))
     table = pl.BlockSpec((length, PAIR), lambda p, low, place: (0, 0))
     flat = pl.BlockSpec((length, PAIR), lambda p, low, place: (0, p + first))
     flat_shape = jax.ShapeDtypeStruct((length, width), jnp.bfloat16)
@@ -160,7 +161,7 @@
             grid=(count,),
             in_specs=[
                 *[part] * ways,
-                pl.BlockSpec((3, 1, PAIR), lambda p, low, place: (0, 0, p + first)),
+                pl.BlockSpec((1, 3 * PAIR), lambda p, low, place: (0, p + first)),
                 table, table, table, table,
             ] + [pl.BlockSpec(memory_space=pl.ANY)] * len(held),
             out_specs=[flat, flat, flat, flat,
@@ -175,7 +176,7 @@
         input_output_aliases={7 + ways + i: i for i in range(len(held))},
         compiler_params=pltpu.CompilerParams(vmem_limit_bytes=48 * 2**20),
         name="attend",
-    )(lows, places, *projected, bias[:, None, :], cos_wide, sin_wide,
+    )(lows, places, *projected, bias[None, :], cos_wide, sin_wide,
       start_wide, valid_wide, *held)
 
 
@@ -234,7 +235,7 @@
         dv_acc[cols, :] = dv
         dq = turn(dq * scale, cos_ref[rows, :], -sin_ref[rows, :]).astype(jnp.bfloat16)
         there = pl.ds(pl.multiple_of(place_ref[i] * BLOCK, BLOCK), BLOCK)
-        grad_ref[0, there, :] = dq
+        grad_ref[there, :PAIR] = dq
         sums_ref[0] += jnp.sum(dq.astype(jnp.float32), axis=0, keepdims=True)
 
     none = jnp.zeros((1, PAIR), jnp.float32)
@@ -252,8 +253,8 @@
         dk = turn(dk_acc[rows, :], cos_ref[rows, :], -sin_ref[rows, :]).astype(jnp.bfloat16)
         dv = dv_acc[rows, :].astype(jnp.bfloat16)
         there = pl.ds(pl.multiple_of(place_ref[i] * BLOCK, BLOCK), BLOCK)
-        grad_ref[1, there, :] = dk
-        grad_ref[2, there, :] = dv
+        grad_ref[there, PAIR : 2 * PAIR] = dk
+        grad_ref[there, 2 * PAIR :] = dv
         return (
             totals[0] + jnp.sum(dk.astype(jnp.float32), axis=0, keepdims=True),
             totals[1] + jnp.sum(dv.astype(jnp.float32), axis=0, keepdims=True),
@@ -289,7 +290,7 @@
                 table,
             ] + [pl.BlockSpec(memory_space=pl.ANY)] * len(held),
             out_specs=[
-                pl.BlockSpec((3, length, PAIR), lambda p, low, place: (0, 0, p + first)),
+                pl.BlockSpec((length, 3 * PAIR), lambda p, low, place: (0, p + first)),
                 pl.BlockSpec((3, 1, PAIR), lambda p, low, place: (0, 0, p + first)),
             ],
             scratch_shapes=[pltpu.VMEM((2, length, PAIR), jnp.bfloat16)] * 4
@@ -297,13 +298,45 @@
             + [pltpu.VMEM((length, PAIR), jnp.float32)] * 2,
         ),
         out_shape=[
-            jax.ShapeDtypeStruct((3, length, width), jnp.bfloat16),
+            jax.ShapeDtypeStruct((length, 3 * width), jnp.bfloat16),
             jax.ShapeDtypeStruct((3, 1, width), jnp.float32),
         ],
         input_output_aliases={10 + ways + i: i for i in range(len(held))},
         compiler_params=pltpu.CompilerParams(vmem_limit_bytes=48 * 2**20),
         name="attend_back",
     )(lows, places, *do, q, k, v, lse, cos_wide, sin_wide, starts[None, :], valid_wide, *held)
+
+
+def hidden_back_kernel(block_ref, weight_ref, slope_ref, *refs):
+    grad = nt(block_ref[...], weight_ref[...])
+    refs[-1][...] = (grad * slope_ref[...]).astype(jnp.bfloat16)
+
+
+def hidden_back(block, weight, slope, place, ways, held=None):
+    rows, model_width = block.shape
+    hidden = weight.shape[0]
+    tile = min(512, hidden)
+    held = () if held is None else (held,)
+    return pl.pallas_call(
+        hidden_back_kernel,
+        grid=(hidden // tile,),
+        in_specs=[
+            pl.BlockSpec((rows, model_width), lambda j: (0, 0)),
+            pl.BlockSpec((tile, model_width), lambda j: (j, 0)),
+            pl.BlockSpec((rows, tile), lambda j: (0, j)),
+        ]
+        + [pl.BlockSpec(memory_space=pl.ANY)] * len(held),
+        out_specs=pl.BlockSpec((rows, tile), lambda j: (place, j)),
+        out_shape=jax.ShapeDtypeStruct((ways * rows, hidden), jnp.bfloat16),
+        input_output_aliases={3: 0} if held else {},
+        compiler_params=pltpu.CompilerParams(vmem_limit_bytes=40 * 2**20),
+        cost_estimate=pl.CostEstimate(
+            flops=2 * rows * model_width * hidden,
+            bytes_accessed=2 * hidden * model_width,
+            transcendentals=0,
+        ),
+        name="hidden_back",
+    )(block, weight, slope, *held)
 
 
 def gelu_and_slope(u):
@@ -449,7 +482,7 @@
     biases = lax.all_gather(biases, "dp", axis=0).astype(jnp.float32)
     third = qkv_bias.shape[1]
     full_qbias = biases[:, : 3 * third].reshape(copies, 3, third)
-    full_qbias = full_qbias.transpose(1, 0, 2).reshape(3, copies * third)
+    full_qbias = full_qbias.transpose(1, 0, 2).reshape(3, -1, PAIR).transpose(1, 0, 2).reshape(-1)
     full_ubias = biases[:, 3 * third :].reshape(-1)
 
     starts = segment_starts(segments)[0]
@@ -469,18 +502,18 @@
     ring[1], cot_mine, tables, full_qbias, full_ubias, cot_columns, resid_square = fixed(
         (ring[1], cotangent, tables, full_qbias, full_ubias, cot_columns, resid_square)
     )
-    pairs = full_qkv.shape[2] // PAIR
+    pairs = qkv_weight.shape[2] // PAIR
+    sorted_qkv = full_qkv.reshape(3, model_width, pairs, PAIR).transpose(1, 2, 0, 3)
+    sorted_qkv = sorted_qkv.reshape(model_width, 3 * pairs * PAIR)
     half = max(1, pairs // 2)
     projected, slopes, hidden_act, mlp_parts = ([None] * ways for _ in range(4))
-    grad_context, grad_pre, pre_sums = ([None] * ways for _ in range(3))
+    grad_context, grad_pre = [None] * ways, [None]
 
     def turned(blocks):
         return [*blocks[1:], blocks[0]]
 
     def project(k):
-        projected[k] = jnp.einsum(
-            "td,cde->cte", ring[k], full_qkv, preferred_element_type=jnp.float32
-        )
+        projected[k] = jnp.dot(ring[k], sorted_qkv, preferred_element_type=jnp.float32)
 
     def widen(k):
         pre = jnp.dot(ring[k], full_up, preferred_element_type=jnp.float32) + full_ubias
@@ -495,9 +528,9 @@
     def back(k):
         block = cot.block(k)
         grad_context[k] = contract_cols(block, full_dense).astype(low)
-        grad_act = contract_cols(block, full_down)
-        grad_pre[k] = (grad_act * slopes[k]).astype(low)
-        pre_sums[k] = jnp.sum(grad_pre[k], axis=0, dtype=jnp.float32)
+        grad_pre[0] = hidden_back(
+            block, full_down, slopes[k], (k - 1) % ways, ways, held=grad_pre[0]
+        )
 
     for k in range(2, ways):
         coming = shift(ring[k - 1], around)
@@ -529,11 +562,8 @@
         cot.step()
         mlp.step()
     attended = attention_forward(turned(projected), full_qbias, tables, 0, pairs)
-    query, keys, values, context_low, logsum = attended
-    mix = lambda rows: jnp.dot(rows, full_dense, preferred_element_type=jnp.float32).astype(low)
-    attn_parts = [mix(context_low[:row_count]), mix(context_low[row_count:])]
-    ring, attended, attn_parts, slopes, hidden_act = together(
-        cot, mlp, after=(ring, attended, attn_parts, slopes, hidden_act)
+    ring, attended, slopes, hidden_act, sorted_qkv = together(
+        cot, mlp, after=(ring, attended, slopes, hidden_act, sorted_qkv)
     )
     query, keys, values, context_low, logsum = attended
 
@@ -542,8 +572,9 @@
     for k in [0, *range(2, ways - 1)]:
         back(k)
     acts = jnp.concatenate(turned(hidden_act), axis=0)
-    grad_context, grad_pre, acts, slopes, pre_sums = together(
-        cot, mlp, after=(grad_context, grad_pre, acts, slopes, pre_sums)
+    attn_part = jnp.dot(context_low, full_dense, preferred_element_type=jnp.float32).astype(low)
+    grad_context, grad_pre, acts, slopes, attn_part = together(
+        cot, mlp, after=(grad_context, grad_pre, acts, slopes, attn_part)
     )
 
     while mlp.k < ways:
@@ -551,20 +582,20 @@
     for k in sorted({1, ways - 1}):
         back(k)
     grad_full = jnp.concatenate(turned([cot.block(k) for k in range(ways)]), axis=0)
-    grad_context, grad_pre, pre_sums, attn_parts, grad_full, acts = together(
-        mlp, after=(grad_context, grad_pre, pre_sums, attn_parts, grad_full, acts)
-    )
-
-    attn = RingScatter(attn_parts, row_count)
+    grad_context, grad_pre, attn_part, grad_full, acts = together(
+        mlp, after=(grad_context, grad_pre, attn_part, grad_full, acts)
+    )
+    [pre_full] = grad_pre
+
+    attn = RingScatter([attn_part], row_count)
     attn.step()
     grads = attention_backward(query, keys, values, turned(grad_context), logsum, tables, 0, half)
     grad_down = contract_rows(acts, grad_full).astype(low)
     normed_low = jnp.concatenate(turned(ring), axis=0)
-    pre_full = jnp.concatenate(turned(grad_pre), axis=0)
-    grads, grad_context, grad_down, grad_full, context_low, normed_low, pre_full, pre_sums = together(
+    grads, grad_context, grad_full, context_low, grad_down, pre_full, normed_low = together(
         attn,
         mlp,
-        after=(grads, grad_context, grad_down, grad_full, context_low, normed_low, pre_full, pre_sums),
+        after=(grads, grad_context, grad_full, context_low, grad_down, pre_full, normed_low),
     )
     part_down = scatter_low(grad_down, "dp", 1)
 
@@ -575,41 +606,38 @@
             query, keys, values, turned(grad_context), logsum, tables, half, pairs - half, held=grads
         )
     grad_up = contract_rows(normed_low, pre_full).astype(low)
-    grads, grad_up, pre_full, pre_sums, normed_low, grad_full, context_low = together(
-        attn, mlp, after=(grads, grad_up, pre_full, pre_sums, normed_low, grad_full, context_low)
+    grads, grad_up, pre_full, normed_low, grad_full, context_low = together(
+        attn, mlp, after=(grads, grad_up, pre_full, normed_low, grad_full, context_low)
     )
     part_up = scatter_low(grad_up, "dp", 0)
     grad_proj, grad_qbias = grads[0], grads[1][:, 0, :]
 
     def return_normed(low_block, high_block):
         rows = slice(low_block * row_count, high_block * row_count)
-        part = contract_cols(pre_full[rows], full_up) + jnp.einsum(
-            "cte,cde->td", grad_proj[:, rows], full_qkv, preferred_element_type=jnp.float32
-        )
+        part = contract_cols(pre_full[rows], full_up) + contract_cols(grad_proj[rows], sorted_qkv)
         return part.astype(low)
 
     attn.step()
-    grad_qkv = jnp.einsum(
-        "td,cte->cde", normed_low, grad_proj, preferred_element_type=jnp.float32
-    ).astype(low)
+    grad_qkv = contract_rows(normed_low, grad_proj).astype(low)
     grad_parts = [return_normed(0, ways // 2)]
-    grad_parts, grad_qkv, pre_full, pre_sums, grad_proj, grad_full, context_low, part_down = together(
+    grad_parts, grad_qkv, pre_full, grad_proj, grad_full, context_low, part_down = together(
         attn,
         mlp,
-        after=(grad_parts, grad_qkv, pre_full, pre_sums, grad_proj, grad_full, context_low, part_down),
-    )
-    part_qkv = scatter_low(grad_qkv, "dp", 1)
+        after=(grad_parts, grad_qkv, pre_full, grad_proj, grad_full, context_low, part_down),
+    )
+    part_qkv = scatter_low(grad_qkv, "dp", 0).reshape(-1, pairs, 3, PAIR)
+    part_qkv = part_qkv.transpose(2, 0, 1, 3).reshape(3, -1, pairs * PAIR)
 
     last = RingScatter(grad_parts, row_count)
     last.step()
+    last.parts.append(return_normed(ways // 2, ways))
     grad_dense = contract_rows(context_low, grad_full).astype(low)
-    last.parts.append(return_normed(ways // 2, ways))
-    grad_dense, pre_sums, part_up = together(last, attn, mlp, after=(grad_dense, pre_sums, part_up))
+    grad_dense, pre_full, part_up = together(last, attn, mlp, after=(grad_dense, pre_full, part_up))
     part_dense = scatter_low(grad_dense, "dp", 1)
     while last.k < ways - 2:
         last.step()
+    grad_ubias = jnp.sum(pre_full, axis=0, dtype=jnp.float32)
     attn_mine, mlp_mine = attn.total(), mlp.total()
-    grad_ubias = sum(pre_sums)
     attn_mine, mlp_mine, grad_ubias, part_qkv = together(
         last, after=(attn_mine, mlp_mine, grad_ubias, part_qkv)
     )

time: 769 us -> 757 us (0.984)
  matrix products: 288 us -> 234 us
  Pallas kernels: 99.5 us -> 132 us
  local copies, waits for them, and re-layouts: 27.5 us -> 38.1 us
    dot_general x9 -> x5, matrix products: 75.2 us -> 32.3 us  [the longest x4 25.5 us: project(): jnp.dot(ring[k], sorted_qkv, preferred_element_type=jnp.float32)]
    pallas_call x0 -> x4, Pallas kernels: none -> 33.7 us  [hidden_back(): pl.pallas_call(hidden_back_kernel, grid=(hidden // tile,), in_specs=[pl.B...]
    dot_general x10 -> x8, matrix products: 88.6 us -> 59.4 us  [contract_cols(): lax.dot_general(left, right, (((1,), (1,)), ((), ())), preferred_element_...]
    dot_general x3 -> x4, matrix products: 53.7 us -> 74 us  [contract_rows(): lax.dot_general(left, right, (((0,), (0,)), ((), ())), preferred_element_...]
    ppermute x21, waiting for transfers between devices: 69.1 us -> 81.6 us  [shift(): return lax.ppermute(x, 'tensor', pairs)]
    reduce_scatter x4, waiting for transfers between devices: 77.5 us -> 67.8 us  [scatter_low(): lax.psum_scatter(part.astype(jnp.bfloat16), axis, scatter_dimension=dim,...]
  transfers between devices with their start and end apart: 30 -> 30, of which waited for: 10 -> 12; matrix products, arithmetic and copies ran while one was open for 53% -> 48% of each run, Pallas kernels for 13% -> 18%
where the time goes in v3:
time: 757 us; the launch traced here: 749 us
  matrix products  234 us (31%)
  waiting for transfers between devices  153 us (20%)
  Pallas kernels  132 us (17%)
  other arithmetic  108 us (14%)
  starting transfers between devices  51.7 us (7%)
  local copies, waits for them, and re-layouts  38.1 us (5%)
  between operations  16.6 us (2%)
  blocking collectives  14.6 us (2%)
    ppermute x21, waiting for transfers between devices, shift(): return lax.ppermute(x, 'tensor', pairs)  81.6 us
    dot_general x4, matrix products, contract_rows(): lax.dot_general(left, right, (((0,), (0,)), ((), ())), preferred_element_...  74 us
    reduce_scatter x4, waiting for transfers between devices, scatter_low(): lax.psum_scatter(part.astype(jnp.bfloat16), axis, scatter_dimension=dim,...  67.8 us
    pallas_call x2, Pallas kernels, attention_backward(): pl.pallas_call(kernel, grid_spec=pltpu.PrefetchScalarGridSpec(num_scalar_...  61.1 us
    dot_general x8, matrix products, contract_cols(): lax.dot_general(left, right, (((1,), (1,)), ((), ())), preferred_element_...  59.4 us
    ppermute x21, starting transfers between devices, shift(): return lax.ppermute(x, 'tensor', pairs)  47 us
    dot_general x4, matrix products, widen(): jnp.dot(ring[k], full_up, preferred_element_type=jnp.float32) + full_ubias  40.9 us
    pallas_call x1, Pallas kernels, attention_forward(): pl.pallas_call(kernel, grid_spec=pltpu.PrefetchScalarGridSpec(num_scalar_...  37.1 us
  transfers between devices with their start and end apart: 30, of which 12 were waited for; matrix products, arithmetic and copies ran while one was open for 48% of the time, Pallas kernels for 18%

profile of v3, /device:TPU:0, one launch (start us, length us, event | category | flops | bytes accessed | tf_op | source)
XLA Modules:
  0.0 748.7 jit_solution(12955016375665794853)
XLA Ops:
  24.9 14.6 %all-reduce = bf16[3584]{0:T(1024)(128)(2,1)S(1)} all-reduce(bf16[3584]{0:T(1024)(128)(2,1)S(1)} %dynamic-update-slice), channel_id=2, replica_groups=mesh['dp'=8,'tensor'=4] {'dp'}, use_global_device_ids=true, to_apply=%add | all-reduce | flops 3584 | bytes 14336
  55.3 14.1 %collective-permute-done = bf16[512,2048]{1,0:T(8,128)(2,1)} collective-permute-done((bf16[512,2048]{1,0:T(8,128)(2,1)}, bf16[512,2048]{1,0:T(8,128)(2,1)}, u32[]{:S(2)}, u32[]{:S(2)}) %collective-permute-start) | collective-permute-done | bytes 2097184 | tf_op jit(solution)/shard_map/ppermute | solution.py:364
  86.4 33.2 %collective-permute-done.1 = bf16[512,2048]{1,0:T(8,128)(2,1)} collective-permute-done((bf16[512,2048]{1,0:T(8,128)(2,1)}, bf16[512,2048]{1,0:T(8,128)(2,1)}, u32[]{:S(2)}, u32[]{:S(2)}) %collective-permute-start.1) | collective-permute-done | bytes 2097184 | tf_op jit(solution)/shard_map/ppermute | solution.py:364
  140.8 16.4 %multiply_convert_fusion.1 = (bf16[512,2048]{1,0:T(8,128)(2,1)}, f32[512,2048]{1,0:T(8,128)}, f32[512,2048]{1,0:T(8,128)}, bf16[512,2048]{1,0:T(8,128)(2,1)}, f32[512,2048]{1,0:T(8,128)}, /*index=5*/bf16[512,2048]{1,0:T(8,128)(2,1)}) fusion(f32[2048]{0:T(1024)S(1)} %bitcast.98, f32[512,2048]{1,0:T(8,128)S(1)} %fusion.68, f32[512,2048]{1,0:T(8,128)} %fusion.67, ...), kind=kOutput, calls=%fused_computation.86 | convolution fusion | flops 4357881856 | bytes 37756928 | tf_op jit(solution)/shard_map/dot_general | solution.py:519
  157.2 10.7 %collective-permute-done.2 = bf16[512,2048]{1,0:T(8,128)(2,1)} collective-permute-done((bf16[512,2048]{1,0:T(8,128)(2,1)}, bf16[512,2048]{1,0:T(8,128)(2,1)}, u32[]{:S(2)}, u32[]{:S(2)}) %collective-permute-start.2) | collective-permute-done | bytes 2097184 | tf_op jit(solution)/shard_map/ppermute | solution.py:364
  172.3 10.5 %multiply_convert_fusion = (bf16[512,2048]{1,0:T(8,128)(2,1)}, f32[512,2048]{1,0:T(8,128)}) fusion(f32[2048]{0:T(1024)S(1)} %bitcast.99, bf16[512,2048]{1,0:T(8,128)(2,1)} %collective-permute-done.2, bf16[2048,2048]{1,0:T(8,128)(2,1)S(1)} %copy-done.52), kind=kOutput, calls=%fused_computation.85 | convolution fusion | flops 4315938816 | bytes 16785408 | tf_op jit(solution)/shard_map/dot_general | solution.py:519
  182.8 10.1 %convolution_convert_fusion.8 = bf16[512,2048]{1,0:T(8,128)(2,1)} fusion(bf16[512,2048]{1,0:T(8,128)(2,1)} %get-tuple-element.267, bf16[2048,2048]{1,0:T(8,128)(2,1)} %all-gather.10.cloned.1.call-done.weight_ref), kind=kOutput, calls=%fused_computation.100 | convolution fusion | flops 4296015872 | bytes 12582912 | tf_op jit(solution)/shard_map/dot_general | solution.py:524
  233.2 37.1 %attend.1 = (bf16[2048,512]{1,0:T(8,128)(2,1)}, bf16[2048,512]{1,0:T(8,128)(2,1)}, bf16[2048,512]{1,0:T(8,128)(2,1)}, bf16[2048,512]{1,0:T(8,128)(2,1)}, f32[4,2,2048]{2,1,0:T(2,128)S(1)}) custom-call(s32[8]{0:T(128)S(1)} %get-tuple-element.229.refs_0_, s32[8]{0:T(128)S(1)} %get-tuple-element.230.refs_1_, f32[512,1536]{1,0:T(8,128)} %fusion.65.refs_2_, ...), custom_call_target="tpu_custom_call" | custom-call | tf_op jit(solution)/shard_map/attend/pallas_call | solution.py:157
  291.8 8.4 %hidden_back.4.refs_0_ = bf16[2048,2048]{1,0:T(8,128)(2,1)} custom-call(bf16[512,2048]{1,0:T(8,128)(2,1)S(1)} %copy-done, bf16[2048,2048]{1,0:T(8,128)(2,1)} %all-gather.10.cloned.1.call-done.weight_ref, f32[512,2048]{1,0:T(8,128)S(1)} %copy-done.9), custom_call_target="tpu_custom_call" | custom-call | flops 4294967296 | bytes 8388608 | tf_op jit(solution)/shard_map/hidden_back/pallas_call | solution.py:320
  330.4 10.7 %collective-permute-start.13 = (bf16[512,2048]{1,0:T(8,128)(2,1)}, bf16[512,2048]{1,0:T(8,128)(2,1)}, u32[]{:S(2)}, u32[]{:S(2)}) collective-permute-start(bf16[512,2048]{1,0:T(8,128)(2,1)} %add_convert_fusion.7), channel_id=1, source_target_pairs={{0,1},{1,2},{2,3},{4,5},{5,6},{6,7},{8,9},{9,10},{10,11},{12,13},{... | collective-permute-start | bytes 6291464 | tf_op jit(solution)/shard_map/ppermute | solution.py:364
  359.1 8.4 %hidden_back.7 = bf16[2048,2048]{1,0:T(8,128)(2,1)} custom-call(bf16[512,2048]{1,0:T(8,128)(2,1)S(1)} %broadcast_select_fusion.block_ref, bf16[2048,2048]{1,0:T(8,128)(2,1)} %all-gather.10.cloned.1.call-done.weight_ref, f32[512,2048]{1,0:T(8,128)S(1)} %copy-done.7, bf16[2048,2048]{1,0:T(8,128)(2,1)} %hidden_back.6.refs_0_), custom_call_target="tpu_custom_call", output_to_operand_aliasing={{}: (3, {})} | custom-call | flops 4294967296 | bytes 8388608 | tf_op jit(solution)/shard_map/hidden_back/pallas_call | solution.py:320
  380.5 9.2 %collective-permute-done.14 = bf16[512,2048]{1,0:T(8,128)(2,1)} collective-permute-done((bf16[512,2048]{1,0:T(8,128)(2,1)}, bf16[512,2048]{1,0:T(8,128)(2,1)}, u32[]{:S(2)}, u32[]{:S(2)}) %collective-permute-start.14) | collective-permute-done | bytes 2097184 | tf_op jit(solution)/shard_map/ppermute | solution.py:364
  392.9 30.6 %attend_back.2 = (bf16[2048,1536]{1,0:T(8,128)(2,1)}, f32[3,1,512]{2,1,0:T(1,128)S(1)}) custom-call(s32[8]{0:T(128)S(1)} %get-tuple-element.229.refs_0_, s32[8]{0:T(128)S(1)} %get-tuple-element.230.refs_1_, bf16[512,512]{1,0:T(8,128)(2,1)S(1)} %convolution_convert_fusion.10.refs_2_, bf16[512,512]{1,0:T(8,128)(2,1)S(1)} %convolution_convert_fusion.11.refs_3_, ...), custom_call_target="tpu_custom_call" | custom-call | tf_op jit(solution)/shard_map/attend_back/pallas_call | solution.py:279
  423.5 23.9 %convolution_convert_fusion.1 = bf16[2048,2048]{1,0:T(8,128)(2,1)} fusion(bf16[2048,2048]{1,0:T(8,128)(2,1)} %pad_maximum_fusion, bf16[2048,2048]{1,0:T(8,128)(2,1)} %pad_maximum_fusion.1), kind=kOutput, calls=%fused_computation.13 | convolution fusion | flops 17184063488 | bytes 25165824 | tf_op jit(solution)/shard_map/dot_general | solution.py:352
  453.5 30.4 %attend_back.3 = (bf16[2048,1536]{1,0:T(8,128)(2,1)}, f32[3,1,512]{2,1,0:T(1,128)S(1)}) custom-call(s32[8]{0:T(128)S(1)} %get-tuple-element.229.refs_0_, s32[8]{0:T(128)S(1)} %get-tuple-element.230.refs_1_, bf16[512,512]{1,0:T(8,128)(2,1)S(1)} %copy-done.15, bf16[512,512]{1,0:T(8,128)(2,1)S(1)} %copy-done.13, ...), custom_call_target="tpu_custom_call", output_to_operand_aliasing={{0}: (14, {}), {1}: (15, {})} | custom-call | tf_op jit(solution)/shard_map/attend_back/pallas_call | solution.py:279
  483.9 24.4 %convolution_convert_fusion = bf16[2048,2048]{1,0:T(8,128)(2,1)} fusion(bf16[2048,2048]{1,0:T(8,128)(2,1)} %pad_maximum_fusion.2, bf16[2048,2048]{1,0:T(8,128)(2,1)} %hidden_back.7), kind=kOutput, calls=%fused_computation.12 | convolution fusion | flops 17184063488 | bytes 25165824 | tf_op jit(solution)/shard_map/dot_general | solution.py:352
  511.7 13.4 %fusion.55 = f32[1024,2048]{1,0:T(8,128)} fusion(bf16[2048,1536]{0,1:T(8,128)(2,1)} %bitcast.83, bf16[2048,1536]{1,0:T(8,128)(2,1)} %get-tuple-element.337), kind=kOutput, calls=%fused_computation.94 | convolution fusion | flops 6442450944 | bytes 17825792 | tf_op jit(solution)/shard_map/dot_general | solution.py:358
  525.1 15.7 %convolution_convert_fusion.3 = bf16[2048,1536]{1,0:T(8,128)(2,1)} fusion(bf16[2048,2048]{1,0:T(8,128)(2,1)S(1)} %bitcast.77, bf16[2048,1536]{1,0:T(8,128)(2,1)S(1)} %bitcast.79), kind=kOutput, calls=%fused_computation.15 | convolution fusion | flops 12888047616 | bytes 20971520 | tf_op jit(solution)/shard_map/dot_general | solution.py:352
  540.8 15.4 %add_convert_fusion.1 = bf16[1024,2048]{1,0:T(8,128)(2,1)} fusion(f32[1024,2048]{1,0:T(8,128)} %fusion.55, bf16[2048,2048]{1,0:T(8,128)(2,1)} %all-gather.8.cloned.1.call-done, bf16[2048,2048]{1,0:T(8,128)(2,1)} %hidden_back.7), kind=kOutput, calls=%fused_computation.6 | convolution fusion | flops 8594128896 | bytes 25165824 | tf_op jit(solution)/shard_map/dot_general | solution.py:358
  565.8 10.0 %convolution_convert_fusion.4 = bf16[512,2048]{1,0:T(8,128)(2,1)} fusion(bf16[2048,512]{1,0:T(8,128)(2,1)} %get-tuple-element.343, bf16[2048,2048]{1,0:T(8,128)(2,1)} %pad_maximum_fusion.1), kind=kOutput, calls=%fused_computation.96 | convolution fusion | flops 4296015872 | bytes 12582912 | tf_op jit(solution)/shard_map/dot_general | solution.py:352
  575.8 9.7 %fusion.53 = f32[1024,2048]{1,0:T(8,128)S(1)} fusion(bf16[2048,1536]{0,1:T(8,128)(2,1)} %bitcast.84, bf16[2048,1536]{1,0:T(8,128)(2,1)} %get-tuple-element.337), kind=kOutput, calls=%fused_computation.92 | convolution fusion | flops 6442450944 | bytes 17825792 | tf_op jit(solution)/shard_map/dot_general | solution.py:358
  585.6 14.0 %add_convert_fusion = bf16[1024,2048]{1,0:T(8,128)(2,1)} fusion(f32[1024,2048]{1,0:T(8,128)S(1)} %fusion.53, bf16[2048,2048]{1,0:T(8,128)(2,1)} %all-gather.8.cloned.1.call-done, bf16[2048,2048]{1,0:T(8,128)(2,1)} %hidden_back.7), kind=kOutput, calls=%fused_computation.5 | convolution fusion | flops 8594128896 | bytes 25165824 | tf_op jit(solution)/shard_map/dot_general | solution.py:358
  629.4 32.3 %reduce-scatter.9.cloned.1.call-done = bf16[256,1536]{1,0:T(8,128)(2,1)} async-done(((bf16[2048,1536]{1,0:T(8,128)(2,1)}), bf16[256,1536]{1,0:T(8,128)(2,1)}) %reduce-scatter.9.cloned.1.call-update) | async-done | bytes 786448 | tf_op jit(solution)/shard_map/reduce_scatter | solution.py:441
  671.8 35.4 %reduce-scatter.11.cloned.1.call-done = bf16[512,256]{1,0:T(8,128)(2,1)} async-done(((bf16[512,2048]{1,0:T(8,128)(2,1)}), bf16[512,256]{1,0:T(8,128)(2,1)}) %reduce-scatter.11.cloned.1.call-update) | async-done | bytes 262160 | tf_op jit(solution)/shard_map/reduce_scatter | solution.py:441
  (301 shorter events, 293.4 us)
Async XLA Ops:
  7.2 63.8 %all-gather.6.cloned.1.call-start = ((), (), s32[]{:S(2)}) async-start(), calls=%async_computation.5 | async-start | bytes 7077888 | tf_op jit(solution)/shard_map/all_gather | solution.py:471
  9.7 117.0 %all-gather.8.cloned.1.call-start = ((), (), s32[]{:S(2)}) async-start(), calls=%async_computation.6 | async-start | bytes 9437184 | tf_op jit(solution)/shard_map/all_gather | solution.py:475
  17.5 165.2 %all-gather.10.cloned.1.call-start = ((), (), s32[]{:S(2)}) async-start(), calls=%async_computation.7 | async-start | bytes 9437184 | tf_op jit(solution)/shard_map/all_gather | solution.py:476
  18.3 211.5 %all-gather.12.cloned.1.call-start = ((), (), s32[]{:S(2)}) async-start(), calls=%async_computation.8 | async-start | bytes 2359296 | tf_op jit(solution)/shard_map/all_gather | solution.py:477
  18.3 51.0 %collective-permute-start = (bf16[512,2048]{1,0:T(8,128)(2,1)}, bf16[512,2048]{1,0:T(8,128)(2,1)}, u32[]{:S(2)}, u32[]{:S(2)}) collective-permute-start(bf16[512,2048]{1,0:T(8,128)(2,1)} %fusion.7), channel_id=1, source_target_pairs={{0,1},{1,2},{2,3},{3,0},{4,5},{5,6},{6,7},{7,4},{8,9},{9,10},{10,1... | collective-permute-start | bytes 6291464 | tf_op jit(solution)/shard_map/ppermute | solution.py:364
  70.7 48.9 %collective-permute-start.1 = (bf16[512,2048]{1,0:T(8,128)(2,1)}, bf16[512,2048]{1,0:T(8,128)(2,1)}, u32[]{:S(2)}, u32[]{:S(2)}) collective-permute-start(bf16[512,2048]{1,0:T(8,128)(2,1)} %collective-permute-done), channel_id=1, source_target_pairs={{0,1},{1,2},{2,3},{3,0},{4,5},{5,6},{6,7},{7,4},{8,9},{9,10},{10,1... | collective-permute-start | bytes 6291464 | tf_op jit(solution)/shard_map/ppermute | solution.py:364
  70.7 485.5 %reduce-scatter.5.cloned.1.call-start = ((), (), s32[]{:S(2)}) async-start(), calls=%async_computation.9 | async-start | bytes 9437184 | tf_op jit(solution)/shard_map/reduce_scatter | solution.py:441
  119.6 48.2 %collective-permute-start.2 = (bf16[512,2048]{1,0:T(8,128)(2,1)}, bf16[512,2048]{1,0:T(8,128)(2,1)}, u32[]{:S(2)}, u32[]{:S(2)}) collective-permute-start(bf16[512,2048]{1,0:T(8,128)(2,1)} %collective-permute-done.1), channel_id=1, source_target_pairs={{0,1},{1,2},{2,3},{3,0},{4,5},{5,6},{6,7},{7,4},{8,9},{9,10},{10,1... | collective-permute-start | bytes 6291464 | tf_op jit(solution)/shard_map/ppermute | solution.py:364
  167.8 49.5 %collective-permute-start.3 = (bf16[512,2048]{1,0:T(8,128)(2,1)S(1)}, bf16[512,2048]{1,0:T(8,128)(2,1)}, u32[]{:S(2)}, u32[]{:S(2)}) collective-permute-start(bf16[512,2048]{1,0:T(8,128)(2,1)S(1)} %copy-done), channel_id=1, source_target_pairs={{0,1},{1,2},{2,3},{4,5},{5,6},{6,7},{8,9},{9,10},{10,11},{12,13},{... | collective-permute-start | bytes 6291464 | tf_op jit(solution)/shard_map/ppermute | solution.py:364
  217.5 52.8 %collective-permute-start.5 = (bf16[512,2048]{1,0:T(8,128)(2,1)}, bf16[512,2048]{1,0:T(8,128)(2,1)}, u32[]{:S(2)}, u32[]{:S(2)}) collective-permute-start(bf16[512,2048]{1,0:T(8,128)(2,1)} %collective-permute-done.3), channel_id=1, source_target_pairs={{1,2},{2,3},{5,6},{6,7},{9,10},{10,11},{13,14},{14,15},{17,18},{18... | collective-permute-start | bytes 6291464 | tf_op jit(solution)/shard_map/ppermute | solution.py:364
  219.5 50.8 %collective-permute-start.6 = (bf16[512,2048]{1,0:T(8,128)(2,1)}, bf16[512,2048]{1,0:T(8,128)(2,1)}, u32[]{:S(2)}, u32[]{:S(2)}) collective-permute-start(bf16[512,2048]{1,0:T(8,128)(2,1)} %collective-permute-done.4), channel_id=1, source_target_pairs={{1,0},{2,1},{5,4},{6,5},{9,8},{10,9},{13,12},{14,13},{17,16},{18,1... | collective-permute-start | bytes 6291464 | tf_op jit(solution)/shard_map/ppermute | solution.py:364
  220.8 49.5 %collective-permute-start.7 = (bf16[512,2048]{1,0:T(8,128)(2,1)}, bf16[512,2048]{1,0:T(8,128)(2,1)}, u32[]{:S(2)}, u32[]{:S(2)}) collective-permute-start(bf16[512,2048]{1,0:T(8,128)(2,1)} %convolution_convert_fusion.7), channel_id=1, source_target_pairs={{0,1},{4,5},{8,9},{12,13},{16,17},{20,21},{24,25},{28,29}} | collective-permute-start | bytes 6291464 | tf_op jit(solution)/shard_map/ppermute | solution.py:364
  270.3 53.5 %collective-permute-start.9 = (bf16[512,2048]{1,0:T(8,128)(2,1)}, bf16[512,2048]{1,0:T(8,128)(2,1)S(1)}, u32[]{:S(2)}, u32[]{:S(2)}) collective-permute-start(bf16[512,2048]{1,0:T(8,128)(2,1)} %collective-permute-done.5), channel_id=1, source_target_pairs={{2,3},{6,7},{10,11},{14,15},{18,19},{22,23},{26,27},{30,31}} | collective-permute-start | bytes 6291464 | tf_op jit(solution)/shard_map/ppermute | solution.py:364
  271.1 52.7 %collective-permute-start.10 = (bf16[512,2048]{1,0:T(8,128)(2,1)}, bf16[512,2048]{1,0:T(8,128)(2,1)S(1)}, u32[]{:S(2)}, u32[]{:S(2)}) collective-permute-start(bf16[512,2048]{1,0:T(8,128)(2,1)} %collective-permute-done.6), channel_id=1, source_target_pairs={{1,0},{5,4},{9,8},{13,12},{17,16},{21,20},{25,24},{29,28}} | collective-permute-start | bytes 6291464 | tf_op jit(solution)/shard_map/ppermute | solution.py:364
  278.4 47.6 %collective-permute-start.11 = (bf16[512,2048]{1,0:T(8,128)(2,1)}, bf16[512,2048]{1,0:T(8,128)(2,1)}, u32[]{:S(2)}, u32[]{:S(2)}) collective-permute-start(bf16[512,2048]{1,0:T(8,128)(2,1)} %get-tuple-element.442), channel_id=1, source_target_pairs={{0,1},{1,2},{4,5},{5,6},{8,9},{9,10},{12,13},{13,14},{16,17},{17,1... | collective-permute-start | bytes 6291464 | tf_op jit(solution)/shard_map/ppermute | solution.py:364
  330.4 50.0 %collective-permute-start.13 = (bf16[512,2048]{1,0:T(8,128)(2,1)}, bf16[512,2048]{1,0:T(8,128)(2,1)}, u32[]{:S(2)}, u32[]{:S(2)}) collective-permute-start(bf16[512,2048]{1,0:T(8,128)(2,1)} %add_convert_fusion.7), channel_id=1, source_target_pairs={{0,1},{1,2},{2,3},{4,5},{5,6},{6,7},{8,9},{9,10},{10,11},{12,13},{... | collective-permute-start | bytes 6291464 | tf_op jit(solution)/shard_map/ppermute | solution.py:364
  392.8 54.5 %collective-permute-start.15 = (bf16[512,2048]{1,0:T(8,128)(2,1)}, bf16[512,2048]{1,0:T(8,128)(2,1)S(1)}, u32[]{:S(2)}, u32[]{:S(2)}) collective-permute-start(bf16[512,2048]{1,0:T(8,128)(2,1)} %slice.67), channel_id=1, source_target_pairs={{0,1},{1,2},{2,3},{3,0},{4,5},{5,6},{6,7},{7,4},{8,9},{9,10},{10,1... | collective-permute-start | bytes 6291464 | tf_op jit(solution)/shard_map/ppermute | solution.py:364
  448.7 150.9 %reduce-scatter.7.cloned.1.call-start = ((), (), s32[]{:S(2)}) async-start(), calls=%async_computation.10 | async-start | bytes 9437184 | tf_op jit(solution)/shard_map/reduce_scatter | solution.py:441
  453.4 54.9 %collective-permute-start.16 = (bf16[512,2048]{1,0:T(8,128)(2,1)}, bf16[512,2048]{1,0:T(8,128)(2,1)}, u32[]{:S(2)}, u32[]{:S(2)}) collective-permute-start(bf16[512,2048]{1,0:T(8,128)(2,1)} %add_convert_fusion.5), channel_id=1, source_target_pairs={{0,1},{1,2},{2,3},{3,0},{4,5},{5,6},{6,7},{7,4},{8,9},{9,10},{10,1... | collective-permute-start | bytes 6291464 | tf_op jit(solution)/shard_map/ppermute | solution.py:364
  508.4 153.4 %reduce-scatter.9.cloned.1.call-start = ((), (), s32[]{:S(2)}) async-start(), calls=%async_computation.11 | async-start | bytes 7077888 | tf_op jit(solution)/shard_map/reduce_scatter | solution.py:441
  511.6 47.4 %collective-permute-start.17 = (bf16[512,2048]{1,0:T(8,128)(2,1)S(1)}, bf16[512,2048]{1,0:T(8,128)(2,1)}, u32[]{:S(2)}, u32[]{:S(2)}) collective-permute-start(bf16[512,2048]{1,0:T(8,128)(2,1)S(1)} %add_convert_fusion.4), channel_id=1, source_target_pairs={{0,1},{1,2},{2,3},{3,0},{4,5},{5,6},{6,7},{7,4},{8,9},{9,10},{10,1... | collective-permute-start | bytes 6291464 | tf_op jit(solution)/shard_map/ppermute | solution.py:364
  559.1 148.1 %reduce-scatter.11.cloned.1.call-start = ((), (), s32[]{:S(2)}) async-start(), calls=%async_computation.12 | async-start | bytes 2359296 | tf_op jit(solution)/shard_map/reduce_scatter | solution.py:441
  612.0 52.6 %collective-permute-start.19 = (bf16[512,2048]{1,0:T(8,128)(2,1)}, bf16[512,2048]{1,0:T(8,128)(2,1)}, u32[]{:S(2)}, u32[]{:S(2)}) collective-permute-start(bf16[512,2048]{1,0:T(8,128)(2,1)} %add_convert_fusion.3), channel_id=1, source_target_pairs={{0,1},{1,2},{2,3},{3,0},{4,5},{5,6},{6,7},{7,4},{8,9},{9,10},{10,1... | collective-permute-start | bytes 6291464 | tf_op jit(solution)/shard_map/ppermute | solution.py:364
  669.2 49.5 %collective-permute-start.20 = (bf16[512,2048]{1,0:T(8,128)(2,1)}, bf16[512,2048]{1,0:T(8,128)(2,1)}, u32[]{:S(2)}, u32[]{:S(2)}) collective-permute-start(bf16[512,2048]{1,0:T(8,128)(2,1)} %add_convert_fusion.2), channel_id=1, source_target_pairs={{0,1},{1,2},{2,3},{3,0},{4,5},{5,6},{6,7},{7,4},{8,9},{9,10},{10,1... | collective-permute-start | bytes 6291464 | tf_op jit(solution)/shard_map/ppermute | solution.py:364
  (70 other events, 1193.7 us)
Sparse Core Ops, SparseCore 0:
  10.5 49.5 all-gather.5
  62.0 54.3 all-gather.7
  118.3 55.9 all-gather.9
  176.0 28.1 all-gather.11
  448.8 72.6 reduce-scatter.4
  525.3 71.2 reduce-scatter.6
  600.0 61.7 reduce-scatter.8
  666.0 41.2 reduce-scatter.10

commit v4 on v3

--- a/solution.py
+++ b/solution.py
@@ -525,9 +525,10 @@
             hidden_act[k], full_down, preferred_element_type=jnp.float32
         ).astype(low)
 
-    def back(k):
-        block = cot.block(k)
+    def context_back(k, block):
         grad_context[k] = contract_cols(block, full_dense).astype(low)
+
+    def inner_back(k, block):
         grad_pre[0] = hidden_back(
             block, full_down, slopes[k], (k - 1) % ways, ways, held=grad_pre[0]
         )
@@ -570,7 +571,8 @@
     cot.step()
     mlp.step()
     for k in [0, *range(2, ways - 1)]:
-        back(k)
+        context_back(k, cot.block(k))
+        inner_back(k, cot.block(k))
     acts = jnp.concatenate(turned(hidden_act), axis=0)
     attn_part = jnp.dot(context_low, full_dense, preferred_element_type=jnp.float32).astype(low)
     grad_context, grad_pre, acts, slopes, attn_part = together(
@@ -579,25 +581,27 @@
 
     while mlp.k < ways:
         mlp.step()
-    for k in sorted({1, ways - 1}):
-        back(k)
-    grad_full = jnp.concatenate(turned([cot.block(k) for k in range(ways)]), axis=0)
-    grad_context, grad_pre, attn_part, grad_full, acts = together(
-        mlp, after=(grad_context, grad_pre, attn_part, grad_full, acts)
-    )
-    [pre_full] = grad_pre
+    blocks = [cot.block(k) for k in range(ways)]
+    late = sorted({1, ways - 1})
+    for k in late:
+        context_back(k, blocks[k])
+    grad_full = jnp.concatenate(turned(blocks), axis=0)
+    grad_down = contract_rows(acts, grad_full).astype(low)
+    grad_context, attn_part, grad_full, grad_down, blocks, grad_pre, slopes = together(
+        mlp, after=(grad_context, attn_part, grad_full, grad_down, blocks, grad_pre, slopes)
+    )
+    part_down = scatter_low(grad_down, "dp", 1)
 
     attn = RingScatter([attn_part], row_count)
     attn.step()
     grads = attention_backward(query, keys, values, turned(grad_context), logsum, tables, 0, half)
-    grad_down = contract_rows(acts, grad_full).astype(low)
+    for k in late:
+        inner_back(k, blocks[k])
     normed_low = jnp.concatenate(turned(ring), axis=0)
-    grads, grad_context, grad_full, context_low, grad_down, pre_full, normed_low = together(
-        attn,
-        mlp,
-        after=(grads, grad_context, grad_full, context_low, grad_down, pre_full, normed_low),
-    )
-    part_down = scatter_low(grad_down, "dp", 1)
+    [pre_full] = grad_pre
+    grads, grad_context, grad_full, context_low, pre_full, normed_low = together(
+        attn, mlp, after=(grads, grad_context, grad_full, context_low, pre_full, normed_low)
+    )
 
     while attn.k < ways - 2:
         attn.step()
@@ -606,8 +610,8 @@
             query, keys, values, turned(grad_context), logsum, tables, half, pairs - half, held=grads
         )
     grad_up = contract_rows(normed_low, pre_full).astype(low)
-    grads, grad_up, pre_full, normed_low, grad_full, context_low = together(
-        attn, mlp, after=(grads, grad_up, pre_full, normed_low, grad_full, context_low)
+    grads, grad_up, pre_full, normed_low, grad_full, context_low, part_down = together(
+        attn, mlp, after=(grads, grad_up, pre_full, normed_low, grad_full, context_low, part_down)
     )
     part_up = scatter_low(grad_up, "dp", 0)
     grad_proj, grad_qbias = grads[0], grads[1][:, 0, :]
@@ -620,10 +624,8 @@
     attn.step()
     grad_qkv = contract_rows(normed_low, grad_proj).astype(low)
     grad_parts = [return_normed(0, ways // 2)]
-    grad_parts, grad_qkv, pre_full, grad_proj, grad_full, context_low, part_down = together(
-        attn,
-        mlp,
-        after=(grad_parts, grad_qkv, pre_full, grad_proj, grad_full, context_low, part_down),
+    grad_parts, grad_qkv, pre_full, grad_proj, grad_full, context_low = together(
+        attn, mlp, after=(grad_parts, grad_qkv, pre_full, grad_proj, grad_full, context_low)
     )
     part_qkv = scatter_low(grad_qkv, "dp", 0).reshape(-1, pairs, 3, PAIR)
     part_qkv = part_qkv.transpose(2, 0, 1, 3).reshape(3, -1, pairs * PAIR)
@@ -645,9 +647,35 @@
     output = (resid + attn_mine + mlp_mine + out_bias).astype(low)
     attn_square = jnp.sum(valid_mine * attn_mine * attn_mine)
     mlp_square = jnp.sum(valid_mine * mlp_mine * mlp_mine)
-    output, attn_square, mlp_square, part_dense = together(
-        last, after=(output, attn_square, mlp_square, part_dense)
-    )
+    totals = jnp.stack(
+        [resid_square, attn_square, mlp_square, jnp.sum(valid_mine) * model_width]
+    )
+    peers = copies * ways
+    share = model_width // peers
+    own_bias = jnp.concatenate(
+        [
+            grad_qbias.reshape(3, copies, third).transpose(1, 0, 2).reshape(copies, 3 * third),
+            grad_ubias.reshape(copies, -1),
+        ],
+        axis=1,
+    )
+    same = (jnp.arange(ways) == me).astype(jnp.float32)[None, :, None]
+    own_bias = (own_bias[:, None, :] * same).reshape(peers, -1)
+
+    def summed(parts):
+        return jnp.sum(lax.all_to_all(parts, ("dp", "tensor"), 0, 0, tiled=True), axis=0)
+
+    small = summed(
+        jnp.concatenate(
+            [cot_columns.reshape(peers, share), own_bias, jnp.broadcast_to(totals, (peers, 4))],
+            axis=1,
+        )
+    )
+    output, small, part_dense = together(last, after=(output, small, part_dense))
+    part_obias = small[:share]
+    part_qbias = small[share : share + 3 * third].reshape(3, third)
+    part_ubias = small[share + 3 * third : -4]
+    root_squares = jnp.sqrt(small[-4:-1] / small[-1])
     grad_mine = last.total()
     scaled = grad_mine * norm_gain
     grad_tokens = (
@@ -660,36 +688,10 @@
         )
     ).astype(low)
 
-    totals = jnp.stack(
-        [resid_square, attn_square, mlp_square, jnp.sum(valid_mine) * model_width]
-    )
-    columns = jnp.stack(
-        [
-            jnp.sum(grad_mine * normed, axis=0),
-            jnp.sum(grad_mine, axis=0),
-            cot_columns,
-        ]
-    )
-    peers = copies * ways
-    share = model_width // peers
-    columns = columns.reshape(3, peers, share).transpose(1, 0, 2).reshape(peers, 3 * share)
-    own_bias = jnp.concatenate(
-        [
-            grad_qbias.reshape(3, copies, third).transpose(1, 0, 2).reshape(copies, 3 * third),
-            grad_ubias.reshape(copies, -1),
-        ],
-        axis=1,
-    )
-    same = (jnp.arange(ways) == me).astype(jnp.float32)[None, :, None]
-    own_bias = (own_bias[:, None, :] * same).reshape(peers, -1)
-    small = jnp.concatenate(
-        [columns, own_bias, jnp.broadcast_to(totals, (peers, 4))], axis=1
-    )
-    small = jnp.sum(lax.all_to_all(small, ("dp", "tensor"), 0, 0, tiled=True), axis=0)
-    part_gain, part_shift, part_obias = small[: 3 * share].reshape(3, share)
-    part_qbias = small[3 * share : 3 * share + 3 * third].reshape(3, third)
-    part_ubias = small[3 * share + 3 * third : -4]
-    root_squares = jnp.sqrt(small[-4:-1] / small[-1])
+    columns = jnp.stack([jnp.sum(grad_mine * normed, axis=0), jnp.sum(grad_mine, axis=0)])
+    columns = columns.reshape(2, peers, share).transpose(1, 0, 2).reshape(peers, 2 * share)
+    columns = summed(columns)
+    part_gain, part_shift = columns[:share], columns[share:]
     return (
         output,
         grad_tokens,

time: 757 us -> 768 us (1.015)
  starting transfers between devices: 51.7 us -> 64.8 us
    all_to_all x1 -> x2, waiting for transfers between devices: 2.88 us -> 33.1 us  [summed(): lax.all_to_all(parts, ('dp', 'tensor'), 0, 0, tiled=True)]
    reduce_scatter x4, waiting for transfers between devices: 67.8 us -> 39.1 us  [scatter_low(): lax.psum_scatter(part.astype(jnp.bfloat16), axis, scatter_dimension=dim,...]
  transfers between devices with their start and end apart: 30 -> 31, of which waited for: 12 -> 10; matrix products, arithmetic and copies ran while one was open for 48% -> 47% of each run, Pallas kernels for 18% -> 18%
where the time goes in v4:
time: 768 us; the launch traced here: 762 us
  matrix products  237 us (31%)
  waiting for transfers between devices  156 us (20%)
  Pallas kernels  135 us (18%)
  other arithmetic  101 us (13%)
  starting transfers between devices  64.8 us (8%)
  local copies, waits for them, and re-layouts  37.6 us (5%)
  between operations  16.8 us (2%)
  blocking collectives  14.6 us (2%)
    ppermute x21, waiting for transfers between devices, shift(): return lax.ppermute(x, 'tensor', pairs)  82.6 us
    dot_general x4, matrix products, contract_rows(): lax.dot_general(left, right, (((0,), (0,)), ((), ())), preferred_element_...  67.3 us
    pallas_call x2, Pallas kernels, attention_backward(): pl.pallas_call(kernel, grid_spec=pltpu.PrefetchScalarGridSpec(num_scalar_...  63.7 us
    dot_general x8, matrix products, contract_cols(): lax.dot_general(left, right, (((1,), (1,)), ((), ())), preferred_element_...  62.2 us
    ppermute x21, starting transfers between devices, shift(): return lax.ppermute(x, 'tensor', pairs)  54 us
    dot_general x4, matrix products, widen(): jnp.dot(ring[k], full_up, preferred_element_type=jnp.float32) + full_ubias  42.4 us
    reduce_scatter x4, waiting for transfers between devices, scatter_low(): lax.psum_scatter(part.astype(jnp.bfloat16), axis, scatter_dimension=dim,...  39.1 us
    pallas_call x1, Pallas kernels, attention_forward(): pl.pallas_call(kernel, grid_spec=pltpu.PrefetchScalarGridSpec(num_scalar_...  37.6 us
  transfers between devices with their start and end apart: 31, of which 10 were waited for; matrix products, arithmetic and copies ran while one was open for 47% of the time, Pallas kernels for 18%

profile of v4, /device:TPU:0, one launch (start us, length us, event | category | flops | bytes accessed | tf_op | source)
XLA Modules:
  0.0 762.5 jit_solution(17356939473664959232)
XLA Ops:
  24.9 14.6 %all-reduce = bf16[3584]{0:T(1024)(128)(2,1)S(1)} all-reduce(bf16[3584]{0:T(1024)(128)(2,1)S(1)} %dynamic-update-slice), channel_id=2, replica_groups=mesh['dp'=8,'tensor'=4] {'dp'}, use_global_device_ids=true, to_apply=%add | all-reduce | flops 3584 | bytes 14336
  55.3 14.1 %collective-permute-done = bf16[512,2048]{1,0:T(8,128)(2,1)} collective-permute-done((bf16[512,2048]{1,0:T(8,128)(2,1)}, bf16[512,2048]{1,0:T(8,128)(2,1)}, u32[]{:S(2)}, u32[]{:S(2)}) %collective-permute-start) | collective-permute-done | bytes 2097184 | tf_op jit(solution)/shard_map/ppermute | solution.py:364
  88.1 31.5 %collective-permute-done.1 = bf16[512,2048]{1,0:T(8,128)(2,1)} collective-permute-done((bf16[512,2048]{1,0:T(8,128)(2,1)}, bf16[512,2048]{1,0:T(8,128)(2,1)}, u32[]{:S(2)}, u32[]{:S(2)}) %collective-permute-start.1) | collective-permute-done | bytes 2097184 | tf_op jit(solution)/shard_map/ppermute | solution.py:364
  142.5 16.4 %multiply_convert_fusion.1 = (bf16[512,2048]{1,0:T(8,128)(2,1)}, f32[512,2048]{1,0:T(8,128)}, f32[512,2048]{1,0:T(8,128)}, bf16[512,2048]{1,0:T(8,128)(2,1)}, f32[512,2048]{1,0:T(8,128)}, /*index=5*/bf16[512,2048]{1,0:T(8,128)(2,1)}) fusion(f32[2048]{0:T(1024)S(1)} %bitcast.102, f32[512,2048]{1,0:T(8,128)} %fusion.68, f32[512,2048]{1,0:T(8,128)S(1)} %fusion.67, ...), kind=kOutput, calls=%fused_computation.86 | convolution fusion | flops 4357881856 | bytes 37756928 | tf_op jit(solution)/shard_map/dot_general | solution.py:519
  158.9 9.8 %collective-permute-done.2 = bf16[512,2048]{1,0:T(8,128)(2,1)} collective-permute-done((bf16[512,2048]{1,0:T(8,128)(2,1)}, bf16[512,2048]{1,0:T(8,128)(2,1)}, u32[]{:S(2)}, u32[]{:S(2)}) %collective-permute-start.2) | collective-permute-done | bytes 2097184 | tf_op jit(solution)/shard_map/ppermute | solution.py:364
  175.9 10.0 %convolution_convert_fusion.8 = bf16[512,2048]{1,0:T(8,128)(2,1)} fusion(bf16[512,2048]{1,0:T(8,128)(2,1)} %get-tuple-element.269, bf16[2048,2048]{1,0:T(8,128)(2,1)} %all-gather.10.cloned.1.call-done.weight_ref), kind=kOutput, calls=%fused_computation.100 | convolution fusion | flops 4296015872 | bytes 12582912 | tf_op jit(solution)/shard_map/dot_general | solution.py:524
  191.9 10.3 %multiply_convert_fusion = (bf16[512,2048]{1,0:T(8,128)(2,1)S(1)}, f32[512,2048]{1,0:T(8,128)}) fusion(f32[2048]{0:T(1024)S(1)} %bitcast.103, bf16[512,2048]{1,0:T(8,128)(2,1)} %collective-permute-done.2, bf16[2048,2048]{1,0:T(8,128)(2,1)S(1)} %bitcast.105), kind=kOutput, calls=%fused_computation.85 | convolution fusion | flops 4315938816 | bytes 16785408 | tf_op jit(solution)/shard_map/dot_general | solution.py:519
  236.6 37.6 %attend.1 = (bf16[2048,512]{1,0:T(8,128)(2,1)}, bf16[2048,512]{1,0:T(8,128)(2,1)}, bf16[2048,512]{1,0:T(8,128)(2,1)}, bf16[2048,512]{1,0:T(8,128)(2,1)}, f32[4,2,2048]{2,1,0:T(2,128)S(1)}) custom-call(s32[8]{0:T(128)S(1)} %get-tuple-element.231.refs_0_, s32[8]{0:T(128)S(1)} %get-tuple-element.232.refs_1_, f32[512,1536]{1,0:T(8,128)} %fusion.65.refs_2_, ...), custom_call_target="tpu_custom_call" | custom-call | tf_op jit(solution)/shard_map/attend/pallas_call | solution.py:157
  313.4 10.1 %convolution_convert_fusion.2 = bf16[2048,2048]{1,0:T(8,128)(2,1)} fusion(bf16[2048,512]{1,0:T(8,128)(2,1)} %get-tuple-element.348, bf16[512,2048]{1,0:T(8,128)(2,1)} %all-gather.12.cloned.1.call-done), kind=kOutput, calls=%fused_computation.14 | convolution fusion | flops 4299161600 | bytes 12582912 | tf_op jit(solution)/shard_map/dot_general | solution.py:577
  323.8 10.9 %collective-permute-done.11 = bf16[512,2048]{1,0:T(8,128)(2,1)S(1)} collective-permute-done((bf16[512,2048]{1,0:T(8,128)(2,1)}, bf16[512,2048]{1,0:T(8,128)(2,1)S(1)}, u32[]{:S(2)}, u32[]{:S(2)}) %collective-permute-start.11) | collective-permute-done | bytes 2097184 | tf_op jit(solution)/shard_map/ppermute | solution.py:364
  344.2 9.4 %collective-permute-start.13 = (bf16[512,2048]{1,0:T(8,128)(2,1)}, bf16[512,2048]{1,0:T(8,128)(2,1)}, u32[]{:S(2)}, u32[]{:S(2)}) collective-permute-start(bf16[512,2048]{1,0:T(8,128)(2,1)} %add_convert_fusion.7), channel_id=1, source_target_pairs={{0,1},{1,2},{2,3},{4,5},{5,6},{6,7},{8,9},{9,10},{10,11},{12,13},{... | collective-permute-start | bytes 6291464 | tf_op jit(solution)/shard_map/ppermute | solution.py:364
  364.3 19.8 %convolution_convert_fusion.1 = bf16[2048,2048]{1,0:T(8,128)(2,1)} fusion(bf16[2048,2048]{1,0:T(8,128)(2,1)S(1)} %pad_maximum_fusion, bf16[512,2048]{1,0:T(8,128)(2,1)S(1)} %copy-done, bf16[512,2048]{1,0:T(8,128)(2,1)S(1)} %broadcast_select_fusion.block_ref, bf16[512,2048]{1,0:T(8,128)(2,1)S(1)} %broadcast_select_fusion.2.block_ref, ...), kind=kOutput, calls=%fused_computation.13 | convolution fusion | flops 17217617920 | bytes 25165824 | tf_op jit(solution)/shard_map/dot_general | solution.py:352
  407.9 32.5 %attend_back.2 = (bf16[2048,1536]{1,0:T(8,128)(2,1)}, f32[3,1,512]{2,1,0:T(1,128)S(1)}) custom-call(s32[8]{0:T(128)S(1)} %get-tuple-element.231.refs_0_, s32[8]{0:T(128)S(1)} %get-tuple-element.232.refs_1_, bf16[512,512]{1,0:T(8,128)(2,1)S(1)} %copy-done.16, bf16[512,512]{1,0:T(8,128)(2,1)S(1)} %copy-done.15, bf16[512,512]{1,0:T(8,128)(2,1)S(1)} %copy-done.17, ...), custom_call_target="tpu_custom_call" | custom-call | tf_op jit(solution)/shard_map/attend_back/pallas_call | solution.py:279
  440.4 8.7 %hidden_back.6.refs_0_ = bf16[2048,2048]{1,0:T(8,128)(2,1)} custom-call(bf16[512,2048]{1,0:T(8,128)(2,1)S(1)} %copy-done.5, bf16[2048,2048]{1,0:T(8,128)(2,1)} %all-gather.10.cloned.1.call-done.weight_ref, f32[512,2048]{1,0:T(8,128)S(1)} %copy-done.10, bf16[2048,2048]{1,0:T(8,128)(2,1)} %hidden_back.5.refs_0_), custom_call_target="tpu_custom_call", output_to_operand_aliasing={{}: (3, {})} | custom-call | flops 4294967296 | bytes 8388608 | tf_op jit(solution)/shard_map/hidden_back/pallas_call | solution.py:320
  465.5 31.1 %attend_back.3 = (bf16[2048,1536]{1,0:T(8,128)(2,1)}, f32[3,1,512]{2,1,0:T(1,128)S(1)}) custom-call(s32[8]{0:T(128)S(1)} %get-tuple-element.231.refs_0_, s32[8]{0:T(128)S(1)} %get-tuple-element.232.refs_1_, bf16[512,512]{1,0:T(8,128)(2,1)S(1)} %copy-done.16, bf16[512,512]{1,0:T(8,128)(2,1)S(1)} %copy-done.15, ...), custom_call_target="tpu_custom_call", output_to_operand_aliasing={{0}: (14, {}), {1}: (15, {})} | custom-call | tf_op jit(solution)/shard_map/attend_back/pallas_call | solution.py:279
  496.7 21.9 %convolution_convert_fusion = bf16[2048,2048]{1,0:T(8,128)(2,1)} fusion(bf16[2048,2048]{1,0:T(8,128)(2,1)} %pad_maximum_fusion.2, bf16[2048,2048]{1,0:T(8,128)(2,1)S(1)} %bitcast.77), kind=kOutput, calls=%fused_computation.12 | convolution fusion | flops 17184063488 | bytes 25165824 | tf_op jit(solution)/shard_map/dot_general | solution.py:352
  527.2 12.9 %fusion.55 = f32[1024,2048]{1,0:T(8,128)} fusion(bf16[2048,1536]{0,1:T(8,128)(2,1)} %bitcast.87, bf16[2048,1536]{1,0:T(8,128)(2,1)} %get-tuple-element.342), kind=kOutput, calls=%fused_computation.94 | convolution fusion | flops 6442450944 | bytes 17825792 | tf_op jit(solution)/shard_map/dot_general | solution.py:358
  540.2 15.7 %convolution_convert_fusion.3 = bf16[2048,1536]{1,0:T(8,128)(2,1)} fusion(bf16[2048,2048]{1,0:T(8,128)(2,1)S(1)} %bitcast.81, bf16[2048,1536]{1,0:T(8,128)(2,1)S(1)} %bitcast.83), kind=kOutput, calls=%fused_computation.15 | convolution fusion | flops 12888047616 | bytes 20971520 | tf_op jit(solution)/shard_map/dot_general | solution.py:352
  555.9 15.4 %add_convert_fusion.1 = bf16[1024,2048]{1,0:T(8,128)(2,1)} fusion(f32[1024,2048]{1,0:T(8,128)} %fusion.55, bf16[2048,2048]{1,0:T(8,128)(2,1)} %all-gather.8.cloned.1.call-done, bf16[2048,2048]{1,0:T(8,128)(2,1)} %hidden_back.7), kind=kOutput, calls=%fused_computation.6 | convolution fusion | flops 8594128896 | bytes 25165824 | tf_op jit(solution)/shard_map/dot_general | solution.py:358
  575.8 9.9 %convolution_convert_fusion.4 = bf16[512,2048]{1,0:T(8,128)(2,1)} fusion(bf16[2048,512]{1,0:T(8,128)(2,1)} %get-tuple-element.348, bf16[2048,2048]{1,0:T(8,128)(2,1)} %pad_maximum_fusion.1), kind=kOutput, calls=%fused_computation.96 | convolution fusion | flops 4296015872 | bytes 12582912 | tf_op jit(solution)/shard_map/dot_general | solution.py:352
  585.8 9.8 %fusion.53 = f32[1024,2048]{1,0:T(8,128)S(1)} fusion(bf16[2048,1536]{0,1:T(8,128)(2,1)} %bitcast.88, bf16[2048,1536]{1,0:T(8,128)(2,1)} %get-tuple-element.342), kind=kOutput, calls=%fused_computation.92 | convolution fusion | flops 6442450944 | bytes 17825792 | tf_op jit(solution)/shard_map/dot_general | solution.py:358
  595.6 14.0 %add_convert_fusion = bf16[1024,2048]{1,0:T(8,128)(2,1)} fusion(f32[1024,2048]{1,0:T(8,128)S(1)} %fusion.53, bf16[2048,2048]{1,0:T(8,128)(2,1)} %all-gather.8.cloned.1.call-done, bf16[2048,2048]{1,0:T(8,128)(2,1)} %hidden_back.7), kind=kOutput, calls=%fused_computation.5 | convolution fusion | flops 8594128896 | bytes 25165824 | tf_op jit(solution)/shard_map/dot_general | solution.py:358
  621.3 39.1 %reduce-scatter.9.cloned.1.call-done = bf16[256,1536]{1,0:T(8,128)(2,1)} async-done(((bf16[2048,1536]{1,0:T(8,128)(2,1)}), bf16[256,1536]{1,0:T(8,128)(2,1)}) %reduce-scatter.9.cloned.1.call-update) | async-done | bytes 786448 | tf_op jit(solution)/shard_map/reduce_scatter | solution.py:441
  703.1 33.1 %all-to-all-done = f32[32,1,516]{2,1,0:T(1,128)S(1)} async-done(((f32[32,1,516]{2,1,0:T(1,128)}), f32[32,1,516]{2,1,0:T(1,128)S(1)}, u32[]{:S(2)}, u32[]{:S(2)}) %all-to-all-start) | async-done | bytes 66080 | tf_op jit(solution)/shard_map/all_to_all | solution.py:666
  (308 shorter events, 307.2 us)
Async XLA Ops:
  7.2 63.8 %all-gather.6.cloned.1.call-start = ((), (), s32[]{:S(2)}) async-start(), calls=%async_computation.6 | async-start | bytes 7077888 | tf_op jit(solution)/shard_map/all_gather | solution.py:471
  9.7 117.1 %all-gather.8.cloned.1.call-start = ((), (), s32[]{:S(2)}) async-start(), calls=%async_computation.7 | async-start | bytes 9437184 | tf_op jit(solution)/shard_map/all_gather | solution.py:475
  17.5 158.4 %all-gather.10.cloned.1.call-start = ((), (), s32[]{:S(2)}) async-start(), calls=%async_computation.8 | async-start | bytes 9437184 | tf_op jit(solution)/shard_map/all_gather | solution.py:476
  18.3 214.1 %all-gather.12.cloned.1.call-start = ((), (), s32[]{:S(2)}) async-start(), calls=%async_computation.9 | async-start | bytes 2359296 | tf_op jit(solution)/shard_map/all_gather | solution.py:477
  18.3 51.0 %collective-permute-start = (bf16[512,2048]{1,0:T(8,128)(2,1)}, bf16[512,2048]{1,0:T(8,128)(2,1)}, u32[]{:S(2)}, u32[]{:S(2)}) collective-permute-start(bf16[512,2048]{1,0:T(8,128)(2,1)} %fusion.7), channel_id=1, source_target_pairs={{0,1},{1,2},{2,3},{3,0},{4,5},{5,6},{6,7},{7,4},{8,9},{9,10},{10,1... | collective-permute-start | bytes 6291464 | tf_op jit(solution)/shard_map/ppermute | solution.py:364
  70.7 48.9 %collective-permute-start.1 = (bf16[512,2048]{1,0:T(8,128)(2,1)}, bf16[512,2048]{1,0:T(8,128)(2,1)}, u32[]{:S(2)}, u32[]{:S(2)}) collective-permute-start(bf16[512,2048]{1,0:T(8,128)(2,1)} %collective-permute-done), channel_id=1, source_target_pairs={{0,1},{1,2},{2,3},{3,0},{4,5},{5,6},{6,7},{7,4},{8,9},{9,10},{10,1... | collective-permute-start | bytes 6291464 | tf_op jit(solution)/shard_map/ppermute | solution.py:364
  70.7 447.9 %reduce-scatter.5.cloned.1.call-start = ((), (), s32[]{:S(2)}) async-start(), calls=%async_computation.10 | async-start | bytes 9437184 | tf_op jit(solution)/shard_map/reduce_scatter | solution.py:441
  119.6 49.1 %collective-permute-start.2 = (bf16[512,2048]{1,0:T(8,128)(2,1)}, bf16[512,2048]{1,0:T(8,128)(2,1)}, u32[]{:S(2)}, u32[]{:S(2)}) collective-permute-start(bf16[512,2048]{1,0:T(8,128)(2,1)} %collective-permute-done.1), channel_id=1, source_target_pairs={{0,1},{1,2},{2,3},{3,0},{4,5},{5,6},{6,7},{7,4},{8,9},{9,10},{10,1... | collective-permute-start | bytes 6291464 | tf_op jit(solution)/shard_map/ppermute | solution.py:364
  168.7 51.7 %collective-permute-start.4 = (bf16[512,2048]{1,0:T(8,128)(2,1)S(1)}, bf16[512,2048]{1,0:T(8,128)(2,1)}, u32[]{:S(2)}, u32[]{:S(2)}) collective-permute-start(bf16[512,2048]{1,0:T(8,128)(2,1)S(1)} %copy-done), channel_id=1, source_target_pairs={{1,0},{2,1},{3,2},{5,4},{6,5},{7,6},{9,8},{10,9},{11,10},{13,12},{... | collective-permute-start | bytes 6291464 | tf_op jit(solution)/shard_map/ppermute | solution.py:364
  170.0 50.5 %collective-permute-start.3 = (bf16[512,2048]{1,0:T(8,128)(2,1)S(1)}, bf16[512,2048]{1,0:T(8,128)(2,1)}, u32[]{:S(2)}, u32[]{:S(2)}) collective-permute-start(bf16[512,2048]{1,0:T(8,128)(2,1)S(1)} %copy-done), channel_id=1, source_target_pairs={{0,1},{1,2},{2,3},{4,5},{5,6},{6,7},{8,9},{9,10},{10,11},{12,13},{... | collective-permute-start | bytes 6291464 | tf_op jit(solution)/shard_map/ppermute | solution.py:364
  220.5 53.7 %collective-permute-start.5 = (bf16[512,2048]{1,0:T(8,128)(2,1)}, bf16[512,2048]{1,0:T(8,128)(2,1)}, u32[]{:S(2)}, u32[]{:S(2)}) collective-permute-start(bf16[512,2048]{1,0:T(8,128)(2,1)} %collective-permute-done.3), channel_id=1, source_target_pairs={{1,2},{2,3},{5,6},{6,7},{9,10},{10,11},{13,14},{14,15},{17,18},{18... | collective-permute-start | bytes 6291464 | tf_op jit(solution)/shard_map/ppermute | solution.py:364
  222.4 51.8 %collective-permute-start.6 = (bf16[512,2048]{1,0:T(8,128)(2,1)}, bf16[512,2048]{1,0:T(8,128)(2,1)}, u32[]{:S(2)}, u32[]{:S(2)}) collective-permute-start(bf16[512,2048]{1,0:T(8,128)(2,1)} %collective-permute-done.4), channel_id=1, source_target_pairs={{1,0},{2,1},{5,4},{6,5},{9,8},{10,9},{13,12},{14,13},{17,16},{18,1... | collective-permute-start | bytes 6291464 | tf_op jit(solution)/shard_map/ppermute | solution.py:364
  223.7 50.5 %collective-permute-start.7 = (bf16[512,2048]{1,0:T(8,128)(2,1)}, bf16[512,2048]{1,0:T(8,128)(2,1)}, u32[]{:S(2)}, u32[]{:S(2)}) collective-permute-start(bf16[512,2048]{1,0:T(8,128)(2,1)} %convolution_convert_fusion.7), channel_id=1, source_target_pairs={{0,1},{4,5},{8,9},{12,13},{16,17},{20,21},{24,25},{28,29}} | collective-permute-start | bytes 6291464 | tf_op jit(solution)/shard_map/ppermute | solution.py:364
  274.2 49.2 %collective-permute-start.9 = (bf16[512,2048]{1,0:T(8,128)(2,1)}, bf16[512,2048]{1,0:T(8,128)(2,1)S(1)}, u32[]{:S(2)}, u32[]{:S(2)}) collective-permute-start(bf16[512,2048]{1,0:T(8,128)(2,1)} %collective-permute-done.5), channel_id=1, source_target_pairs={{2,3},{6,7},{10,11},{14,15},{18,19},{22,23},{26,27},{30,31}} | collective-permute-start | bytes 6291464 | tf_op jit(solution)/shard_map/ppermute | solution.py:364
  275.2 48.7 %collective-permute-start.10 = (bf16[512,2048]{1,0:T(8,128)(2,1)}, bf16[512,2048]{1,0:T(8,128)(2,1)S(1)}, u32[]{:S(2)}, u32[]{:S(2)}) collective-permute-start(bf16[512,2048]{1,0:T(8,128)(2,1)} %collective-permute-done.6), channel_id=1, source_target_pairs={{1,0},{5,4},{9,8},{13,12},{17,16},{21,20},{25,24},{29,28}} | collective-permute-start | bytes 6291464 | tf_op jit(solution)/shard_map/ppermute | solution.py:364
  339.2 51.0 %collective-permute-start.14 = (bf16[512,2048]{1,0:T(8,128)(2,1)}, bf16[512,2048]{1,0:T(8,128)(2,1)}, u32[]{:S(2)}, u32[]{:S(2)}) collective-permute-start(bf16[512,2048]{1,0:T(8,128)(2,1)} %add_convert_fusion.6), channel_id=1, source_target_pairs={{1,0},{2,1},{3,2},{5,4},{6,5},{7,6},{9,8},{10,9},{11,10},{13,12},{... | collective-permute-start | bytes 6291464 | tf_op jit(solution)/shard_map/ppermute | solution.py:364
  344.2 50.9 %collective-permute-start.13 = (bf16[512,2048]{1,0:T(8,128)(2,1)}, bf16[512,2048]{1,0:T(8,128)(2,1)}, u32[]{:S(2)}, u32[]{:S(2)}) collective-permute-start(bf16[512,2048]{1,0:T(8,128)(2,1)} %add_convert_fusion.7), channel_id=1, source_target_pairs={{0,1},{1,2},{2,3},{4,5},{5,6},{6,7},{8,9},{9,10},{10,11},{12,13},{... | collective-permute-start | bytes 6291464 | tf_op jit(solution)/shard_map/ppermute | solution.py:364
  395.2 214.3 %reduce-scatter.7.cloned.1.call-start = ((), (), s32[]{:S(2)}) async-start(), calls=%async_computation.11 | async-start | bytes 9437184 | tf_op jit(solution)/shard_map/reduce_scatter | solution.py:441
  398.6 58.9 %collective-permute-start.15 = (bf16[512,2048]{1,0:T(8,128)(2,1)}, bf16[512,2048]{1,0:T(8,128)(2,1)}, u32[]{:S(2)}, u32[]{:S(2)}) collective-permute-start(bf16[512,2048]{1,0:T(8,128)(2,1)} %slice.69), channel_id=1, source_target_pairs={{0,1},{1,2},{2,3},{3,0},{4,5},{5,6},{6,7},{7,4},{8,9},{9,10},{10,1... | collective-permute-start | bytes 6291464 | tf_op jit(solution)/shard_map/ppermute | solution.py:364
  462.1 59.2 %collective-permute-start.16 = (bf16[512,2048]{1,0:T(8,128)(2,1)}, bf16[512,2048]{1,0:T(8,128)(2,1)}, u32[]{:S(2)}, u32[]{:S(2)}) collective-permute-start(bf16[512,2048]{1,0:T(8,128)(2,1)} %add_convert_fusion.5), channel_id=1, source_target_pairs={{0,1},{1,2},{2,3},{3,0},{4,5},{5,6},{6,7},{7,4},{8,9},{9,10},{10,1... | collective-permute-start | bytes 6291464 | tf_op jit(solution)/shard_map/ppermute | solution.py:364
  521.3 139.1 %reduce-scatter.9.cloned.1.call-start = ((), (), s32[]{:S(2)}) async-start(), calls=%async_computation.12 | async-start | bytes 7077888 | tf_op jit(solution)/shard_map/reduce_scatter | solution.py:441
  571.3 165.0 %reduce-scatter.11.cloned.1.call-start = ((), (), s32[]{:S(2)}) async-start(), calls=%async_computation.13 | async-start | bytes 2359296 | tf_op jit(solution)/shard_map/reduce_scatter | solution.py:441
  621.0 54.6 %collective-permute-start.19 = (bf16[512,2048]{1,0:T(8,128)(2,1)}, bf16[512,2048]{1,0:T(8,128)(2,1)}, u32[]{:S(2)}, u32[]{:S(2)}) collective-permute-start(bf16[512,2048]{1,0:T(8,128)(2,1)} %add_convert_fusion.3), channel_id=1, source_target_pairs={{0,1},{1,2},{2,3},{3,0},{4,5},{5,6},{6,7},{7,4},{8,9},{9,10},{10,1... | collective-permute-start | bytes 6291464 | tf_op jit(solution)/shard_map/ppermute | solution.py:364
  680.3 57.8 %collective-permute-start.20 = (bf16[512,2048]{1,0:T(8,128)(2,1)}, bf16[512,2048]{1,0:T(8,128)(2,1)}, u32[]{:S(2)}, u32[]{:S(2)}) collective-permute-start(bf16[512,2048]{1,0:T(8,128)(2,1)} %add_convert_fusion.2), channel_id=1, source_target_pairs={{0,1},{1,2},{2,3},{3,0},{4,5},{5,6},{6,7},{7,4},{8,9},{9,10},{10,1... | collective-permute-start | bytes 6291464 | tf_op jit(solution)/shard_map/ppermute | solution.py:364
  (71 other events, 1156.2 us)
Sparse Core Ops, SparseCore 0:
  10.5 49.5 all-gather.5
  62.0 54.3 all-gather.7
  118.3 55.9 all-gather.9
  176.0 28.1 all-gather.11
  395.3 77.0 reduce-scatter.4
  521.5 73.7 reduce-scatter.6
  598.6 61.7 reduce-scatter.8
  664.0 41.4 reduce-scatter.10

commit v5 on v3

--- a/solution.py
+++ b/solution.py
@@ -440,7 +440,7 @@
 def scatter_low(part, axis, dim):
     return lax.psum_scatter(
         part.astype(jnp.bfloat16), axis, scatter_dimension=dim, tiled=True
-    ).astype(jnp.float32)
+    )
 
 
 def body(
@@ -525,9 +525,10 @@
             hidden_act[k], full_down, preferred_element_type=jnp.float32
         ).astype(low)
 
-    def back(k):
-        block = cot.block(k)
+    def context_back(k, block):
         grad_context[k] = contract_cols(block, full_dense).astype(low)
+
+    def inner_back(k, block):
         grad_pre[0] = hidden_back(
             block, full_down, slopes[k], (k - 1) % ways, ways, held=grad_pre[0]
         )
@@ -570,34 +571,35 @@
     cot.step()
     mlp.step()
     for k in [0, *range(2, ways - 1)]:
-        back(k)
+        context_back(k, cot.block(k))
+        inner_back(k, cot.block(k))
     acts = jnp.concatenate(turned(hidden_act), axis=0)
     attn_part = jnp.dot(context_low, full_dense, preferred_element_type=jnp.float32).astype(low)
-    grad_context, grad_pre, acts, slopes, attn_part = together(
-        cot, mlp, after=(grad_context, grad_pre, acts, slopes, attn_part)
+    normed_low = jnp.concatenate(turned(ring), axis=0)
+    grad_context, grad_pre, acts, slopes, attn_part, normed_low = together(
+        cot, mlp, after=(grad_context, grad_pre, acts, slopes, attn_part, normed_low)
     )
 
     while mlp.k < ways:
         mlp.step()
-    for k in sorted({1, ways - 1}):
-        back(k)
-    grad_full = jnp.concatenate(turned([cot.block(k) for k in range(ways)]), axis=0)
-    grad_context, grad_pre, attn_part, grad_full, acts = together(
-        mlp, after=(grad_context, grad_pre, attn_part, grad_full, acts)
-    )
-    [pre_full] = grad_pre
+    blocks = [cot.block(k) for k in range(ways)]
+    late = sorted({1, ways - 1})
+    for k in late:
+        context_back(k, blocks[k])
+    grad_full = jnp.concatenate(turned(blocks), axis=0)
+    grad_down = contract_rows(acts, grad_full).astype(low)
+    grad_context, attn_part, grad_full, grad_down, blocks, grad_pre, slopes = together(
+        mlp, after=(grad_context, attn_part, grad_full, grad_down, blocks, grad_pre, slopes)
+    )
+    part_down = scatter_low(grad_down, "dp", 1)
 
     attn = RingScatter([attn_part], row_count)
     attn.step()
     grads = attention_backward(query, keys, values, turned(grad_context), logsum, tables, 0, half)
-    grad_down = contract_rows(acts, grad_full).astype(low)
-    normed_low = jnp.concatenate(turned(ring), axis=0)
-    grads, grad_context, grad_full, context_low, grad_down, pre_full, normed_low = together(
-        attn,
-        mlp,
-        after=(grads, grad_context, grad_full, context_low, grad_down, pre_full, normed_low),
-    )
-    part_down = scatter_low(grad_down, "dp", 1)
+    inner_back(late[0], blocks[late[0]])
+    grads, grad_context, grad_full, context_low, grad_pre, normed_low = together(
+        attn, mlp, after=(grads, grad_context, grad_full, context_low, grad_pre, normed_low)
+    )
 
     while attn.k < ways - 2:
         attn.step()
@@ -605,12 +607,15 @@
         grads = attention_backward(
             query, keys, values, turned(grad_context), logsum, tables, half, pairs - half, held=grads
         )
-    grad_up = contract_rows(normed_low, pre_full).astype(low)
-    grads, grad_up, pre_full, normed_low, grad_full, context_low = together(
-        attn, mlp, after=(grads, grad_up, pre_full, normed_low, grad_full, context_low)
-    )
-    part_up = scatter_low(grad_up, "dp", 0)
+    for k in late[1:]:
+        inner_back(k, blocks[k])
+    grad_dense = contract_rows(context_low, grad_full).astype(low)
+    grads, grad_dense, grad_pre, normed_low, part_down = together(
+        attn, mlp, after=(grads, grad_dense, grad_pre, normed_low, part_down)
+    )
+    part_dense = scatter_low(grad_dense, "dp", 1)
     grad_proj, grad_qbias = grads[0], grads[1][:, 0, :]
+    [pre_full] = grad_pre
 
     def return_normed(low_block, high_block):
         rows = slice(low_block * row_count, high_block * row_count)
@@ -620,33 +625,36 @@
     attn.step()
     grad_qkv = contract_rows(normed_low, grad_proj).astype(low)
     grad_parts = [return_normed(0, ways // 2)]
-    grad_parts, grad_qkv, pre_full, grad_proj, grad_full, context_low, part_down = together(
-        attn,
-        mlp,
-        after=(grad_parts, grad_qkv, pre_full, grad_proj, grad_full, context_low, part_down),
-    )
-    part_qkv = scatter_low(grad_qkv, "dp", 0).reshape(-1, pairs, 3, PAIR)
-    part_qkv = part_qkv.transpose(2, 0, 1, 3).reshape(3, -1, pairs * PAIR)
+    grad_parts, grad_qkv, pre_full, grad_proj, normed_low = together(
+        attn, mlp, after=(grad_parts, grad_qkv, pre_full, grad_proj, normed_low)
+    )
+    part_qkv = scatter_low(grad_qkv, "dp", 0)
 
     last = RingScatter(grad_parts, row_count)
     last.step()
     last.parts.append(return_normed(ways // 2, ways))
-    grad_dense = contract_rows(context_low, grad_full).astype(low)
-    grad_dense, pre_full, part_up = together(last, attn, mlp, after=(grad_dense, pre_full, part_up))
-    part_dense = scatter_low(grad_dense, "dp", 1)
+    grad_up = contract_rows(normed_low, pre_full).astype(low)
+    grad_up, pre_full, part_dense = together(
+        last, attn, mlp, after=(grad_up, pre_full, part_dense)
+    )
+    part_up = scatter_low(grad_up, "dp", 0)
     while last.k < ways - 2:
         last.step()
     grad_ubias = jnp.sum(pre_full, axis=0, dtype=jnp.float32)
+    part_down, part_dense = part_down.astype(jnp.float32), part_dense.astype(jnp.float32)
     attn_mine, mlp_mine = attn.total(), mlp.total()
-    attn_mine, mlp_mine, grad_ubias, part_qkv = together(
-        last, after=(attn_mine, mlp_mine, grad_ubias, part_qkv)
-    )
+    attn_mine, mlp_mine, grad_ubias, part_down, part_dense, part_qkv = together(
+        last, after=(attn_mine, mlp_mine, grad_ubias, part_down, part_dense, part_qkv)
+    )
+    part_qkv = part_qkv.astype(jnp.float32).reshape(-1, pairs, 3, PAIR)
+    part_qkv = part_qkv.transpose(2, 0, 1, 3).reshape(3, -1, pairs * PAIR)
     last.step()
     output = (resid + attn_mine + mlp_mine + out_bias).astype(low)
     attn_square = jnp.sum(valid_mine * attn_mine * attn_mine)
     mlp_square = jnp.sum(valid_mine * mlp_mine * mlp_mine)
-    output, attn_square, mlp_square, part_dense = together(
-        last, after=(output, attn_square, mlp_square, part_dense)
+    part_up = part_up.astype(jnp.float32)
+    output, attn_square, mlp_square, part_up, part_qkv = together(
+        last, after=(output, attn_square, mlp_square, part_up, part_qkv)
     )
     grad_mine = last.total()
     scaled = grad_mine * norm_gain

time: 757 us -> 743 us (0.982)
  waiting for transfers between devices: 153 us -> 143 us
    reduce_scatter x4, waiting for transfers between devices: 67.8 us -> 19 us  [scatter_low(): lax.psum_scatter(part.astype(jnp.bfloat16), axis, scatter_dimension=dim,...]
    ppermute x21, waiting for transfers between devices: 81.6 us -> 123 us  [shift(): return lax.ppermute(x, 'tensor', pairs)]
where the time goes in v5:
time: 743 us; the launch traced here: 729 us
  matrix products  234 us (31%)
  waiting for transfers between devices  143 us (19%)
  Pallas kernels  131 us (18%)
  other arithmetic  102 us (14%)
  starting transfers between devices  51.4 us (7%)
  local copies, waits for them, and re-layouts  36.2 us (5%)
  between operations  16.7 us (2%)
  blocking collectives  14.6 us (2%)
    ppermute x21, waiting for transfers between devices, shift(): return lax.ppermute(x, 'tensor', pairs)  123 us
    dot_general x4, matrix products, contract_rows(): lax.dot_general(left, right, (((0,), (0,)), ((), ())), preferred_element_...  67 us
    dot_general x8, matrix products, contract_cols(): lax.dot_general(left, right, (((1,), (1,)), ((), ())), preferred_element_...  63 us
    pallas_call x2, Pallas kernels, attention_backward(): pl.pallas_call(kernel, grid_spec=pltpu.PrefetchScalarGridSpec(num_scalar_...  60.8 us
    ppermute x21, starting transfers between devices, shift(): return lax.ppermute(x, 'tensor', pairs)  47.7 us
    dot_general x4, matrix products, widen(): jnp.dot(ring[k], full_up, preferred_element_type=jnp.float32) + full_ubias  42.3 us
    pallas_call x1, Pallas kernels, attention_forward(): pl.pallas_call(kernel, grid_spec=pltpu.PrefetchScalarGridSpec(num_scalar_...  36.7 us
    pallas_call x4, Pallas kernels, hidden_back(): pl.pallas_call(hidden_back_kernel, grid=(hidden // tile,), in_specs=[pl.B...  33.6 us
  transfers between devices with their start and end apart: 30, of which 12 were waited for; matrix products, arithmetic and copies ran while one was open for 48% of the time, Pallas kernels for 18%

profile of v5, /device:TPU:0, one launch (start us, length us, event | category | flops | bytes accessed | tf_op | source)
XLA Modules:
  0.0 728.8 jit_solution(2871891381910922665)
XLA Ops:
  24.9 14.6 %all-reduce = bf16[3584]{0:T(1024)(128)(2,1)S(1)} all-reduce(bf16[3584]{0:T(1024)(128)(2,1)S(1)} %dynamic-update-slice), channel_id=2, replica_groups=mesh['dp'=8,'tensor'=4] {'dp'}, use_global_device_ids=true, to_apply=%add | all-reduce | flops 3584 | bytes 14336
  55.4 14.0 %collective-permute-done = bf16[512,2048]{1,0:T(8,128)(2,1)} collective-permute-done((bf16[512,2048]{1,0:T(8,128)(2,1)}, bf16[512,2048]{1,0:T(8,128)(2,1)}, u32[]{:S(2)}, u32[]{:S(2)}) %collective-permute-start) | collective-permute-done | bytes 2097184 | tf_op jit(solution)/shard_map/ppermute | solution.py:364
  88.1 31.5 %collective-permute-done.1 = bf16[512,2048]{1,0:T(8,128)(2,1)} collective-permute-done((bf16[512,2048]{1,0:T(8,128)(2,1)}, bf16[512,2048]{1,0:T(8,128)(2,1)}, u32[]{:S(2)}, u32[]{:S(2)}) %collective-permute-start.1) | collective-permute-done | bytes 2097184 | tf_op jit(solution)/shard_map/ppermute | solution.py:364
  142.2 16.4 %multiply_convert_fusion.1 = (bf16[512,2048]{1,0:T(8,128)(2,1)}, f32[512,2048]{1,0:T(8,128)}, f32[512,2048]{1,0:T(8,128)}, bf16[512,2048]{1,0:T(8,128)(2,1)}, f32[512,2048]{1,0:T(8,128)}, /*index=5*/bf16[512,2048]{1,0:T(8,128)(2,1)}) fusion(f32[2048]{0:T(1024)S(1)} %bitcast.97, f32[512,2048]{1,0:T(8,128)} %fusion.68, f32[512,2048]{1,0:T(8,128)S(1)} %fusion.67, ...), kind=kOutput, calls=%fused_computation.86 | convolution fusion | flops 4357881856 | bytes 37756928 | tf_op jit(solution)/shard_map/dot_general | solution.py:519
  158.5 9.9 %collective-permute-done.2 = bf16[512,2048]{1,0:T(8,128)(2,1)} collective-permute-done((bf16[512,2048]{1,0:T(8,128)(2,1)}, bf16[512,2048]{1,0:T(8,128)(2,1)}, u32[]{:S(2)}, u32[]{:S(2)}) %collective-permute-start.2) | collective-permute-done | bytes 2097184 | tf_op jit(solution)/shard_map/ppermute | solution.py:364
  175.7 10.0 %convolution_convert_fusion.8 = bf16[512,2048]{1,0:T(8,128)(2,1)} fusion(bf16[512,2048]{1,0:T(8,128)(2,1)} %get-tuple-element.271, bf16[2048,2048]{1,0:T(8,128)(2,1)} %all-gather.10.cloned.1.call-done.weight_ref), kind=kOutput, calls=%fused_computation.100 | convolution fusion | flops 4296015872 | bytes 12582912 | tf_op jit(solution)/shard_map/dot_general | solution.py:524
  191.7 10.2 %multiply_convert_fusion = (bf16[512,2048]{1,0:T(8,128)(2,1)S(1)}, f32[512,2048]{1,0:T(8,128)}) fusion(f32[2048]{0:T(1024)S(1)} %bitcast.98, bf16[512,2048]{1,0:T(8,128)(2,1)} %collective-permute-done.2, bf16[2048,2048]{1,0:T(8,128)(2,1)S(1)} %bitcast.100), kind=kOutput, calls=%fused_computation.85 | convolution fusion | flops 4315938816 | bytes 16785408 | tf_op jit(solution)/shard_map/dot_general | solution.py:519
  237.1 36.7 %attend.1 = (bf16[2048,512]{1,0:T(8,128)(2,1)}, bf16[2048,512]{1,0:T(8,128)(2,1)}, bf16[2048,512]{1,0:T(8,128)(2,1)}, bf16[2048,512]{1,0:T(8,128)(2,1)}, f32[4,2,2048]{2,1,0:T(2,128)S(1)}) custom-call(s32[8]{0:T(128)S(1)} %get-tuple-element.233.refs_0_, s32[8]{0:T(128)S(1)} %get-tuple-element.234.refs_1_, f32[512,1536]{1,0:T(8,128)} %fusion.65.refs_2_, ...), custom_call_target="tpu_custom_call" | custom-call | tf_op jit(solution)/shard_map/attend/pallas_call | solution.py:157
  294.8 8.4 %hidden_back.4.refs_0_ = bf16[2048,2048]{1,0:T(8,128)(2,1)} custom-call(bf16[512,2048]{1,0:T(8,128)(2,1)S(1)} %copy-done, bf16[2048,2048]{1,0:T(8,128)(2,1)} %all-gather.10.cloned.1.call-done.weight_ref, f32[512,2048]{1,0:T(8,128)S(1)} %copy-done.13), custom_call_target="tpu_custom_call" | custom-call | flops 4294967296 | bytes 8388608 | tf_op jit(solution)/shard_map/hidden_back/pallas_call | solution.py:320
  327.2 10.1 %collective-permute-done.11 = bf16[512,2048]{1,0:T(8,128)(2,1)} collective-permute-done((bf16[512,2048]{1,0:T(8,128)(2,1)}, bf16[512,2048]{1,0:T(8,128)(2,1)}, u32[]{:S(2)}, u32[]{:S(2)}) %collective-permute-start.11) | collective-permute-done | bytes 2097184 | tf_op jit(solution)/shard_map/ppermute | solution.py:364
  368.5 19.8 %convolution_convert_fusion.1 = bf16[2048,2048]{1,0:T(8,128)(2,1)} fusion(bf16[2048,2048]{1,0:T(8,128)(2,1)S(1)} %pad_maximum_fusion, bf16[512,2048]{1,0:T(8,128)(2,1)S(1)} %copy-done, bf16[512,2048]{1,0:T(8,128)(2,1)S(1)} %broadcast_select_fusion.block_ref, bf16[512,2048]{1,0:T(8,128)(2,1)S(1)} %broadcast_select_fusion.2.block_ref, ...), kind=kOutput, calls=%fused_computation.13 | convolution fusion | flops 17217617920 | bytes 25165824 | tf_op jit(solution)/shard_map/dot_general | solution.py:352
  403.7 30.4 %attend_back.2 = (bf16[2048,1536]{1,0:T(8,128)(2,1)}, f32[3,1,512]{2,1,0:T(1,128)S(1)}) custom-call(s32[8]{0:T(128)S(1)} %get-tuple-element.233.refs_0_, s32[8]{0:T(128)S(1)} %get-tuple-element.234.refs_1_, bf16[512,512]{1,0:T(8,128)(2,1)S(1)} %copy-done.16, bf16[512,512]{1,0:T(8,128)(2,1)S(1)} %copy-done.15, bf16[512,512]{1,0:T(8,128)(2,1)S(1)} %copy-done.17, ...), custom_call_target="tpu_custom_call" | custom-call | tf_op jit(solution)/shard_map/attend_back/pallas_call | solution.py:279
  454.6 30.3 %attend_back.3 = (bf16[2048,1536]{1,0:T(8,128)(2,1)}, f32[3,1,512]{2,1,0:T(1,128)S(1)}) custom-call(s32[8]{0:T(128)S(1)} %get-tuple-element.233.refs_0_, s32[8]{0:T(128)S(1)} %get-tuple-element.234.refs_1_, bf16[512,512]{1,0:T(8,128)(2,1)S(1)} %copy-done.16, bf16[512,512]{1,0:T(8,128)(2,1)S(1)} %copy-done.15, ...), custom_call_target="tpu_custom_call", output_to_operand_aliasing={{0}: (14, {}), {1}: (15, {})} | custom-call | tf_op jit(solution)/shard_map/attend_back/pallas_call | solution.py:279
  485.0 8.4 %hidden_back.7 = bf16[2048,2048]{1,0:T(8,128)(2,1)} custom-call(bf16[512,2048]{1,0:T(8,128)(2,1)S(1)} %copy-done.3, bf16[2048,2048]{1,0:T(8,128)(2,1)} %all-gather.10.cloned.1.call-done.weight_ref, f32[512,2048]{1,0:T(8,128)S(1)} %copy-done.10, bf16[2048,2048]{1,0:T(8,128)(2,1)} %hidden_back.6.refs_0_), custom_call_target="tpu_custom_call", output_to_operand_aliasing={{}: (3, {})} | custom-call | flops 4294967296 | bytes 8388608 | tf_op jit(solution)/shard_map/hidden_back/pallas_call | solution.py:320
  493.4 9.1 %convolution_convert_fusion.4 = bf16[512,2048]{1,0:T(8,128)(2,1)} fusion(bf16[2048,512]{1,0:T(8,128)(2,1)S(1)} %copy-done.55, bf16[2048,2048]{1,0:T(8,128)(2,1)} %pad_maximum_fusion.2), kind=kOutput, calls=%fused_computation.96 | convolution fusion | flops 4296015872 | bytes 12582912 | tf_op jit(solution)/shard_map/dot_general | solution.py:352
  506.7 17.5 %convolution_convert_fusion.3 = bf16[2048,1536]{1,0:T(8,128)(2,1)} fusion(bf16[2048,2048]{1,0:T(8,128)(2,1)} %pad_maximum_fusion.1, bf16[2048,1536]{1,0:T(8,128)(2,1)S(1)} %copy-done.24), kind=kOutput, calls=%fused_computation.15 | convolution fusion | flops 12888047616 | bytes 20971520 | tf_op jit(solution)/shard_map/dot_general | solution.py:352
  524.1 9.9 %fusion.55 = f32[1024,2048]{1,0:T(8,128)S(1)} fusion(bf16[2048,1536]{0,1:T(8,128)(2,1)} %bitcast.82, bf16[2048,1536]{1,0:T(8,128)(2,1)} %get-tuple-element.343), kind=kOutput, calls=%fused_computation.94 | convolution fusion | flops 6442450944 | bytes 17825792 | tf_op jit(solution)/shard_map/dot_general | solution.py:358
  534.1 13.9 %add_convert_fusion.1 = bf16[1024,2048]{1,0:T(8,128)(2,1)} fusion(f32[1024,2048]{1,0:T(8,128)S(1)} %fusion.55, bf16[2048,2048]{1,0:T(8,128)(2,1)} %all-gather.8.cloned.1.call-done, bf16[2048,2048]{1,0:T(8,128)(2,1)} %hidden_back.7), kind=kOutput, calls=%fused_computation.6 | convolution fusion | flops 8594128896 | bytes 25165824 | tf_op jit(solution)/shard_map/dot_general | solution.py:358
  556.3 13.8 %fusion.53 = f32[1024,2048]{1,0:T(8,128)} fusion(bf16[2048,1536]{0,1:T(8,128)(2,1)} %bitcast.83, bf16[2048,1536]{1,0:T(8,128)(2,1)} %get-tuple-element.343), kind=kOutput, calls=%fused_computation.92 | convolution fusion | flops 6442450944 | bytes 17825792 | tf_op jit(solution)/shard_map/dot_general | solution.py:358
  570.2 20.6 %convolution_convert_fusion = bf16[2048,2048]{1,0:T(8,128)(2,1)} fusion(bf16[2048,2048]{1,0:T(8,128)(2,1)S(1)} %bitcast.78, bf16[2048,2048]{1,0:T(8,128)(2,1)S(1)} %bitcast.76), kind=kOutput, calls=%fused_computation.12 | convolution fusion | flops 17184063488 | bytes 25165824 | tf_op jit(solution)/shard_map/dot_general | solution.py:352
  590.8 15.2 %add_convert_fusion = bf16[1024,2048]{1,0:T(8,128)(2,1)} fusion(f32[1024,2048]{1,0:T(8,128)} %fusion.53, bf16[2048,2048]{1,0:T(8,128)(2,1)} %all-gather.8.cloned.1.call-done, bf16[2048,2048]{1,0:T(8,128)(2,1)} %hidden_back.7), kind=kOutput, calls=%fused_computation.5 | convolution fusion | flops 8594128896 | bytes 25165824 | tf_op jit(solution)/shard_map/dot_general | solution.py:358
  627.2 25.8 %collective-permute-done.19 = bf16[512,2048]{1,0:T(8,128)(2,1)S(1)} collective-permute-done((bf16[512,2048]{1,0:T(8,128)(2,1)S(1)}, bf16[512,2048]{1,0:T(8,128)(2,1)S(1)}, u32[]{:S(2)}, u32[]{:S(2)}) %collective-permute-start.19) | collective-permute-done | bytes 2097184 | tf_op jit(solution)/shard_map/ppermute | solution.py:364
  668.5 19.0 %reduce-scatter.11.cloned.1.call-done = bf16[256,2048]{1,0:T(8,128)(2,1)} async-done(((bf16[2048,2048]{1,0:T(8,128)(2,1)}), bf16[256,2048]{1,0:T(8,128)(2,1)}) %reduce-scatter.11.cloned.1.call-update) | async-done | bytes 1048592 | tf_op jit(solution)/shard_map/reduce_scatter | solution.py:441
  690.4 9.8 %collective-permute-done.20 = bf16[512,2048]{1,0:T(8,128)(2,1)} collective-permute-done((bf16[512,2048]{1,0:T(8,128)(2,1)}, bf16[512,2048]{1,0:T(8,128)(2,1)}, u32[]{:S(2)}, u32[]{:S(2)}) %collective-permute-start.20) | collective-permute-done | bytes 2097184 | tf_op jit(solution)/shard_map/ppermute | solution.py:364
  (306 shorter events, 306.7 us)
Async XLA Ops:
  7.2 64.0 %all-gather.6.cloned.1.call-start = ((), (), s32[]{:S(2)}) async-start(), calls=%async_computation.5 | async-start | bytes 7077888 | tf_op jit(solution)/shard_map/all_gather | solution.py:471
  9.7 116.8 %all-gather.8.cloned.1.call-start = ((), (), s32[]{:S(2)}) async-start(), calls=%async_computation.6 | async-start | bytes 9437184 | tf_op jit(solution)/shard_map/all_gather | solution.py:475
  17.5 158.1 %all-gather.10.cloned.1.call-start = ((), (), s32[]{:S(2)}) async-start(), calls=%async_computation.7 | async-start | bytes 9437184 | tf_op jit(solution)/shard_map/all_gather | solution.py:476
  18.3 214.6 %all-gather.12.cloned.1.call-start = ((), (), s32[]{:S(2)}) async-start(), calls=%async_computation.8 | async-start | bytes 2359296 | tf_op jit(solution)/shard_map/all_gather | solution.py:477
  18.3 51.0 %collective-permute-start = (bf16[512,2048]{1,0:T(8,128)(2,1)}, bf16[512,2048]{1,0:T(8,128)(2,1)}, u32[]{:S(2)}, u32[]{:S(2)}) collective-permute-start(bf16[512,2048]{1,0:T(8,128)(2,1)} %fusion.7), channel_id=1, source_target_pairs={{0,1},{1,2},{2,3},{3,0},{4,5},{5,6},{6,7},{7,4},{8,9},{9,10},{10,1... | collective-permute-start | bytes 6291464 | tf_op jit(solution)/shard_map/ppermute | solution.py:364
  70.7 48.9 %collective-permute-start.1 = (bf16[512,2048]{1,0:T(8,128)(2,1)}, bf16[512,2048]{1,0:T(8,128)(2,1)}, u32[]{:S(2)}, u32[]{:S(2)}) collective-permute-start(bf16[512,2048]{1,0:T(8,128)(2,1)} %collective-permute-done), channel_id=1, source_target_pairs={{0,1},{1,2},{2,3},{3,0},{4,5},{5,6},{6,7},{7,4},{8,9},{9,10},{10,1... | collective-permute-start | bytes 6291464 | tf_op jit(solution)/shard_map/ppermute | solution.py:364
  70.7 431.8 %reduce-scatter.5.cloned.1.call-start = ((), (), s32[]{:S(2)}) async-start(), calls=%async_computation.9 | async-start | bytes 9437184 | tf_op jit(solution)/shard_map/reduce_scatter | solution.py:441
  119.6 48.9 %collective-permute-start.2 = (bf16[512,2048]{1,0:T(8,128)(2,1)}, bf16[512,2048]{1,0:T(8,128)(2,1)}, u32[]{:S(2)}, u32[]{:S(2)}) collective-permute-start(bf16[512,2048]{1,0:T(8,128)(2,1)} %collective-permute-done.1), channel_id=1, source_target_pairs={{0,1},{1,2},{2,3},{3,0},{4,5},{5,6},{6,7},{7,4},{8,9},{9,10},{10,1... | collective-permute-start | bytes 6291464 | tf_op jit(solution)/shard_map/ppermute | solution.py:364
  168.5 51.8 %collective-permute-start.4 = (bf16[512,2048]{1,0:T(8,128)(2,1)S(1)}, bf16[512,2048]{1,0:T(8,128)(2,1)}, u32[]{:S(2)}, u32[]{:S(2)}) collective-permute-start(bf16[512,2048]{1,0:T(8,128)(2,1)S(1)} %copy-done), channel_id=1, source_target_pairs={{1,0},{2,1},{3,2},{5,4},{6,5},{7,6},{9,8},{10,9},{11,10},{13,12},{... | collective-permute-start | bytes 6291464 | tf_op jit(solution)/shard_map/ppermute | solution.py:364
  169.8 50.5 %collective-permute-start.3 = (bf16[512,2048]{1,0:T(8,128)(2,1)S(1)}, bf16[512,2048]{1,0:T(8,128)(2,1)}, u32[]{:S(2)}, u32[]{:S(2)}) collective-permute-start(bf16[512,2048]{1,0:T(8,128)(2,1)S(1)} %copy-done), channel_id=1, source_target_pairs={{0,1},{1,2},{2,3},{4,5},{5,6},{6,7},{8,9},{9,10},{10,11},{12,13},{... | collective-permute-start | bytes 6291464 | tf_op jit(solution)/shard_map/ppermute | solution.py:364
  220.3 53.5 %collective-permute-start.5 = (bf16[512,2048]{1,0:T(8,128)(2,1)}, bf16[512,2048]{1,0:T(8,128)(2,1)}, u32[]{:S(2)}, u32[]{:S(2)}) collective-permute-start(bf16[512,2048]{1,0:T(8,128)(2,1)} %collective-permute-done.3), channel_id=1, source_target_pairs={{1,2},{2,3},{5,6},{6,7},{9,10},{10,11},{13,14},{14,15},{17,18},{18... | collective-permute-start | bytes 6291464 | tf_op jit(solution)/shard_map/ppermute | solution.py:364
  222.3 51.5 %collective-permute-start.6 = (bf16[512,2048]{1,0:T(8,128)(2,1)}, bf16[512,2048]{1,0:T(8,128)(2,1)}, u32[]{:S(2)}, u32[]{:S(2)}) collective-permute-start(bf16[512,2048]{1,0:T(8,128)(2,1)} %collective-permute-done.4), channel_id=1, source_target_pairs={{1,0},{2,1},{5,4},{6,5},{9,8},{10,9},{13,12},{14,13},{17,16},{18,1... | collective-permute-start | bytes 6291464 | tf_op jit(solution)/shard_map/ppermute | solution.py:364
  223.6 50.7 %collective-permute-start.7 = (bf16[512,2048]{1,0:T(8,128)(2,1)}, bf16[512,2048]{1,0:T(8,128)(2,1)}, u32[]{:S(2)}, u32[]{:S(2)}) collective-permute-start(bf16[512,2048]{1,0:T(8,128)(2,1)} %convolution_convert_fusion.7), channel_id=1, source_target_pairs={{0,1},{4,5},{8,9},{12,13},{16,17},{20,21},{24,25},{28,29}} | collective-permute-start | bytes 6291464 | tf_op jit(solution)/shard_map/ppermute | solution.py:364
  274.3 52.9 %collective-permute-start.9 = (bf16[512,2048]{1,0:T(8,128)(2,1)}, bf16[512,2048]{1,0:T(8,128)(2,1)S(1)}, u32[]{:S(2)}, u32[]{:S(2)}) collective-permute-start(bf16[512,2048]{1,0:T(8,128)(2,1)} %collective-permute-done.5), channel_id=1, source_target_pairs={{2,3},{6,7},{10,11},{14,15},{18,19},{22,23},{26,27},{30,31}} | collective-permute-start | bytes 6291464 | tf_op jit(solution)/shard_map/ppermute | solution.py:364
  275.2 52.0 %collective-permute-start.10 = (bf16[512,2048]{1,0:T(8,128)(2,1)}, bf16[512,2048]{1,0:T(8,128)(2,1)}, u32[]{:S(2)}, u32[]{:S(2)}) collective-permute-start(bf16[512,2048]{1,0:T(8,128)(2,1)} %collective-permute-done.6), channel_id=1, source_target_pairs={{1,0},{5,4},{9,8},{13,12},{17,16},{21,20},{25,24},{29,28}} | collective-permute-start | bytes 6291464 | tf_op jit(solution)/shard_map/ppermute | solution.py:364
  286.7 50.6 %collective-permute-start.11 = (bf16[512,2048]{1,0:T(8,128)(2,1)}, bf16[512,2048]{1,0:T(8,128)(2,1)}, u32[]{:S(2)}, u32[]{:S(2)}) collective-permute-start(bf16[512,2048]{1,0:T(8,128)(2,1)} %get-tuple-element.450), channel_id=1, source_target_pairs={{0,1},{1,2},{4,5},{5,6},{8,9},{9,10},{12,13},{13,14},{16,17},{17,1... | collective-permute-start | bytes 6291464 | tf_op jit(solution)/shard_map/ppermute | solution.py:364
  341.8 50.0 %collective-permute-start.14 = (bf16[512,2048]{1,0:T(8,128)(2,1)}, bf16[512,2048]{1,0:T(8,128)(2,1)}, u32[]{:S(2)}, u32[]{:S(2)}) collective-permute-start(bf16[512,2048]{1,0:T(8,128)(2,1)} %add_convert_fusion.6), channel_id=1, source_target_pairs={{1,0},{2,1},{3,2},{5,4},{6,5},{7,6},{9,8},{10,9},{11,10},{13,12},{... | collective-permute-start | bytes 6291464 | tf_op jit(solution)/shard_map/ppermute | solution.py:364
  347.5 49.9 %collective-permute-start.13 = (bf16[512,2048]{1,0:T(8,128)(2,1)}, bf16[512,2048]{1,0:T(8,128)(2,1)}, u32[]{:S(2)}, u32[]{:S(2)}) collective-permute-start(bf16[512,2048]{1,0:T(8,128)(2,1)} %add_convert_fusion.7), channel_id=1, source_target_pairs={{0,1},{1,2},{2,3},{4,5},{5,6},{6,7},{8,9},{9,10},{10,11},{12,13},{... | collective-permute-start | bytes 6291464 | tf_op jit(solution)/shard_map/ppermute | solution.py:364
  397.4 208.6 %reduce-scatter.7.cloned.1.call-start = ((), (), s32[]{:S(2)}) async-start(), calls=%async_computation.10 | async-start | bytes 2359296 | tf_op jit(solution)/shard_map/reduce_scatter | solution.py:441
  400.8 49.8 %collective-permute-start.15 = (bf16[512,2048]{1,0:T(8,128)(2,1)}, bf16[512,2048]{1,0:T(8,128)(2,1)S(1)}, u32[]{:S(2)}, u32[]{:S(2)}) collective-permute-start(bf16[512,2048]{1,0:T(8,128)(2,1)} %slice.67), channel_id=1, source_target_pairs={{0,1},{1,2},{2,3},{3,0},{4,5},{5,6},{6,7},{7,4},{8,9},{9,10},{10,1... | collective-permute-start | bytes 6291464 | tf_op jit(solution)/shard_map/ppermute | solution.py:364
  454.5 48.1 %collective-permute-start.16 = (bf16[512,2048]{1,0:T(8,128)(2,1)}, bf16[512,2048]{1,0:T(8,128)(2,1)}, u32[]{:S(2)}, u32[]{:S(2)}) collective-permute-start(bf16[512,2048]{1,0:T(8,128)(2,1)} %add_convert_fusion.5), channel_id=1, source_target_pairs={{0,1},{1,2},{2,3},{3,0},{4,5},{5,6},{6,7},{7,4},{8,9},{9,10},{10,1... | collective-permute-start | bytes 6291464 | tf_op jit(solution)/shard_map/ppermute | solution.py:364
  502.6 150.4 %reduce-scatter.9.cloned.1.call-start = ((), (), s32[]{:S(2)}) async-start(), calls=%async_computation.11 | async-start | bytes 7077888 | tf_op jit(solution)/shard_map/reduce_scatter | solution.py:441
  552.5 135.0 %reduce-scatter.11.cloned.1.call-start = ((), (), s32[]{:S(2)}) async-start(), calls=%async_computation.12 | async-start | bytes 9437184 | tf_op jit(solution)/shard_map/reduce_scatter | solution.py:441
  556.3 49.7 %collective-permute-start.18 = (bf16[512,2048]{1,0:T(8,128)(2,1)}, bf16[512,2048]{1,0:T(8,128)(2,1)S(1)}, u32[]{:S(2)}, u32[]{:S(2)}) collective-permute-start(bf16[512,2048]{1,0:T(8,128)(2,1)} %slice.74), channel_id=1, source_target_pairs={{0,1},{1,2},{2,3},{3,0},{4,5},{5,6},{6,7},{7,4},{8,9},{9,10},{10,1... | collective-permute-start | bytes 6291464 | tf_op jit(solution)/shard_map/ppermute | solution.py:364
  (72 other events, 1076.0 us)
Sparse Core Ops, SparseCore 0:
  10.5 49.5 all-gather.5
  62.0 54.3 all-gather.7
  118.3 55.9 all-gather.9
  176.0 28.1 all-gather.11
  397.5 74.7 reduce-scatter.4
  502.7 42.1 reduce-scatter.6
  552.6 59.6 reduce-scatter.8
  616.2 71.2 reduce-scatter.10

commit v6 on v5

--- a/solution.py
+++ b/solution.py
@@ -339,6 +339,23 @@
     )(block, weight, slope, *held)
 
 
+def columns_back_kernel(part_ref, out_ref):
+    for c in range(3):
+        out_ref[c] = part_ref[:, c * PAIR : (c + 1) * PAIR].astype(jnp.float32)
+
+
+def columns_back(part):
+    rows, width = part.shape
+    return pl.pallas_call(
+        columns_back_kernel,
+        grid=(width // (3 * PAIR),),
+        in_specs=[pl.BlockSpec((rows, 3 * PAIR), lambda p: (0, p))],
+        out_specs=pl.BlockSpec((3, rows, PAIR), lambda p: (0, 0, p)),
+        out_shape=jax.ShapeDtypeStruct((3, rows, width // 3), jnp.float32),
+        name="columns_back",
+    )(part)
+
+
 def gelu_and_slope(u):
     tanh_value = jnp.tanh(GELU_C * (u + 0.044715 * u * u * u))
     value = 0.5 * u * (1.0 + tanh_value)
@@ -563,8 +580,8 @@
         cot.step()
         mlp.step()
     attended = attention_forward(turned(projected), full_qbias, tables, 0, pairs)
-    ring, attended, slopes, hidden_act, sorted_qkv = together(
-        cot, mlp, after=(ring, attended, slopes, hidden_act, sorted_qkv)
+    ring, attended, slopes, hidden_act, sorted_qkv, cot.up[0] = together(
+        cot, mlp, after=(ring, attended, slopes, hidden_act, sorted_qkv, cot.up[0])
     )
     query, keys, values, context_low, logsum = attended
 
@@ -574,7 +591,10 @@
         context_back(k, cot.block(k))
         inner_back(k, cot.block(k))
     acts = jnp.concatenate(turned(hidden_act), axis=0)
-    attn_part = jnp.dot(context_low, full_dense, preferred_element_type=jnp.float32).astype(low)
+    attn_part = [
+        jnp.dot(rows, full_dense, preferred_element_type=jnp.float32).astype(low)
+        for rows in (context_low[:row_count], context_low[row_count:])
+    ]
     normed_low = jnp.concatenate(turned(ring), axis=0)
     grad_context, grad_pre, acts, slopes, attn_part, normed_low = together(
         cot, mlp, after=(grad_context, grad_pre, acts, slopes, attn_part, normed_low)
@@ -593,7 +613,7 @@
     )
     part_down = scatter_low(grad_down, "dp", 1)
 
-    attn = RingScatter([attn_part], row_count)
+    attn = RingScatter(attn_part, row_count)
     attn.step()
     grads = attention_backward(query, keys, values, turned(grad_context), logsum, tables, 0, half)
     inner_back(late[0], blocks[late[0]])
@@ -624,7 +644,7 @@
 
     attn.step()
     grad_qkv = contract_rows(normed_low, grad_proj).astype(low)
-    grad_parts = [return_normed(0, ways // 2)]
+    grad_parts = [return_normed(0, 1)]
     grad_parts, grad_qkv, pre_full, grad_proj, normed_low = together(
         attn, mlp, after=(grad_parts, grad_qkv, pre_full, grad_proj, normed_low)
     )
@@ -632,29 +652,30 @@
 
     last = RingScatter(grad_parts, row_count)
     last.step()
-    last.parts.append(return_normed(ways // 2, ways))
     grad_up = contract_rows(normed_low, pre_full).astype(low)
-    grad_up, pre_full, part_dense = together(
-        last, attn, mlp, after=(grad_up, pre_full, part_dense)
+    last.parts.append(return_normed(1, 2))
+    grad_up, pre_full, grad_proj, part_dense = together(
+        last, attn, mlp, after=(grad_up, pre_full, grad_proj, part_dense)
     )
     part_up = scatter_low(grad_up, "dp", 0)
+    last.parts.append(return_normed(2, ways))
     while last.k < ways - 2:
         last.step()
     grad_ubias = jnp.sum(pre_full, axis=0, dtype=jnp.float32)
-    part_down, part_dense = part_down.astype(jnp.float32), part_dense.astype(jnp.float32)
     attn_mine, mlp_mine = attn.total(), mlp.total()
     attn_mine, mlp_mine, grad_ubias, part_down, part_dense, part_qkv = together(
         last, after=(attn_mine, mlp_mine, grad_ubias, part_down, part_dense, part_qkv)
     )
-    part_qkv = part_qkv.astype(jnp.float32).reshape(-1, pairs, 3, PAIR)
-    part_qkv = part_qkv.transpose(2, 0, 1, 3).reshape(3, -1, pairs * PAIR)
+    part_qkv = columns_back(part_qkv)
+    part_down, part_dense = part_down.astype(jnp.float32), part_dense.astype(jnp.float32)
     last.step()
     output = (resid + attn_mine + mlp_mine + out_bias).astype(low)
     attn_square = jnp.sum(valid_mine * attn_mine * attn_mine)
     mlp_square = jnp.sum(valid_mine * mlp_mine * mlp_mine)
     part_up = part_up.astype(jnp.float32)
-    output, attn_square, mlp_square, part_up, part_qkv = together(
-        last, after=(output, attn_square, mlp_square, part_up, part_qkv)
+    output, attn_square, mlp_square, part_up, part_qkv, part_down, part_dense = together(
+        last,
+        after=(output, attn_square, mlp_square, part_up, part_qkv, part_down, part_dense),
     )
     grad_mine = last.total()
     scaled = grad_mine * norm_gain

time: 743 us -> 722 us (0.972)
  waiting for transfers between devices: 143 us -> 105 us
  matrix products: 234 us -> 247 us
  starting transfers between devices: 51.4 us -> 60.9 us
  local copies, waits for them, and re-layouts: 36.2 us -> 28.4 us
    ppermute x21, waiting for transfers between devices: 123 us -> 72 us  [shift(): return lax.ppermute(x, 'tensor', pairs)]
    reduce_scatter x4, waiting for transfers between devices: 19 us -> 29.7 us  [scatter_low(): lax.psum_scatter(part.astype(jnp.bfloat16), axis, scatter_dimension=dim,...]
    ppermute x21, starting transfers between devices: 47.7 us -> 56 us  [shift(): return lax.ppermute(x, 'tensor', pairs)]
    dot_general x8 -> x10, matrix products: 63 us -> 69.6 us  [contract_cols(): lax.dot_general(left, right, (((1,), (1,)), ((), ())), preferred_element_...]
  transfers between devices with their start and end apart: 30 -> 30, of which waited for: 12 -> 10; matrix products, arithmetic and copies ran while one was open for 48% -> 50% of each run, Pallas kernels for 18% -> 19%
where the time goes in v6:
time: 722 us; the launch traced here: 714 us
  matrix products  247 us (34%)
  Pallas kernels  135 us (19%)
  other arithmetic  106 us (15%)
  waiting for transfers between devices  105 us (15%)
  starting transfers between devices  60.9 us (8%)
  local copies, waits for them, and re-layouts  28.4 us (4%)
  between operations  16.6 us (2%)
  blocking collectives  14.6 us (2%)
    dot_general x4, matrix products, contract_rows(): lax.dot_general(left, right, (((0,), (0,)), ((), ())), preferred_element_...  72.4 us
    ppermute x21, waiting for transfers between devices, shift(): return lax.ppermute(x, 'tensor', pairs)  72 us
    dot_general x10, matrix products, contract_cols(): lax.dot_general(left, right, (((1,), (1,)), ((), ())), preferred_element_...  69.6 us
    pallas_call x2, Pallas kernels, attention_backward(): pl.pallas_call(kernel, grid_spec=pltpu.PrefetchScalarGridSpec(num_scalar_...  61.1 us
    ppermute x21, starting transfers between devices, shift(): return lax.ppermute(x, 'tensor', pairs)  56 us
    dot_general x4, matrix products, widen(): jnp.dot(ring[k], full_up, preferred_element_type=jnp.float32) + full_ubias  42.7 us
    pallas_call x1, Pallas kernels, attention_forward(): pl.pallas_call(kernel, grid_spec=pltpu.PrefetchScalarGridSpec(num_scalar_...  37.1 us
    pallas_call x4, Pallas kernels, hidden_back(): pl.pallas_call(hidden_back_kernel, grid=(hidden // tile,), in_specs=[pl.B...  33.6 us
  transfers between devices with their start and end apart: 30, of which 10 were waited for; matrix products, arithmetic and copies ran while one was open for 50% of the time, Pallas kernels for 19%

profile of v6, /device:TPU:0, one launch (start us, length us, event | category | flops | bytes accessed | tf_op | source)
XLA Modules:
  0.0 714.4 jit_solution(16982450711886312457)
XLA Ops:
  24.9 14.6 %all-reduce = bf16[3584]{0:T(1024)(128)(2,1)S(1)} all-reduce(bf16[3584]{0:T(1024)(128)(2,1)S(1)} %dynamic-update-slice), channel_id=2, replica_groups=mesh['dp'=8,'tensor'=4] {'dp'}, use_global_device_ids=true, to_apply=%add | all-reduce | flops 3584 | bytes 14336
  55.4 14.0 %collective-permute-done = bf16[512,2048]{1,0:T(8,128)(2,1)} collective-permute-done((bf16[512,2048]{1,0:T(8,128)(2,1)}, bf16[512,2048]{1,0:T(8,128)(2,1)}, u32[]{:S(2)}, u32[]{:S(2)}) %collective-permute-start) | collective-permute-done | bytes 2097184 | tf_op jit(solution)/shard_map/ppermute | solution.py:381
  74.6 8.5 %fusion.67.refs_2_ = f32[512,1536]{1,0:T(8,128)} fusion(bf16[512,2048]{1,0:T(8,128)(2,1)} %collective-permute-done, bf16[2048,1536]{0,1:T(8,128)(2,1)S(1)} %bitcast.77), kind=kOutput, calls=%fused_computation.156 | convolution fusion | flops 3221225472 | bytes 11534336 | tf_op jit(solution)/shard_map/dot_general | solution.py:533
  88.2 31.8 %collective-permute-done.1 = bf16[512,2048]{1,0:T(8,128)(2,1)} collective-permute-done((bf16[512,2048]{1,0:T(8,128)(2,1)}, bf16[512,2048]{1,0:T(8,128)(2,1)}, u32[]{:S(2)}, u32[]{:S(2)}) %collective-permute-start.1) | collective-permute-done | bytes 2097184 | tf_op jit(solution)/shard_map/ppermute | solution.py:381
  142.8 16.4 %multiply_convert_fusion.1 = (bf16[512,2048]{1,0:T(8,128)(2,1)}, f32[512,2048]{1,0:T(8,128)}, f32[512,2048]{1,0:T(8,128)}, bf16[512,2048]{1,0:T(8,128)(2,1)}, f32[512,2048]{1,0:T(8,128)}, /*index=5*/bf16[512,2048]{1,0:T(8,128)(2,1)}) fusion(f32[2048]{0:T(1024)S(1)} %bitcast.94, f32[512,2048]{1,0:T(8,128)} %fusion.70, f32[512,2048]{1,0:T(8,128)S(1)} %fusion.69, ...), kind=kOutput, calls=%fused_computation.85 | convolution fusion | flops 4357881856 | bytes 37756928 | tf_op jit(solution)/shard_map/dot_general | solution.py:536
  159.2 9.0 %collective-permute-done.2 = bf16[512,2048]{1,0:T(8,128)(2,1)} collective-permute-done((bf16[512,2048]{1,0:T(8,128)(2,1)}, bf16[512,2048]{1,0:T(8,128)(2,1)}, u32[]{:S(2)}, u32[]{:S(2)}) %collective-permute-start.2) | collective-permute-done | bytes 2097184 | tf_op jit(solution)/shard_map/ppermute | solution.py:381
  172.4 10.5 %multiply_convert_fusion = (bf16[512,2048]{1,0:T(8,128)(2,1)}, f32[512,2048]{1,0:T(8,128)}) fusion(f32[2048]{0:T(1024)S(1)} %bitcast.95, bf16[512,2048]{1,0:T(8,128)(2,1)} %collective-permute-done.2, bf16[2048,2048]{1,0:T(8,128)(2,1)S(1)} %copy-done.50), kind=kOutput, calls=%fused_computation.84 | convolution fusion | flops 4315938816 | bytes 16785408 | tf_op jit(solution)/shard_map/dot_general | solution.py:536
  182.9 10.0 %convolution_convert_fusion.6 = bf16[512,2048]{1,0:T(8,128)(2,1)} fusion(bf16[512,2048]{1,0:T(8,128)(2,1)} %get-tuple-element.276, bf16[2048,2048]{1,0:T(8,128)(2,1)} %all-gather.10.cloned.1.call-done.weight_ref), kind=kOutput, calls=%fused_computation.95 | convolution fusion | flops 4296015872 | bytes 12582912 | tf_op jit(solution)/shard_map/dot_general | solution.py:541
  232.9 37.1 %attend.1 = (bf16[2048,512]{1,0:T(8,128)(2,1)}, bf16[2048,512]{1,0:T(8,128)(2,1)}, bf16[2048,512]{1,0:T(8,128)(2,1)}, bf16[2048,512]{1,0:T(8,128)(2,1)}, f32[4,2,2048]{2,1,0:T(2,128)S(1)}) custom-call(s32[8]{0:T(128)S(1)} %get-tuple-element.238.refs_0_, s32[8]{0:T(128)S(1)} %get-tuple-element.239.refs_1_, f32[512,1536]{1,0:T(8,128)} %fusion.67.refs_2_, ...), custom_call_target="tpu_custom_call" | custom-call | tf_op jit(solution)/shard_map/attend/pallas_call | solution.py:157
  286.8 8.4 %hidden_back.4.refs_0_ = bf16[2048,2048]{1,0:T(8,128)(2,1)} custom-call(bf16[512,2048]{1,0:T(8,128)(2,1)S(1)} %copy-done, bf16[2048,2048]{1,0:T(8,128)(2,1)} %all-gather.10.cloned.1.call-done.weight_ref, f32[512,2048]{1,0:T(8,128)S(1)} %copy-done.14), custom_call_target="tpu_custom_call" | custom-call | flops 4294967296 | bytes 8388608 | tf_op jit(solution)/shard_map/hidden_back/pallas_call | solution.py:320
  306.9 8.3 %hidden_back.5.refs_0_ = bf16[2048,2048]{1,0:T(8,128)(2,1)} custom-call(bf16[512,2048]{1,0:T(8,128)(2,1)S(1)} %copy-done.4, bf16[2048,2048]{1,0:T(8,128)(2,1)} %all-gather.10.cloned.1.call-done.weight_ref, f32[512,2048]{1,0:T(8,128)S(1)} %copy-done.13, bf16[2048,2048]{1,0:T(8,128)(2,1)} %hidden_back.4.refs_0_), custom_call_target="tpu_custom_call", output_to_operand_aliasing={{}: (3, {})} | custom-call | flops 4294967296 | bytes 8388608 | tf_op jit(solution)/shard_map/hidden_back/pallas_call | solution.py:320
  361.3 19.8 %convolution_convert_fusion.1 = bf16[2048,2048]{1,0:T(8,128)(2,1)} fusion(bf16[2048,2048]{1,0:T(8,128)(2,1)S(1)} %pad_maximum_fusion, bf16[512,2048]{1,0:T(8,128)(2,1)S(1)} %copy-done, bf16[512,2048]{1,0:T(8,128)(2,1)S(1)} %broadcast_select_fusion.block_ref, bf16[512,2048]{1,0:T(8,128)(2,1)S(1)} %copy-done.4, ...), kind=kOutput, calls=%fused_computation.12 | convolution fusion | flops 17217617920 | bytes 25165824 | tf_op jit(solution)/shard_map/dot_general | solution.py:369
  398.1 30.9 %attend_back.2 = (bf16[2048,1536]{1,0:T(8,128)(2,1)}, f32[3,1,512]{2,1,0:T(1,128)S(1)}) custom-call(s32[8]{0:T(128)S(1)} %get-tuple-element.238.refs_0_, s32[8]{0:T(128)S(1)} %get-tuple-element.239.refs_1_, bf16[512,512]{1,0:T(8,128)(2,1)S(1)} %copy-done.18, bf16[512,512]{1,0:T(8,128)(2,1)S(1)} %copy-done.16, bf16[512,512]{1,0:T(8,128)(2,1)S(1)} %copy-done.17, ...), custom_call_target="tpu_custom_call" | custom-call | tf_op jit(solution)/shard_map/attend_back/pallas_call | solution.py:279
  429.0 8.5 %hidden_back.6.refs_0_ = bf16[2048,2048]{1,0:T(8,128)(2,1)} custom-call(bf16[512,2048]{1,0:T(8,128)(2,1)S(1)} %copy-done.6, bf16[2048,2048]{1,0:T(8,128)(2,1)} %all-gather.10.cloned.1.call-done.weight_ref, f32[512,2048]{1,0:T(8,128)S(1)} %copy-done.12, bf16[2048,2048]{1,0:T(8,128)(2,1)} %hidden_back.5.refs_0_), custom_call_target="tpu_custom_call", output_to_operand_aliasing={{}: (3, {})} | custom-call | flops 4294967296 | bytes 8388608 | tf_op jit(solution)/shard_map/hidden_back/pallas_call | solution.py:320
  445.5 30.2 %attend_back.3 = (bf16[2048,1536]{1,0:T(8,128)(2,1)}, f32[3,1,512]{2,1,0:T(1,128)S(1)}) custom-call(s32[8]{0:T(128)S(1)} %get-tuple-element.238.refs_0_, s32[8]{0:T(128)S(1)} %get-tuple-element.239.refs_1_, bf16[512,512]{1,0:T(8,128)(2,1)S(1)} %copy-done.18, bf16[512,512]{1,0:T(8,128)(2,1)S(1)} %copy-done.16, ...), custom_call_target="tpu_custom_call", output_to_operand_aliasing={{0}: (14, {}), {1}: (15, {})} | custom-call | tf_op jit(solution)/shard_map/attend_back/pallas_call | solution.py:279
  475.7 8.4 %hidden_back.7 = bf16[2048,2048]{1,0:T(8,128)(2,1)} custom-call(bf16[512,2048]{1,0:T(8,128)(2,1)S(1)} %copy-done.3, bf16[2048,2048]{1,0:T(8,128)(2,1)} %all-gather.10.cloned.1.call-done.weight_ref, f32[512,2048]{1,0:T(8,128)S(1)} %copy-done.11, bf16[2048,2048]{1,0:T(8,128)(2,1)} %hidden_back.6.refs_0_), custom_call_target="tpu_custom_call", output_to_operand_aliasing={{}: (3, {})} | custom-call | flops 4294967296 | bytes 8388608 | tf_op jit(solution)/shard_map/hidden_back/pallas_call | solution.py:320
  484.2 9.3 %convolution_convert_fusion.4 = bf16[512,2048]{1,0:T(8,128)(2,1)} fusion(bf16[2048,512]{1,0:T(8,128)(2,1)S(1)} %copy-done.52, bf16[2048,2048]{1,0:T(8,128)(2,1)} %pad_maximum_fusion.2), kind=kOutput, calls=%fused_computation.93 | convolution fusion | flops 4296015872 | bytes 12582912 | tf_op jit(solution)/shard_map/dot_general | solution.py:369
  499.0 19.2 %convolution_convert_fusion.3 = bf16[2048,1536]{1,0:T(8,128)(2,1)} fusion(bf16[2048,2048]{1,0:T(8,128)(2,1)} %pad_maximum_fusion.1, bf16[2048,1536]{1,0:T(8,128)(2,1)} %get-tuple-element.361), kind=kOutput, calls=%fused_computation.14 | convolution fusion | flops 12888047616 | bytes 20971520 | tf_op jit(solution)/shard_map/dot_general | solution.py:369
  524.2 10.0 %add_convert_fusion.4 = bf16[512,2048]{1,0:T(8,128)(2,1)} fusion(f32[512,2048]{1,0:T(8,128)S(1)} %fusion.55, bf16[2048,2048]{1,0:T(8,128)(2,1)} %all-gather.8.cloned.1.call-done, bf16[2048,2048]{1,0:T(8,128)(2,1)} %hidden_back.7), kind=kOutput, calls=%fused_computation.79 | convolution fusion | flops 4297064448 | bytes 16777216 | tf_op jit(solution)/shard_map/dot_general | solution.py:375
  544.5 24.2 %convolution_convert_fusion = bf16[2048,2048]{1,0:T(8,128)(2,1)} fusion(bf16[2048,2048]{1,0:T(8,128)(2,1)} %pad_maximum_fusion.1, bf16[2048,2048]{1,0:T(8,128)(2,1)} %hidden_back.7), kind=kOutput, calls=%fused_computation.11 | convolution fusion | flops 17184063488 | bytes 25165824 | tf_op jit(solution)/shard_map/dot_general | solution.py:369
  574.7 10.0 %add_convert_fusion.3 = bf16[512,2048]{1,0:T(8,128)(2,1)} fusion(f32[512,2048]{1,0:T(8,128)S(1)} %fusion.53, bf16[2048,2048]{1,0:T(8,128)(2,1)} %all-gather.8.cloned.1.call-done, bf16[2048,2048]{1,0:T(8,128)(2,1)} %hidden_back.7), kind=kOutput, calls=%fused_computation.78 | convolution fusion | flops 4297064448 | bytes 16777216 | tf_op jit(solution)/shard_map/dot_general | solution.py:375
  606.0 11.0 %fusion.49 = f32[1024,2048]{1,0:T(8,128)} fusion(bf16[2048,1536]{0,1:T(8,128)(2,1)} %bitcast.82, bf16[2048,1536]{1,0:T(8,128)(2,1)S(1)} %bitcast.76), kind=kOutput, calls=%fused_computation.91 | convolution fusion | flops 6442450944 | bytes 17825792 | tf_op jit(solution)/shard_map/dot_general | solution.py:375
  617.0 16.5 %add_convert_fusion = bf16[1024,2048]{1,0:T(8,128)(2,1)} fusion(f32[1024,2048]{1,0:T(8,128)} %fusion.49, bf16[2048,2048]{1,0:T(8,128)(2,1)} %all-gather.8.cloned.1.call-done, bf16[2048,2048]{1,0:T(8,128)(2,1)S(1)} %bitcast.74), kind=kOutput, calls=%fused_computation.5 | convolution fusion | flops 8594128896 | bytes 25165824 | tf_op jit(solution)/shard_map/dot_general | solution.py:375
  651.2 29.6 %reduce-scatter.11.cloned.1.call-done = bf16[256,2048]{1,0:T(8,128)(2,1)} async-done(((bf16[2048,2048]{1,0:T(8,128)(2,1)}), bf16[256,2048]{1,0:T(8,128)(2,1)}) %reduce-scatter.11.cloned.1.call-update) | async-done | bytes 1048592 | tf_op jit(solution)/shard_map/reduce_scatter | solution.py:458
  (298 shorter events, 301.6 us)
Async XLA Ops:
  7.2 63.9 %all-gather.6.cloned.1.call-start = ((), (), s32[]{:S(2)}) async-start(), calls=%async_computation.5 | async-start | bytes 7077888 | tf_op jit(solution)/shard_map/all_gather | solution.py:488
  9.7 117.3 %all-gather.8.cloned.1.call-start = ((), (), s32[]{:S(2)}) async-start(), calls=%async_computation.6 | async-start | bytes 9437184 | tf_op jit(solution)/shard_map/all_gather | solution.py:492
  17.5 165.4 %all-gather.10.cloned.1.call-start = ((), (), s32[]{:S(2)}) async-start(), calls=%async_computation.7 | async-start | bytes 9437184 | tf_op jit(solution)/shard_map/all_gather | solution.py:493
  18.3 280.1 %all-gather.12.cloned.1.call-start = ((), (), s32[]{:S(2)}) async-start(), calls=%async_computation.8 | async-start | bytes 2359296 | tf_op jit(solution)/shard_map/all_gather | solution.py:494
  18.3 51.0 %collective-permute-start = (bf16[512,2048]{1,0:T(8,128)(2,1)}, bf16[512,2048]{1,0:T(8,128)(2,1)}, u32[]{:S(2)}, u32[]{:S(2)}) collective-permute-start(bf16[512,2048]{1,0:T(8,128)(2,1)} %fusion.7), channel_id=1, source_target_pairs={{0,1},{1,2},{2,3},{3,0},{4,5},{5,6},{6,7},{7,4},{8,9},{9,10},{10,1... | collective-permute-start | bytes 6291464 | tf_op jit(solution)/shard_map/ppermute | solution.py:381
  70.7 49.4 %collective-permute-start.1 = (bf16[512,2048]{1,0:T(8,128)(2,1)}, bf16[512,2048]{1,0:T(8,128)(2,1)}, u32[]{:S(2)}, u32[]{:S(2)}) collective-permute-start(bf16[512,2048]{1,0:T(8,128)(2,1)} %collective-permute-done), channel_id=1, source_target_pairs={{0,1},{1,2},{2,3},{3,0},{4,5},{5,6},{6,7},{7,4},{8,9},{9,10},{10,1... | collective-permute-start | bytes 6291464 | tf_op jit(solution)/shard_map/ppermute | solution.py:381
  120.0 48.2 %collective-permute-start.2 = (bf16[512,2048]{1,0:T(8,128)(2,1)}, bf16[512,2048]{1,0:T(8,128)(2,1)}, u32[]{:S(2)}, u32[]{:S(2)}) collective-permute-start(bf16[512,2048]{1,0:T(8,128)(2,1)} %collective-permute-done.1), channel_id=1, source_target_pairs={{0,1},{1,2},{2,3},{3,0},{4,5},{5,6},{6,7},{7,4},{8,9},{9,10},{10,1... | collective-permute-start | bytes 6291464 | tf_op jit(solution)/shard_map/ppermute | solution.py:381
  168.2 49.4 %collective-permute-start.3 = (bf16[512,2048]{1,0:T(8,128)(2,1)S(1)}, bf16[512,2048]{1,0:T(8,128)(2,1)}, u32[]{:S(2)}, u32[]{:S(2)}) collective-permute-start(bf16[512,2048]{1,0:T(8,128)(2,1)S(1)} %copy-done), channel_id=1, source_target_pairs={{0,1},{1,2},{2,3},{4,5},{5,6},{6,7},{8,9},{9,10},{10,11},{12,13},{... | collective-permute-start | bytes 6291464 | tf_op jit(solution)/shard_map/ppermute | solution.py:381
  170.9 47.0 %collective-permute-start.4 = (bf16[512,2048]{1,0:T(8,128)(2,1)S(1)}, bf16[512,2048]{1,0:T(8,128)(2,1)}, u32[]{:S(2)}, u32[]{:S(2)}) collective-permute-start(bf16[512,2048]{1,0:T(8,128)(2,1)S(1)} %copy-done), channel_id=1, source_target_pairs={{1,0},{2,1},{3,2},{5,4},{6,5},{7,6},{9,8},{10,9},{11,10},{13,12},{... | collective-permute-start | bytes 6291464 | tf_op jit(solution)/shard_map/ppermute | solution.py:381
  217.9 52.2 %collective-permute-start.5 = (bf16[512,2048]{1,0:T(8,128)(2,1)}, bf16[512,2048]{1,0:T(8,128)(2,1)}, u32[]{:S(2)}, u32[]{:S(2)}) collective-permute-start(bf16[512,2048]{1,0:T(8,128)(2,1)} %collective-permute-done.3), channel_id=1, source_target_pairs={{1,2},{2,3},{5,6},{6,7},{9,10},{10,11},{13,14},{14,15},{17,18},{18... | collective-permute-start | bytes 6291464 | tf_op jit(solution)/shard_map/ppermute | solution.py:381
  219.9 50.2 %collective-permute-start.6 = (bf16[512,2048]{1,0:T(8,128)(2,1)}, bf16[512,2048]{1,0:T(8,128)(2,1)}, u32[]{:S(2)}, u32[]{:S(2)}) collective-permute-start(bf16[512,2048]{1,0:T(8,128)(2,1)} %collective-permute-done.4), channel_id=1, source_target_pairs={{1,0},{2,1},{5,4},{6,5},{9,8},{10,9},{13,12},{14,13},{17,16},{18,1... | collective-permute-start | bytes 6291464 | tf_op jit(solution)/shard_map/ppermute | solution.py:381
  221.2 48.9 %collective-permute-start.7 = (bf16[512,2048]{1,0:T(8,128)(2,1)}, bf16[512,2048]{1,0:T(8,128)(2,1)}, u32[]{:S(2)}, u32[]{:S(2)}) collective-permute-start(bf16[512,2048]{1,0:T(8,128)(2,1)} %convolution_convert_fusion.8), channel_id=1, source_target_pairs={{0,1},{4,5},{8,9},{12,13},{16,17},{20,21},{24,25},{28,29}} | collective-permute-start | bytes 6291464 | tf_op jit(solution)/shard_map/ppermute | solution.py:381
  230.1 263.4 %reduce-scatter.5.cloned.1.call-start = ((), (), s32[]{:S(2)}) async-start(), calls=%async_computation.9 | async-start | bytes 9437184 | tf_op jit(solution)/shard_map/reduce_scatter | solution.py:458
  276.0 54.0 %collective-permute-start.11 = (bf16[512,2048]{1,0:T(8,128)(2,1)}, bf16[512,2048]{1,0:T(8,128)(2,1)}, u32[]{:S(2)}, u32[]{:S(2)}) collective-permute-start(bf16[512,2048]{1,0:T(8,128)(2,1)} %get-tuple-element.412), channel_id=1, source_target_pairs={{0,1},{1,2},{4,5},{5,6},{8,9},{9,10},{12,13},{13,14},{16,17},{17,1... | collective-permute-start | bytes 6291464 | tf_op jit(solution)/shard_map/ppermute | solution.py:381
  281.6 48.5 %collective-permute-start.12 = (bf16[512,2048]{1,0:T(8,128)(2,1)}, bf16[512,2048]{1,0:T(8,128)(2,1)}, u32[]{:S(2)}, u32[]{:S(2)}) collective-permute-start(bf16[512,2048]{1,0:T(8,128)(2,1)} %get-tuple-element.411), channel_id=1, source_target_pairs={{2,1},{3,2},{6,5},{7,6},{10,9},{11,10},{14,13},{15,14},{18,17},{19... | collective-permute-start | bytes 6291464 | tf_op jit(solution)/shard_map/ppermute | solution.py:381
  283.5 46.5 %collective-permute-start.10 = (bf16[512,2048]{1,0:T(8,128)(2,1)}, bf16[512,2048]{1,0:T(8,128)(2,1)}, u32[]{:S(2)}, u32[]{:S(2)}) collective-permute-start(bf16[512,2048]{1,0:T(8,128)(2,1)} %collective-permute-done.6), channel_id=1, source_target_pairs={{1,0},{5,4},{9,8},{13,12},{17,16},{21,20},{25,24},{29,28}} | collective-permute-start | bytes 6291464 | tf_op jit(solution)/shard_map/ppermute | solution.py:381
  334.5 48.3 %collective-permute-start.14 = (bf16[512,2048]{1,0:T(8,128)(2,1)}, bf16[512,2048]{1,0:T(8,128)(2,1)}, u32[]{:S(2)}, u32[]{:S(2)}) collective-permute-start(bf16[512,2048]{1,0:T(8,128)(2,1)} %add_convert_fusion.7), channel_id=1, source_target_pairs={{1,0},{2,1},{3,2},{5,4},{6,5},{7,6},{9,8},{10,9},{11,10},{13,12},{... | collective-permute-start | bytes 6291464 | tf_op jit(solution)/shard_map/ppermute | solution.py:381
  340.3 48.9 %collective-permute-start.13 = (bf16[512,2048]{1,0:T(8,128)(2,1)}, bf16[512,2048]{1,0:T(8,128)(2,1)}, u32[]{:S(2)}, u32[]{:S(2)}) collective-permute-start(bf16[512,2048]{1,0:T(8,128)(2,1)} %add_convert_fusion.8), channel_id=1, source_target_pairs={{0,1},{1,2},{2,3},{4,5},{5,6},{6,7},{8,9},{9,10},{10,11},{12,13},{... | collective-permute-start | bytes 6291464 | tf_op jit(solution)/shard_map/ppermute | solution.py:381
  389.2 195.5 %reduce-scatter.7.cloned.1.call-start = ((), (), s32[]{:S(2)}) async-start(), calls=%async_computation.10 | async-start | bytes 2359296 | tf_op jit(solution)/shard_map/reduce_scatter | solution.py:458
  389.3 48.3 %collective-permute-start.15 = (bf16[512,2048]{1,0:T(8,128)(2,1)}, bf16[512,2048]{1,0:T(8,128)(2,1)S(1)}, u32[]{:S(2)}, u32[]{:S(2)}) collective-permute-start(bf16[512,2048]{1,0:T(8,128)(2,1)} %convolution_convert_fusion.5), channel_id=1, source_target_pairs={{0,1},{1,2},{2,3},{3,0},{4,5},{5,6},{6,7},{7,4},{8,9},{9,10},{10,1... | collective-permute-start | bytes 6291464 | tf_op jit(solution)/shard_map/ppermute | solution.py:381
  441.4 52.0 %collective-permute-start.16 = (bf16[512,2048]{1,0:T(8,128)(2,1)}, bf16[512,2048]{1,0:T(8,128)(2,1)}, u32[]{:S(2)}, u32[]{:S(2)}) collective-permute-start(bf16[512,2048]{1,0:T(8,128)(2,1)} %add_convert_fusion.6), channel_id=1, source_target_pairs={{0,1},{1,2},{2,3},{3,0},{4,5},{5,6},{6,7},{7,4},{8,9},{9,10},{10,1... | collective-permute-start | bytes 6291464 | tf_op jit(solution)/shard_map/ppermute | solution.py:381
  498.9 134.6 %reduce-scatter.9.cloned.1.call-start = ((), (), s32[]{:S(2)}) async-start(), calls=%async_computation.11 | async-start | bytes 7077888 | tf_op jit(solution)/shard_map/reduce_scatter | solution.py:458
  542.1 138.8 %reduce-scatter.11.cloned.1.call-start = ((), (), s32[]{:S(2)}) async-start(), calls=%async_computation.12 | async-start | bytes 9437184 | tf_op jit(solution)/shard_map/reduce_scatter | solution.py:458
  637.8 46.0 %collective-permute-start.20 = (bf16[512,2048]{1,0:T(8,128)(2,1)}, bf16[512,2048]{1,0:T(8,128)(2,1)}, u32[]{:S(2)}, u32[]{:S(2)}) collective-permute-start(bf16[512,2048]{1,0:T(8,128)(2,1)} %add_convert_fusion.1), channel_id=1, source_target_pairs={{0,1},{1,2},{2,3},{3,0},{4,5},{5,6},{6,7},{7,4},{8,9},{9,10},{10,1... | collective-permute-start | bytes 6291464 | tf_op jit(solution)/shard_map/ppermute | solution.py:381
  (69 other events, 980.0 us)
Sparse Core Ops, SparseCore 0:
  10.5 49.5 all-gather.5
  62.0 54.3 all-gather.7
  118.3 55.9 all-gather.9
  230.2 29.5 all-gather.11
  389.3 77.5 reduce-scatter.4
  499.0 41.4 reduce-scatter.6
  543.9 61.7 reduce-scatter.8
  609.5 71.2 reduce-scatter.10

commit v7 on v6

--- a/solution.py
+++ b/solution.py
@@ -339,6 +339,67 @@
     )(block, weight, slope, *held)
 
 
+def normalize_kernel(x_ref, gain_ref, shift_ref, out_ref):
+    x = x_ref[...].astype(jnp.float32)
+    centered = x - jnp.mean(x, axis=-1, keepdims=True)
+    inverse = lax.rsqrt(jnp.mean(centered * centered, axis=-1, keepdims=True) + EPS)
+    out_ref[...] = (centered * inverse * gain_ref[...] + shift_ref[...]).astype(jnp.bfloat16)
+
+
+def normalize(x, gain, shift_in):
+    rows, width = x.shape
+    block = pl.BlockSpec((128, width), lambda i: (i, 0))
+    wide = pl.BlockSpec((1, width), lambda i: (0, 0))
+    return pl.pallas_call(
+        normalize_kernel,
+        grid=(rows // 128,),
+        in_specs=[block, wide, wide],
+        out_specs=block,
+        out_shape=jax.ShapeDtypeStruct((rows, width), jnp.bfloat16),
+        name="normalize",
+    )(x, gain[None, :], shift_in[None, :])
+
+
+def add_pair_kernel(a_ref, b_ref, c_ref, d_ref, ab_ref, cd_ref):
+    ab_ref[...] = (a_ref[...].astype(jnp.float32) + b_ref[...].astype(jnp.float32)).astype(
+        jnp.bfloat16
+    )
+    cd_ref[...] = (c_ref[...].astype(jnp.float32) + d_ref[...].astype(jnp.float32)).astype(
+        jnp.bfloat16
+    )
+
+
+def add_pair(a, b, c, d):
+    rows, width = a.shape
+    block = pl.BlockSpec((128, width), lambda i: (i, 0))
+    return pl.pallas_call(
+        add_pair_kernel,
+        grid=(rows // 128,),
+        in_specs=[block] * 4,
+        out_specs=[block] * 2,
+        out_shape=[jax.ShapeDtypeStruct((rows, width), jnp.bfloat16)] * 2,
+        name="add_pair",
+    )(a, b, c, d)
+
+
+def columns_sorted_kernel(weight_ref, out_ref):
+    for c in range(3):
+        out_ref[:, c * PAIR : (c + 1) * PAIR] = weight_ref[c]
+
+
+def columns_sorted(weight):
+    _, rows, width = weight.shape
+    tile = min(512, rows)
+    return pl.pallas_call(
+        columns_sorted_kernel,
+        grid=(rows // tile, width // PAIR),
+        in_specs=[pl.BlockSpec((3, tile, PAIR), lambda r, p: (0, r, p))],
+        out_specs=pl.BlockSpec((tile, 3 * PAIR), lambda r, p: (r, p)),
+        out_shape=jax.ShapeDtypeStruct((rows, 3 * width), weight.dtype),
+        name="columns_sorted",
+    )(weight)
+
+
 def columns_back_kernel(part_ref, out_ref):
     for c in range(3):
         out_ref[c] = part_ref[:, c * PAIR : (c + 1) * PAIR].astype(jnp.float32)
@@ -425,10 +486,9 @@
         n, k = lax.axis_size("tensor"), self.k
         mine_up, mine_down = self.parts[k], self.parts[n - k]
         if k > 1:
-            mine_up = mine_up.astype(jnp.float32) + self.up.astype(jnp.float32)
-            mine_down = mine_down.astype(jnp.float32) + self.down.astype(jnp.float32)
-        self.up = shift(mine_up.astype(jnp.bfloat16), [(i, i + 1) for i in range(k)])
-        self.down = shift(mine_down.astype(jnp.bfloat16), [(i, i - 1) for i in range(n - k, n)])
+            mine_up, mine_down = add_pair(mine_up, self.up, mine_down, self.down)
+        self.up = shift(mine_up, [(i, i + 1) for i in range(k)])
+        self.down = shift(mine_down, [(i, i - 1) for i in range(n - k, n)])
         self.k = k + 1
 
     def total(self):
@@ -484,7 +544,7 @@
     centered = resid - row_mean
     inverse = lax.rsqrt(jnp.mean(centered * centered, axis=-1, keepdims=True) + EPS)
     normed = centered * inverse
-    normed_mine = (normed * norm_gain + norm_shift).astype(low)
+    normed_mine = normalize(tokens, norm_gain, norm_shift)
     full_qkv = lax.all_gather(qkv_weight, "dp", axis=1, tiled=True)
     normed_mine, up_weight, down_weight, dense_weight = lax.optimization_barrier(
         (normed_mine, up_weight, down_weight, dense_weight)
@@ -520,8 +580,7 @@
         (ring[1], cotangent, tables, full_qbias, full_ubias, cot_columns, resid_square)
     )
     pairs = qkv_weight.shape[2] // PAIR
-    sorted_qkv = full_qkv.reshape(3, model_width, pairs, PAIR).transpose(1, 2, 0, 3)
-    sorted_qkv = sorted_qkv.reshape(model_width, 3 * pairs * PAIR)
+    sorted_qkv = columns_sorted(full_qkv)
     half = max(1, pairs // 2)
     projected, slopes, hidden_act, mlp_parts = ([None] * ways for _ in range(4))
     grad_context, grad_pre = [None] * ways, [None]
@@ -616,10 +675,11 @@
     attn = RingScatter(attn_part, row_count)
     attn.step()
     grads = attention_backward(query, keys, values, turned(grad_context), logsum, tables, 0, half)
-    inner_back(late[0], blocks[late[0]])
-    grads, grad_context, grad_full, context_low, grad_pre, normed_low = together(
-        attn, mlp, after=(grads, grad_context, grad_full, context_low, grad_pre, normed_low)
-    )
+    grad_dense = contract_rows(context_low, grad_full).astype(low)
+    grads, grad_context, grad_dense, grad_pre, normed_low, blocks, slopes = together(
+        attn, mlp, after=(grads, grad_context, grad_dense, grad_pre, normed_low, blocks, slopes)
+    )
+    part_dense = scatter_low(grad_dense, "dp", 1)
 
     while attn.k < ways - 2:
         attn.step()
@@ -627,13 +687,11 @@
         grads = attention_backward(
             query, keys, values, turned(grad_context), logsum, tables, half, pairs - half, held=grads
         )
-    for k in late[1:]:
+    for k in late:
         inner_back(k, blocks[k])
-    grad_dense = contract_rows(context_low, grad_full).astype(low)
-    grads, grad_dense, grad_pre, normed_low, part_down = together(
-        attn, mlp, after=(grads, grad_dense, grad_pre, normed_low, part_down)
-    )
-    part_dense = scatter_low(grad_dense, "dp", 1)
+    grads, grad_pre, normed_low, part_down = together(
+        attn, mlp, after=(grads, grad_pre, normed_low, part_down)
+    )
     grad_proj, grad_qbias = grads[0], grads[1][:, 0, :]
     [pre_full] = grad_pre
 
@@ -643,28 +701,26 @@
         return part.astype(low)
 
     attn.step()
-    grad_qkv = contract_rows(normed_low, grad_proj).astype(low)
+    grad_up = contract_rows(normed_low, pre_full).astype(low)
     grad_parts = [return_normed(0, 1)]
-    grad_parts, grad_qkv, pre_full, grad_proj, normed_low = together(
-        attn, mlp, after=(grad_parts, grad_qkv, pre_full, grad_proj, normed_low)
-    )
-    part_qkv = scatter_low(grad_qkv, "dp", 0)
+    grad_parts, grad_up, pre_full, grad_proj, normed_low, part_dense = together(
+        attn, mlp, after=(grad_parts, grad_up, pre_full, grad_proj, normed_low, part_dense)
+    )
+    part_up = scatter_low(grad_up, "dp", 0)
 
     last = RingScatter(grad_parts, row_count)
     last.step()
-    grad_up = contract_rows(normed_low, pre_full).astype(low)
+    grad_qkv = contract_rows(normed_low, grad_proj).astype(low)
     last.parts.append(return_normed(1, 2))
-    grad_up, pre_full, grad_proj, part_dense = together(
-        last, attn, mlp, after=(grad_up, pre_full, grad_proj, part_dense)
-    )
-    part_up = scatter_low(grad_up, "dp", 0)
+    grad_qkv, pre_full, grad_proj = together(last, attn, mlp, after=(grad_qkv, pre_full, grad_proj))
+    part_qkv = scatter_low(grad_qkv, "dp", 0)
     last.parts.append(return_normed(2, ways))
     while last.k < ways - 2:
         last.step()
     grad_ubias = jnp.sum(pre_full, axis=0, dtype=jnp.float32)
     attn_mine, mlp_mine = attn.total(), mlp.total()
-    attn_mine, mlp_mine, grad_ubias, part_down, part_dense, part_qkv = together(
-        last, after=(attn_mine, mlp_mine, grad_ubias, part_down, part_dense, part_qkv)
+    attn_mine, mlp_mine, grad_ubias, part_down, part_dense, part_up = together(
+        last, after=(attn_mine, mlp_mine, grad_ubias, part_down, part_dense, part_up)
     )
     part_qkv = columns_back(part_qkv)
     part_down, part_dense = part_down.astype(jnp.float32), part_dense.astype(jnp.float32)

time: 722 us -> 788 us (1.091)
  starting transfers between devices: 60.9 us -> 93.2 us
  Pallas kernels: 135 us -> 164 us
  other arithmetic: 106 us -> 90.9 us
  waiting for transfers between devices: 105 us -> 117 us
    ppermute x21, starting transfers between devices: 56 us -> 88.1 us  [shift(): return lax.ppermute(x, 'tensor', pairs)]
    pallas_call x0 -> x4, Pallas kernels: none -> 28.4 us  [the longest x2 12.1 us: add_pair(): pl.pallas_call(add_pair_kernel, grid=(rows // 128,), in_specs=[block] * 4...]
    convert_element_type x4 -> x0, other arithmetic: 17 us -> none  [the longest x2 10.4 us: step(): mine_down.astype(jnp.bfloat16)]
    reduce_scatter x4, waiting for transfers between devices: 29.7 us -> 38.1 us  [scatter_low(): lax.psum_scatter(part.astype(jnp.bfloat16), axis, scatter_dimension=dim,...]
    unnamed x132 -> x141, local copies, waits for them, and re-layouts: 10.2 us -> 17.6 us
  transfers between devices with their start and end apart: 30 -> 30, of which waited for: 10 -> 10; matrix products, arithmetic and copies ran while one was open for 50% -> 44% of each run, Pallas kernels for 19% -> 20%
where the time goes in v7:
time: 788 us; the launch traced here: 777 us
  matrix products  249 us (32%)
  Pallas kernels  164 us (21%)
  waiting for transfers between devices  117 us (15%)
  starting transfers between devices  93.2 us (12%)
  other arithmetic  90.9 us (12%)
  local copies, waits for them, and re-layouts  32.6 us (4%)
  between operations  16.4 us (2%)
  blocking collectives  14.7 us (2%)
    ppermute x21, starting transfers between devices, shift(): return lax.ppermute(x, 'tensor', pairs)  88.1 us
    ppermute x21, waiting for transfers between devices, shift(): return lax.ppermute(x, 'tensor', pairs)  74.3 us
    dot_general x4, matrix products, contract_rows(): lax.dot_general(left, right, (((0,), (0,)), ((), ())), preferred_element_...  73.9 us
    dot_general x10, matrix products, contract_cols(): lax.dot_general(left, right, (((1,), (1,)), ((), ())), preferred_element_...  69.3 us
    pallas_call x2, Pallas kernels, attention_backward(): pl.pallas_call(kernel, grid_spec=pltpu.PrefetchScalarGridSpec(num_scalar_...  61.6 us
    dot_general x4, matrix products, widen(): jnp.dot(ring[k], full_up, preferred_element_type=jnp.float32) + full_ubias  42.9 us
    reduce_scatter x4, waiting for transfers between devices, scatter_low(): lax.psum_scatter(part.astype(jnp.bfloat16), axis, scatter_dimension=dim,...  38.1 us
    pallas_call x1, Pallas kernels, attention_forward(): pl.pallas_call(kernel, grid_spec=pltpu.PrefetchScalarGridSpec(num_scalar_...  36.7 us
  transfers between devices with their start and end apart: 30, of which 10 were waited for; matrix products, arithmetic and copies ran while one was open for 44% of the time, Pallas kernels for 20%

profile of v7, /device:TPU:0, one launch (start us, length us, event | category | flops | bytes accessed | tf_op | source)
XLA Modules:
  0.0 777.1 jit_solution(10586815115212860419)
XLA Ops:
  19.9 14.7 %all-reduce = bf16[3584]{0:T(1024)(128)(2,1)S(1)} all-reduce(bf16[3584]{0:T(1024)(128)(2,1)S(1)} %dynamic-update-slice), channel_id=2, replica_groups=mesh['dp'=8,'tensor'=4] {'dp'}, use_global_device_ids=true, to_apply=%add | all-reduce | flops 3584 | bytes 14336
  66.0 11.8 %columns_sorted.1 = bf16[2048,1536]{1,0:T(8,128)(2,1)} custom-call(bf16[3,2048,512]{2,1,0:T(8,128)(2,1)} %all-gather.6.cloned.1.call-done.weight_ref), custom_call_target="tpu_custom_call" | custom-call | tf_op jit(solution)/shard_map/columns_sorted/pallas_call | solution.py:393
  77.8 8.6 %fusion.62.refs_2_ = f32[512,1536]{1,0:T(8,128)} fusion(bf16[512,2048]{1,0:T(8,128)(2,1)} %collective-permute-done, bf16[2048,1536]{1,0:T(8,128)(2,1)} %columns_sorted.1), kind=kOutput, calls=%fused_computation.147 | convolution fusion | flops 3221225472 | bytes 11534336 | tf_op jit(solution)/shard_map/dot_general | solution.py:592
  91.6 23.1 %collective-permute-done.1 = bf16[512,2048]{1,0:T(8,128)(2,1)} collective-permute-done((bf16[512,2048]{1,0:T(8,128)(2,1)}, bf16[512,2048]{1,0:T(8,128)(2,1)}, u32[]{:S(2)}, u32[]{:S(2)}) %collective-permute-start.1) | collective-permute-done | bytes 2097184 | tf_op jit(solution)/shard_map/ppermute | solution.py:442
  137.6 16.4 %multiply_convert_fusion.1 = (bf16[512,2048]{1,0:T(8,128)(2,1)}, f32[512,2048]{1,0:T(8,128)}, f32[512,2048]{1,0:T(8,128)}, bf16[512,2048]{1,0:T(8,128)(2,1)}, f32[512,2048]{1,0:T(8,128)}, /*index=5*/bf16[512,2048]{1,0:T(8,128)(2,1)}) fusion(f32[2048]{0:T(1024)S(1)} %bitcast.88, f32[512,2048]{1,0:T(8,128)} %fusion.65, f32[512,2048]{1,0:T(8,128)S(1)} %fusion.64, ...), kind=kOutput, calls=%fused_computation.76 | convolution fusion | flops 4357881856 | bytes 37756928 | tf_op jit(solution)/shard_map/dot_general | solution.py:595
  154.0 15.6 %collective-permute-done.2 = bf16[512,2048]{1,0:T(8,128)(2,1)} collective-permute-done((bf16[512,2048]{1,0:T(8,128)(2,1)}, bf16[512,2048]{1,0:T(8,128)(2,1)}, u32[]{:S(2)}, u32[]{:S(2)}) %collective-permute-start.2) | collective-permute-done | bytes 2097184 | tf_op jit(solution)/shard_map/ppermute | solution.py:442
  173.8 10.4 %multiply_convert_fusion = (bf16[512,2048]{1,0:T(8,128)(2,1)}, f32[512,2048]{1,0:T(8,128)}) fusion(f32[2048]{0:T(1024)S(1)} %bitcast.89, bf16[512,2048]{1,0:T(8,128)(2,1)} %collective-permute-done.2, bf16[2048,2048]{1,0:T(8,128)(2,1)S(1)} %copy-done.53), kind=kOutput, calls=%fused_computation.75 | convolution fusion | flops 4315938816 | bytes 16785408 | tf_op jit(solution)/shard_map/dot_general | solution.py:595
  184.2 10.0 %convolution_convert_fusion.6.a_ref = bf16[512,2048]{1,0:T(8,128)(2,1)} fusion(bf16[512,2048]{1,0:T(8,128)(2,1)} %get-tuple-element.284, bf16[2048,2048]{1,0:T(8,128)(2,1)} %all-gather.10.cloned.1.call-done.weight_ref), kind=kOutput, calls=%fused_computation.86 | convolution fusion | flops 4296015872 | bytes 12582912 | tf_op jit(solution)/shard_map/dot_general | solution.py:600
  234.0 36.7 %attend.1 = (bf16[2048,512]{1,0:T(8,128)(2,1)}, bf16[2048,512]{1,0:T(8,128)(2,1)}, bf16[2048,512]{1,0:T(8,128)(2,1)}, bf16[2048,512]{1,0:T(8,128)(2,1)}, f32[4,2,2048]{2,1,0:T(2,128)S(1)}) custom-call(s32[8]{0:T(128)S(1)} %get-tuple-element.244.refs_0_, s32[8]{0:T(128)S(1)} %get-tuple-element.245.refs_1_, f32[512,1536]{1,0:T(8,128)} %fusion.62.refs_2_, ...), custom_call_target="tpu_custom_call" | custom-call | tf_op jit(solution)/shard_map/attend/pallas_call | solution.py:157
  290.0 8.4 %hidden_back.4.refs_0_ = bf16[2048,2048]{1,0:T(8,128)(2,1)} custom-call(bf16[512,2048]{1,0:T(8,128)(2,1)S(1)} %copy-done, bf16[2048,2048]{1,0:T(8,128)(2,1)} %all-gather.10.cloned.1.call-done.weight_ref, f32[512,2048]{1,0:T(8,128)S(1)} %copy-done.17), custom_call_target="tpu_custom_call" | custom-call | flops 4294967296 | bytes 8388608 | tf_op jit(solution)/shard_map/hidden_back/pallas_call | solution.py:320
  363.8 19.8 %convolution_convert_fusion.1 = bf16[2048,2048]{1,0:T(8,128)(2,1)} fusion(bf16[2048,2048]{1,0:T(8,128)(2,1)S(1)} %bitcast.74, bf16[512,2048]{1,0:T(8,128)(2,1)S(1)} %copy-done, bf16[512,2048]{1,0:T(8,128)(2,1)S(1)} %broadcast_select_fusion.block_ref, bf16[512,2048]{1,0:T(8,128)(2,1)S(1)} %copy-done.7, bf16[512,2048]{1,0:T(8,128)(2,1)S(1)} %broadcast_select_fusion.1.block_ref), kind=kOutput, calls=%fused_computation.12 | convolution fusion | flops 17217617920 | bytes 25165824 | tf_op jit(solution)/shard_map/dot_general | solution.py:430
  395.5 46.3 %collective-permute-start.15 = (bf16[512,2048]{1,0:T(8,128)(2,1)}, bf16[512,2048]{1,0:T(8,128)(2,1)}, u32[]{:S(2)}, u32[]{:S(2)}) collective-permute-start(bf16[512,2048]{1,0:T(8,128)(2,1)} %convolution_convert_fusion.5), channel_id=1, source_target_pairs={{0,1},{1,2},{2,3},{3,0},{4,5},{5,6},{6,7},{7,4},{8,9},{9,10},{10,1... | collective-permute-start | bytes 6291464 | tf_op jit(solution)/shard_map/ppermute | solution.py:442
  446.2 30.8 %attend_back.2 = (bf16[2048,1536]{1,0:T(8,128)(2,1)}, f32[3,1,512]{2,1,0:T(1,128)S(1)}) custom-call(s32[8]{0:T(128)S(1)} %get-tuple-element.244.refs_0_, s32[8]{0:T(128)S(1)} %get-tuple-element.245.refs_1_, bf16[512,512]{1,0:T(8,128)(2,1)S(1)} %copy-done.24, bf16[512,512]{1,0:T(8,128)(2,1)S(1)} %copy-done.20, bf16[512,512]{1,0:T(8,128)(2,1)S(1)} %copy-done.22, ...), custom_call_target="tpu_custom_call" | custom-call | tf_op jit(solution)/shard_map/attend_back/pallas_call | solution.py:279
  477.0 9.4 %convolution_convert_fusion.4 = bf16[512,2048]{1,0:T(8,128)(2,1)} fusion(bf16[2048,512]{1,0:T(8,128)(2,1)S(1)} %copy-done.57, bf16[2048,2048]{1,0:T(8,128)(2,1)} %pad_maximum_fusion.2), kind=kOutput, calls=%fused_computation.84 | convolution fusion | flops 4296015872 | bytes 12582912 | tf_op jit(solution)/shard_map/dot_general | solution.py:430
  500.0 30.8 %attend_back.3 = (bf16[2048,1536]{1,0:T(8,128)(2,1)}, f32[3,1,512]{2,1,0:T(1,128)S(1)}) custom-call(s32[8]{0:T(128)S(1)} %get-tuple-element.244.refs_0_, s32[8]{0:T(128)S(1)} %get-tuple-element.245.refs_1_, bf16[512,512]{1,0:T(8,128)(2,1)S(1)} %copy-done.25, bf16[512,512]{1,0:T(8,128)(2,1)S(1)} %copy-done.21, ...), custom_call_target="tpu_custom_call", output_to_operand_aliasing={{0}: (14, {}), {1}: (15, {})} | custom-call | tf_op jit(solution)/shard_map/attend_back/pallas_call | solution.py:279
  530.8 8.5 %hidden_back.6.refs_0_ = bf16[2048,2048]{1,0:T(8,128)(2,1)} custom-call(bf16[512,2048]{1,0:T(8,128)(2,1)S(1)} %copy-done.5, bf16[2048,2048]{1,0:T(8,128)(2,1)} %all-gather.10.cloned.1.call-done.weight_ref, f32[512,2048]{1,0:T(8,128)S(1)} %copy-done.14, bf16[2048,2048]{1,0:T(8,128)(2,1)} %hidden_back.5.refs_0_), custom_call_target="tpu_custom_call", output_to_operand_aliasing={{}: (3, {})} | custom-call | flops 4294967296 | bytes 8388608 | tf_op jit(solution)/shard_map/hidden_back/pallas_call | solution.py:320
  551.2 24.1 %convolution_convert_fusion = bf16[2048,2048]{1,0:T(8,128)(2,1)} fusion(bf16[2048,2048]{1,0:T(8,128)(2,1)} %pad_maximum_fusion.1, bf16[2048,2048]{1,0:T(8,128)(2,1)} %hidden_back.7), kind=kOutput, calls=%fused_computation.11 | convolution fusion | flops 17184063488 | bytes 25165824 | tf_op jit(solution)/shard_map/dot_general | solution.py:430
  581.4 9.9 %add_convert_fusion.4 = bf16[512,2048]{1,0:T(8,128)(2,1)} fusion(f32[512,2048]{1,0:T(8,128)S(1)} %fusion.50, bf16[2048,2048]{1,0:T(8,128)(2,1)} %all-gather.8.cloned.1.call-done, bf16[2048,2048]{1,0:T(8,128)(2,1)} %hidden_back.7), kind=kOutput, calls=%fused_computation.72 | convolution fusion | flops 4297064448 | bytes 16777216 | tf_op jit(solution)/shard_map/dot_general | solution.py:436
  598.2 20.6 %convolution_convert_fusion.3 = bf16[2048,1536]{1,0:T(8,128)(2,1)} fusion(bf16[2048,2048]{1,0:T(8,128)(2,1)} %pad_maximum_fusion.1, bf16[2048,1536]{1,0:T(8,128)(2,1)} %get-tuple-element.373), kind=kOutput, calls=%fused_computation.14 | convolution fusion | flops 12888047616 | bytes 20971520 | tf_op jit(solution)/shard_map/dot_general | solution.py:430
  625.6 10.2 %add_convert_fusion.3 = bf16[512,2048]{1,0:T(8,128)(2,1)} fusion(f32[512,2048]{1,0:T(8,128)S(1)} %fusion.48, bf16[2048,2048]{1,0:T(8,128)(2,1)} %all-gather.8.cloned.1.call-done, bf16[2048,2048]{1,0:T(8,128)(2,1)} %hidden_back.7), kind=kOutput, calls=%fused_computation.71 | convolution fusion | flops 4297064448 | bytes 16777216 | tf_op jit(solution)/shard_map/dot_general | solution.py:436
  635.8 8.5 %collective-permute-done.18 = bf16[512,2048]{1,0:T(8,128)(2,1)S(1)} collective-permute-done((bf16[512,2048]{1,0:T(8,128)(2,1)}, bf16[512,2048]{1,0:T(8,128)(2,1)S(1)}, u32[]{:S(2)}, u32[]{:S(2)}) %collective-permute-start.18) | collective-permute-done | bytes 2097184 | tf_op jit(solution)/shard_map/ppermute | solution.py:442
  662.6 11.0 %fusion.44 = f32[1024,2048]{1,0:T(8,128)} fusion(bf16[2048,1536]{1,0:T(8,128)(2,1)} %columns_sorted.1, bf16[2048,1536]{1,0:T(8,128)(2,1)S(1)} %bitcast.76), kind=kOutput, calls=%fused_computation.82 | convolution fusion | flops 6442450944 | bytes 17825792 | tf_op jit(solution)/shard_map/dot_general | solution.py:436
  673.6 15.3 %add_convert_fusion = bf16[1024,2048]{1,0:T(8,128)(2,1)} fusion(f32[1024,2048]{1,0:T(8,128)} %fusion.44, bf16[2048,2048]{1,0:T(8,128)(2,1)} %all-gather.8.cloned.1.call-done, bf16[2048,2048]{1,0:T(8,128)(2,1)S(1)} %bitcast.72), kind=kOutput, calls=%fused_computation.5 | convolution fusion | flops 8594128896 | bytes 25165824 | tf_op jit(solution)/shard_map/dot_general | solution.py:436
  693.8 38.1 %reduce-scatter.11.cloned.1.call-done.part_ref = bf16[256,1536]{1,0:T(8,128)(2,1)} async-done(((bf16[2048,1536]{1,0:T(8,128)(2,1)}), bf16[256,1536]{1,0:T(8,128)(2,1)}) %reduce-scatter.11.cloned.1.call-update) | async-done | bytes 786448 | tf_op jit(solution)/shard_map/reduce_scatter | solution.py:518
  (306 shorter events, 321.6 us)
Async XLA Ops:
  7.2 58.7 %all-gather.6.cloned.1.call-start = ((), (), s32[]{:S(2)}) async-start(), calls=%async_computation.5 | async-start | bytes 7077888 | tf_op jit(solution)/shard_map/all_gather | solution.py:548
  8.0 113.6 %all-gather.8.cloned.1.call-start = ((), (), s32[]{:S(2)}) async-start(), calls=%async_computation.6 | async-start | bytes 9437184 | tf_op jit(solution)/shard_map/all_gather | solution.py:552
  12.6 171.6 %all-gather.10.cloned.1.call-start = ((), (), s32[]{:S(2)}) async-start(), calls=%async_computation.7 | async-start | bytes 9437184 | tf_op jit(solution)/shard_map/all_gather | solution.py:553
  13.3 288.2 %all-gather.12.cloned.1.call-start = ((), (), s32[]{:S(2)}) async-start(), calls=%async_computation.8 | async-start | bytes 2359296 | tf_op jit(solution)/shard_map/all_gather | solution.py:554
  13.3 51.0 %collective-permute-start = (bf16[512,2048]{1,0:T(8,128)(2,1)}, bf16[512,2048]{1,0:T(8,128)(2,1)}, u32[]{:S(2)}, u32[]{:S(2)}) collective-permute-start(bf16[512,2048]{1,0:T(8,128)(2,1)} %normalize.1), channel_id=1, source_target_pairs={{0,1},{1,2},{2,3},{3,0},{4,5},{5,6},{6,7},{7,4},{8,9},{9,10},{10,1... | collective-permute-start | bytes 6291464 | tf_op jit(solution)/shard_map/ppermute | solution.py:442
  65.7 48.9 %collective-permute-start.1 = (bf16[512,2048]{1,0:T(8,128)(2,1)}, bf16[512,2048]{1,0:T(8,128)(2,1)}, u32[]{:S(2)}, u32[]{:S(2)}) collective-permute-start(bf16[512,2048]{1,0:T(8,128)(2,1)} %collective-permute-done), channel_id=1, source_target_pairs={{0,1},{1,2},{2,3},{3,0},{4,5},{5,6},{6,7},{7,4},{8,9},{9,10},{10,1... | collective-permute-start | bytes 6291464 | tf_op jit(solution)/shard_map/ppermute | solution.py:442
  65.7 481.9 %reduce-scatter.5.cloned.1.call-start = ((), (), s32[]{:S(2)}) async-start(), calls=%async_computation.9 | async-start | bytes 9437184 | tf_op jit(solution)/shard_map/reduce_scatter | solution.py:518
  121.3 48.3 %collective-permute-start.2 = (bf16[512,2048]{1,0:T(8,128)(2,1)}, bf16[512,2048]{1,0:T(8,128)(2,1)}, u32[]{:S(2)}, u32[]{:S(2)}) collective-permute-start(bf16[512,2048]{1,0:T(8,128)(2,1)} %collective-permute-done.1), channel_id=1, source_target_pairs={{0,1},{1,2},{2,3},{3,0},{4,5},{5,6},{6,7},{7,4},{8,9},{9,10},{10,1... | collective-permute-start | bytes 6291464 | tf_op jit(solution)/shard_map/ppermute | solution.py:442
  169.6 49.2 %collective-permute-start.3 = (bf16[512,2048]{1,0:T(8,128)(2,1)S(1)}, bf16[512,2048]{1,0:T(8,128)(2,1)}, u32[]{:S(2)}, u32[]{:S(2)}) collective-permute-start(bf16[512,2048]{1,0:T(8,128)(2,1)S(1)} %copy-done), channel_id=1, source_target_pairs={{0,1},{1,2},{2,3},{4,5},{5,6},{6,7},{8,9},{9,10},{10,11},{12,13},{... | collective-permute-start | bytes 6291464 | tf_op jit(solution)/shard_map/ppermute | solution.py:442
  219.3 51.4 %collective-permute-start.5 = (bf16[512,2048]{1,0:T(8,128)(2,1)}, bf16[512,2048]{1,0:T(8,128)(2,1)}, u32[]{:S(2)}, u32[]{:S(2)}) collective-permute-start(bf16[512,2048]{1,0:T(8,128)(2,1)} %collective-permute-done.3), channel_id=1, source_target_pairs={{1,2},{2,3},{5,6},{6,7},{9,10},{10,11},{13,14},{14,15},{17,18},{18... | collective-permute-start | bytes 6291464 | tf_op jit(solution)/shard_map/ppermute | solution.py:442
  221.3 49.4 %collective-permute-start.6 = (bf16[512,2048]{1,0:T(8,128)(2,1)}, bf16[512,2048]{1,0:T(8,128)(2,1)}, u32[]{:S(2)}, u32[]{:S(2)}) collective-permute-start(bf16[512,2048]{1,0:T(8,128)(2,1)} %collective-permute-done.4), channel_id=1, source_target_pairs={{1,0},{2,1},{5,4},{6,5},{9,8},{10,9},{13,12},{14,13},{17,16},{18,1... | collective-permute-start | bytes 6291464 | tf_op jit(solution)/shard_map/ppermute | solution.py:442
  222.5 48.2 %collective-permute-start.7 = (bf16[512,2048]{1,0:T(8,128)(2,1)}, bf16[512,2048]{1,0:T(8,128)(2,1)}, u32[]{:S(2)}, u32[]{:S(2)}) collective-permute-start(bf16[512,2048]{1,0:T(8,128)(2,1)} %convolution_convert_fusion.8.c_ref), channel_id=1, source_target_pairs={{0,1},{4,5},{8,9},{12,13},{16,17},{20,21},{24,25},{28,29}} | collective-permute-start | bytes 6291464 | tf_op jit(solution)/shard_map/ppermute | solution.py:442
  277.0 58.5 %collective-permute-start.11 = (bf16[512,2048]{1,0:T(8,128)(2,1)}, bf16[512,2048]{1,0:T(8,128)(2,1)}, u32[]{:S(2)}, u32[]{:S(2)}) collective-permute-start(bf16[512,2048]{1,0:T(8,128)(2,1)} %get-tuple-element.276), channel_id=1, source_target_pairs={{0,1},{1,2},{4,5},{5,6},{8,9},{9,10},{12,13},{13,14},{16,17},{17,1... | collective-permute-start | bytes 6291464 | tf_op jit(solution)/shard_map/ppermute | solution.py:442
  282.5 53.0 %collective-permute-start.12 = (bf16[512,2048]{1,0:T(8,128)(2,1)}, bf16[512,2048]{1,0:T(8,128)(2,1)}, u32[]{:S(2)}, u32[]{:S(2)}) collective-permute-start(bf16[512,2048]{1,0:T(8,128)(2,1)} %get-tuple-element.277), channel_id=1, source_target_pairs={{2,1},{3,2},{6,5},{7,6},{10,9},{11,10},{14,13},{15,14},{18,17},{19... | collective-permute-start | bytes 6291464 | tf_op jit(solution)/shard_map/ppermute | solution.py:442
  284.5 51.1 %collective-permute-start.10 = (bf16[512,2048]{1,0:T(8,128)(2,1)}, bf16[512,2048]{1,0:T(8,128)(2,1)}, u32[]{:S(2)}, u32[]{:S(2)}) collective-permute-start(bf16[512,2048]{1,0:T(8,128)(2,1)} %collective-permute-done.6), channel_id=1, source_target_pairs={{1,0},{5,4},{9,8},{13,12},{17,16},{21,20},{25,24},{29,28}} | collective-permute-start | bytes 6291464 | tf_op jit(solution)/shard_map/ppermute | solution.py:442
  285.8 49.8 %collective-permute-start.9 = (bf16[512,2048]{1,0:T(8,128)(2,1)}, bf16[512,2048]{1,0:T(8,128)(2,1)}, u32[]{:S(2)}, u32[]{:S(2)}) collective-permute-start(bf16[512,2048]{1,0:T(8,128)(2,1)} %collective-permute-done.5), channel_id=1, source_target_pairs={{2,3},{6,7},{10,11},{14,15},{18,19},{22,23},{26,27},{30,31}} | collective-permute-start | bytes 6291464 | tf_op jit(solution)/shard_map/ppermute | solution.py:442
  341.4 47.6 %collective-permute-start.13 = (bf16[512,2048]{1,0:T(8,128)(2,1)}, bf16[512,2048]{1,0:T(8,128)(2,1)}, u32[]{:S(2)}, u32[]{:S(2)}) collective-permute-start(bf16[512,2048]{1,0:T(8,128)(2,1)} %get-tuple-element.298), channel_id=1, source_target_pairs={{0,1},{1,2},{2,3},{4,5},{5,6},{6,7},{8,9},{9,10},{10,11},{12,13},{... | collective-permute-start | bytes 6291464 | tf_op jit(solution)/shard_map/ppermute | solution.py:442
  395.5 195.8 %reduce-scatter.7.cloned.1.call-start = ((), (), s32[]{:S(2)}) async-start(), calls=%async_computation.10 | async-start | bytes 2359296 | tf_op jit(solution)/shard_map/reduce_scatter | solution.py:518
  395.5 90.8 %collective-permute-start.15 = (bf16[512,2048]{1,0:T(8,128)(2,1)}, bf16[512,2048]{1,0:T(8,128)(2,1)}, u32[]{:S(2)}, u32[]{:S(2)}) collective-permute-start(bf16[512,2048]{1,0:T(8,128)(2,1)} %convolution_convert_fusion.5), channel_id=1, source_target_pairs={{0,1},{1,2},{2,3},{3,0},{4,5},{5,6},{6,7},{7,4},{8,9},{9,10},{10,1... | collective-permute-start | bytes 6291464 | tf_op jit(solution)/shard_map/ppermute | solution.py:442
  490.8 56.8 %collective-permute-start.16 = (bf16[512,2048]{1,0:T(8,128)(2,1)}, bf16[512,2048]{1,0:T(8,128)(2,1)}, u32[]{:S(2)}, u32[]{:S(2)}) collective-permute-start(bf16[512,2048]{1,0:T(8,128)(2,1)} %add_convert_fusion.6), channel_id=1, source_target_pairs={{0,1},{1,2},{2,3},{3,0},{4,5},{5,6},{6,7},{7,4},{8,9},{9,10},{10,1... | collective-permute-start | bytes 6291464 | tf_op jit(solution)/shard_map/ppermute | solution.py:442
  493.0 196.0 %reduce-scatter.9.cloned.1.call-start = ((), (), s32[]{:S(2)}) async-start(), calls=%async_computation.11 | async-start | bytes 9437184 | tf_op jit(solution)/shard_map/reduce_scatter | solution.py:518
  550.9 47.2 %collective-permute-start.17 = (bf16[512,2048]{1,0:T(8,128)(2,1)S(1)}, bf16[512,2048]{1,0:T(8,128)(2,1)}, u32[]{:S(2)}, u32[]{:S(2)}) collective-permute-start(bf16[512,2048]{1,0:T(8,128)(2,1)S(1)} %add_convert_fusion.5), channel_id=1, source_target_pairs={{0,1},{1,2},{2,3},{3,0},{4,5},{5,6},{6,7},{7,4},{8,9},{9,10},{10,1... | collective-permute-start | bytes 6291464 | tf_op jit(solution)/shard_map/ppermute | solution.py:442
  598.1 133.8 %reduce-scatter.11.cloned.1.call-start = ((), (), s32[]{:S(2)}) async-start(), calls=%async_computation.12 | async-start | bytes 7077888 | tf_op jit(solution)/shard_map/reduce_scatter | solution.py:518
  692.6 54.2 %collective-permute-start.20 = (bf16[512,2048]{1,0:T(8,128)(2,1)}, bf16[512,2048]{1,0:T(8,128)(2,1)}, u32[]{:S(2)}, u32[]{:S(2)}) collective-permute-start(bf16[512,2048]{1,0:T(8,128)(2,1)} %add_convert_fusion.1), channel_id=1, source_target_pairs={{0,1},{1,2},{2,3},{3,0},{4,5},{5,6},{6,7},{7,4},{8,9},{9,10},{10,1... | collective-permute-start | bytes 6291464 | tf_op jit(solution)/shard_map/ppermute | solution.py:442
  (74 other events, 960.5 us)
Sparse Core Ops, SparseCore 0:
  10.0 48.4 all-gather.5
  60.4 54.3 all-gather.7
  116.7 55.9 all-gather.9
  174.4 28.1 all-gather.11
  395.6 113.9 reduce-scatter.4
  513.6 41.2 reduce-scatter.6
  598.2 68.0 reduce-scatter.8
  670.1 61.7 reduce-scatter.10

commit v8 on v6

--- a/solution.py
+++ b/solution.py
@@ -339,6 +339,45 @@
     )(block, weight, slope, *held)
 
 
+def normalize_kernel(x_ref, gain_ref, shift_ref, out_ref):
+    x = x_ref[...].astype(jnp.float32)
+    centered = x - jnp.mean(x, axis=-1, keepdims=True)
+    inverse = lax.rsqrt(jnp.mean(centered * centered, axis=-1, keepdims=True) + EPS)
+    out_ref[...] = (centered * inverse * gain_ref[...] + shift_ref[...]).astype(jnp.bfloat16)
+
+
+def normalize(x, gain, shift_in):
+    rows, width = x.shape
+    block = pl.BlockSpec((128, width), lambda i: (i, 0))
+    wide = pl.BlockSpec((1, width), lambda i: (0, 0))
+    return pl.pallas_call(
+        normalize_kernel,
+        grid=(rows // 128,),
+        in_specs=[block, wide, wide],
+        out_specs=block,
+        out_shape=jax.ShapeDtypeStruct((rows, width), jnp.bfloat16),
+        name="normalize",
+    )(x, gain[None, :], shift_in[None, :])
+
+
+def columns_sorted_kernel(weight_ref, out_ref):
+    for c in range(3):
+        out_ref[:, c * PAIR : (c + 1) * PAIR] = weight_ref[c]
+
+
+def columns_sorted(weight):
+    _, rows, width = weight.shape
+    tile = min(512, rows)
+    return pl.pallas_call(
+        columns_sorted_kernel,
+        grid=(rows // tile, width // PAIR),
+        in_specs=[pl.BlockSpec((3, tile, PAIR), lambda r, p: (0, r, p))],
+        out_specs=pl.BlockSpec((tile, 3 * PAIR), lambda r, p: (r, p)),
+        out_shape=jax.ShapeDtypeStruct((rows, 3 * width), weight.dtype),
+        name="columns_sorted",
+    )(weight)
+
+
 def columns_back_kernel(part_ref, out_ref):
     for c in range(3):
         out_ref[c] = part_ref[:, c * PAIR : (c + 1) * PAIR].astype(jnp.float32)
@@ -484,7 +523,7 @@
     centered = resid - row_mean
     inverse = lax.rsqrt(jnp.mean(centered * centered, axis=-1, keepdims=True) + EPS)
     normed = centered * inverse
-    normed_mine = (normed * norm_gain + norm_shift).astype(low)
+    normed_mine = normalize(tokens, norm_gain, norm_shift)
     full_qkv = lax.all_gather(qkv_weight, "dp", axis=1, tiled=True)
     normed_mine, up_weight, down_weight, dense_weight = lax.optimization_barrier(
         (normed_mine, up_weight, down_weight, dense_weight)
@@ -520,8 +559,7 @@
         (ring[1], cotangent, tables, full_qbias, full_ubias, cot_columns, resid_square)
     )
     pairs = qkv_weight.shape[2] // PAIR
-    sorted_qkv = full_qkv.reshape(3, model_width, pairs, PAIR).transpose(1, 2, 0, 3)
-    sorted_qkv = sorted_qkv.reshape(model_width, 3 * pairs * PAIR)
+    sorted_qkv = columns_sorted(full_qkv)
     half = max(1, pairs // 2)
     projected, slopes, hidden_act, mlp_parts = ([None] * ways for _ in range(4))
     grad_context, grad_pre = [None] * ways, [None]

time: 722 us -> 718 us (level)
  Pallas kernels: 135 us -> 154 us
  waiting for transfers between devices: 105 us -> 88 us
    pallas_call x0 -> x2, Pallas kernels: none -> 16.3 us  [the longest x1 11.8 us: columns_sorted(): pl.pallas_call(columns_sorted_kernel, grid=(rows // tile, width // PAIR),...]
    ppermute x21, waiting for transfers between devices: 72 us -> 57.6 us  [shift(): return lax.ppermute(x, 'tensor', pairs)]
  transfers between devices with their start and end apart: 30 -> 30, of which waited for: 10 -> 10; matrix products, arithmetic and copies ran while one was open for 50% -> 49% of each run, Pallas kernels for 19% -> 22%
where the time goes in v8:
time: 718 us; the launch traced here: 708 us
  matrix products  248 us (35%)
  Pallas kernels  154 us (21%)
  other arithmetic  104 us (14%)
  waiting for transfers between devices  88 us (12%)
  starting transfers between devices  60 us (8%)
  local copies, waits for them, and re-layouts  22.7 us (3%)
  between operations  16.6 us (2%)
  blocking collectives  14.7 us (2%)
    dot_general x4, matrix products, contract_rows(): lax.dot_general(left, right, (((0,), (0,)), ((), ())), preferred_element_...  73 us
    dot_general x10, matrix products, contract_cols(): lax.dot_general(left, right, (((1,), (1,)), ((), ())), preferred_element_...  69.7 us
    pallas_call x2, Pallas kernels, attention_backward(): pl.pallas_call(kernel, grid_spec=pltpu.PrefetchScalarGridSpec(num_scalar_...  63 us
    ppermute x21, waiting for transfers between devices, shift(): return lax.ppermute(x, 'tensor', pairs)  57.6 us
    ppermute x21, starting transfers between devices, shift(): return lax.ppermute(x, 'tensor', pairs)  55.1 us
    dot_general x4, matrix products, widen(): jnp.dot(ring[k], full_up, preferred_element_type=jnp.float32) + full_ubias  42.9 us
    pallas_call x1, Pallas kernels, attention_forward(): pl.pallas_call(kernel, grid_spec=pltpu.PrefetchScalarGridSpec(num_scalar_...  37.7 us
    pallas_call x4, Pallas kernels, hidden_back(): pl.pallas_call(hidden_back_kernel, grid=(hidden // tile,), in_specs=[pl.B...  33.8 us
  transfers between devices with their start and end apart: 30, of which 10 were waited for; matrix products, arithmetic and copies ran while one was open for 49% of the time, Pallas kernels for 22%

profile of v8, /device:TPU:0, one launch (start us, length us, event | category | flops | bytes accessed | tf_op | source)
XLA Modules:
  0.0 708.1 jit_solution(5515911559672487885)
XLA Ops:
  19.9 14.7 %all-reduce = bf16[3584]{0:T(1024)(128)(2,1)S(1)} all-reduce(bf16[3584]{0:T(1024)(128)(2,1)S(1)} %dynamic-update-slice), channel_id=2, replica_groups=mesh['dp'=8,'tensor'=4] {'dp'}, use_global_device_ids=true, to_apply=%add | all-reduce | flops 3584 | bytes 14336
  65.7 11.8 %columns_sorted.1 = bf16[2048,1536]{1,0:T(8,128)(2,1)} custom-call(bf16[3,2048,512]{2,1,0:T(8,128)(2,1)} %all-gather.6.cloned.1.call-done.weight_ref), custom_call_target="tpu_custom_call" | custom-call | tf_op jit(solution)/shard_map/columns_sorted/pallas_call | solution.py:371
  77.5 8.6 %fusion.64.refs_2_ = f32[512,1536]{1,0:T(8,128)} fusion(bf16[512,2048]{1,0:T(8,128)(2,1)} %collective-permute-done, bf16[2048,1536]{1,0:T(8,128)(2,1)} %columns_sorted.1), kind=kOutput, calls=%fused_computation.153 | convolution fusion | flops 3221225472 | bytes 11534336 | tf_op jit(solution)/shard_map/dot_general | solution.py:571
  91.2 23.5 %collective-permute-done.1 = bf16[512,2048]{1,0:T(8,128)(2,1)} collective-permute-done((bf16[512,2048]{1,0:T(8,128)(2,1)}, bf16[512,2048]{1,0:T(8,128)(2,1)}, u32[]{:S(2)}, u32[]{:S(2)}) %collective-permute-start.1) | collective-permute-done | bytes 2097184 | tf_op jit(solution)/shard_map/ppermute | solution.py:420
  121.8 8.4 %fusion.66 = f32[512,2048]{1,0:T(8,128)S(1)} fusion(bf16[512,2048]{1,0:T(8,128)(2,1)} %normalize.1, bf16[2048,2048]{1,0:T(8,128)(2,1)} %all-gather.8.cloned.1.call-done), kind=kOutput, calls=%fused_computation.155 | convolution fusion | flops 4294967296 | bytes 14680064 | tf_op jit(solution)/shard_map/dot_general | solution.py:574
  137.9 16.4 %multiply_convert_fusion.1 = (bf16[512,2048]{1,0:T(8,128)(2,1)}, f32[512,2048]{1,0:T(8,128)}, f32[512,2048]{1,0:T(8,128)}, bf16[512,2048]{1,0:T(8,128)(2,1)}, f32[512,2048]{1,0:T(8,128)}, /*index=5*/bf16[512,2048]{1,0:T(8,128)(2,1)}) fusion(f32[2048]{0:T(1024)S(1)} %bitcast.86, f32[512,2048]{1,0:T(8,128)} %fusion.67, f32[512,2048]{1,0:T(8,128)S(1)} %fusion.66, ...), kind=kOutput, calls=%fused_computation.82 | convolution fusion | flops 4357881856 | bytes 37756928 | tf_op jit(solution)/shard_map/dot_general | solution.py:574
  154.3 8.8 %collective-permute-done.2 = bf16[512,2048]{1,0:T(8,128)(2,1)} collective-permute-done((bf16[512,2048]{1,0:T(8,128)(2,1)}, bf16[512,2048]{1,0:T(8,128)(2,1)}, u32[]{:S(2)}, u32[]{:S(2)}) %collective-permute-start.2) | collective-permute-done | bytes 2097184 | tf_op jit(solution)/shard_map/ppermute | solution.py:420
  167.2 10.4 %multiply_convert_fusion = (bf16[512,2048]{1,0:T(8,128)(2,1)}, f32[512,2048]{1,0:T(8,128)}) fusion(f32[2048]{0:T(1024)S(1)} %bitcast.87, bf16[512,2048]{1,0:T(8,128)(2,1)} %collective-permute-done.2, bf16[2048,2048]{1,0:T(8,128)(2,1)S(1)} %copy-done.46), kind=kOutput, calls=%fused_computation.81 | convolution fusion | flops 4315938816 | bytes 16785408 | tf_op jit(solution)/shard_map/dot_general | solution.py:574
  177.6 10.0 %convolution_convert_fusion.6 = bf16[512,2048]{1,0:T(8,128)(2,1)} fusion(bf16[512,2048]{1,0:T(8,128)(2,1)} %get-tuple-element.276, bf16[2048,2048]{1,0:T(8,128)(2,1)} %all-gather.10.cloned.1.call-done.weight_ref), kind=kOutput, calls=%fused_computation.92 | convolution fusion | flops 4296015872 | bytes 12582912 | tf_op jit(solution)/shard_map/dot_general | solution.py:579
  227.3 37.7 %attend.1 = (bf16[2048,512]{1,0:T(8,128)(2,1)}, bf16[2048,512]{1,0:T(8,128)(2,1)}, bf16[2048,512]{1,0:T(8,128)(2,1)}, bf16[2048,512]{1,0:T(8,128)(2,1)}, f32[4,2,2048]{2,1,0:T(2,128)S(1)}) custom-call(s32[8]{0:T(128)S(1)} %get-tuple-element.238.refs_0_, s32[8]{0:T(128)S(1)} %get-tuple-element.239.refs_1_, f32[512,1536]{1,0:T(8,128)} %fusion.64.refs_2_, ...), custom_call_target="tpu_custom_call" | custom-call | tf_op jit(solution)/shard_map/attend/pallas_call | solution.py:157
  280.6 8.6 %hidden_back.4.refs_0_ = bf16[2048,2048]{1,0:T(8,128)(2,1)} custom-call(bf16[512,2048]{1,0:T(8,128)(2,1)S(1)} %copy-done, bf16[2048,2048]{1,0:T(8,128)(2,1)} %all-gather.10.cloned.1.call-done.weight_ref, f32[512,2048]{1,0:T(8,128)S(1)} %copy-done.14), custom_call_target="tpu_custom_call" | custom-call | flops 4294967296 | bytes 8388608 | tf_op jit(solution)/shard_map/hidden_back/pallas_call | solution.py:320
  355.7 19.8 %convolution_convert_fusion.1 = bf16[2048,2048]{1,0:T(8,128)(2,1)} fusion(bf16[2048,2048]{1,0:T(8,128)(2,1)S(1)} %pad_maximum_fusion, bf16[512,2048]{1,0:T(8,128)(2,1)S(1)} %copy-done, bf16[512,2048]{1,0:T(8,128)(2,1)S(1)} %broadcast_select_fusion.block_ref, bf16[512,2048]{1,0:T(8,128)(2,1)S(1)} %copy-done.4, ...), kind=kOutput, calls=%fused_computation.12 | convolution fusion | flops 17217617920 | bytes 25165824 | tf_op jit(solution)/shard_map/dot_general | solution.py:408
  392.5 31.6 %attend_back.2 = (bf16[2048,1536]{1,0:T(8,128)(2,1)}, f32[3,1,512]{2,1,0:T(1,128)S(1)}) custom-call(s32[8]{0:T(128)S(1)} %get-tuple-element.238.refs_0_, s32[8]{0:T(128)S(1)} %get-tuple-element.239.refs_1_, bf16[512,512]{1,0:T(8,128)(2,1)S(1)} %copy-done.18, bf16[512,512]{1,0:T(8,128)(2,1)S(1)} %copy-done.16, bf16[512,512]{1,0:T(8,128)(2,1)S(1)} %copy-done.17, ...), custom_call_target="tpu_custom_call" | custom-call | tf_op jit(solution)/shard_map/attend_back/pallas_call | solution.py:279
  424.1 8.5 %hidden_back.6.refs_0_ = bf16[2048,2048]{1,0:T(8,128)(2,1)} custom-call(bf16[512,2048]{1,0:T(8,128)(2,1)S(1)} %copy-done.6, bf16[2048,2048]{1,0:T(8,128)(2,1)} %all-gather.10.cloned.1.call-done.weight_ref, f32[512,2048]{1,0:T(8,128)S(1)} %copy-done.12, bf16[2048,2048]{1,0:T(8,128)(2,1)} %hidden_back.5.refs_0_), custom_call_target="tpu_custom_call", output_to_operand_aliasing={{}: (3, {})} | custom-call | flops 4294967296 | bytes 8388608 | tf_op jit(solution)/shard_map/hidden_back/pallas_call | solution.py:320
  440.8 31.4 %attend_back.3 = (bf16[2048,1536]{1,0:T(8,128)(2,1)}, f32[3,1,512]{2,1,0:T(1,128)S(1)}) custom-call(s32[8]{0:T(128)S(1)} %get-tuple-element.238.refs_0_, s32[8]{0:T(128)S(1)} %get-tuple-element.239.refs_1_, bf16[512,512]{1,0:T(8,128)(2,1)S(1)} %copy-done.18, bf16[512,512]{1,0:T(8,128)(2,1)S(1)} %copy-done.16, ...), custom_call_target="tpu_custom_call", output_to_operand_aliasing={{0}: (14, {}), {1}: (15, {})} | custom-call | tf_op jit(solution)/shard_map/attend_back/pallas_call | solution.py:279
  472.2 8.5 %hidden_back.7 = bf16[2048,2048]{1,0:T(8,128)(2,1)} custom-call(bf16[512,2048]{1,0:T(8,128)(2,1)S(1)} %copy-done.3, bf16[2048,2048]{1,0:T(8,128)(2,1)} %all-gather.10.cloned.1.call-done.weight_ref, f32[512,2048]{1,0:T(8,128)S(1)} %copy-done.11, bf16[2048,2048]{1,0:T(8,128)(2,1)} %hidden_back.6.refs_0_), custom_call_target="tpu_custom_call", output_to_operand_aliasing={{}: (3, {})} | custom-call | flops 4294967296 | bytes 8388608 | tf_op jit(solution)/shard_map/hidden_back/pallas_call | solution.py:320
  480.6 9.2 %convolution_convert_fusion.4 = bf16[512,2048]{1,0:T(8,128)(2,1)} fusion(bf16[2048,512]{1,0:T(8,128)(2,1)S(1)} %copy-done.48, bf16[2048,2048]{1,0:T(8,128)(2,1)} %pad_maximum_fusion.2), kind=kOutput, calls=%fused_computation.90 | convolution fusion | flops 4296015872 | bytes 12582912 | tf_op jit(solution)/shard_map/dot_general | solution.py:408
  495.0 19.4 %convolution_convert_fusion.3 = bf16[2048,1536]{1,0:T(8,128)(2,1)} fusion(bf16[2048,2048]{1,0:T(8,128)(2,1)} %pad_maximum_fusion.1, bf16[2048,1536]{1,0:T(8,128)(2,1)} %get-tuple-element.361), kind=kOutput, calls=%fused_computation.14 | convolution fusion | flops 12888047616 | bytes 20971520 | tf_op jit(solution)/shard_map/dot_general | solution.py:408
  520.4 10.0 %add_convert_fusion.4 = bf16[512,2048]{1,0:T(8,128)(2,1)} fusion(f32[512,2048]{1,0:T(8,128)S(1)} %fusion.52, bf16[2048,2048]{1,0:T(8,128)(2,1)} %all-gather.8.cloned.1.call-done, bf16[2048,2048]{1,0:T(8,128)(2,1)} %hidden_back.7), kind=kOutput, calls=%fused_computation.76 | convolution fusion | flops 4297064448 | bytes 16777216 | tf_op jit(solution)/shard_map/dot_general | solution.py:414
  540.5 24.6 %convolution_convert_fusion = bf16[2048,2048]{1,0:T(8,128)(2,1)} fusion(bf16[2048,2048]{1,0:T(8,128)(2,1)} %pad_maximum_fusion.1, bf16[2048,2048]{1,0:T(8,128)(2,1)} %hidden_back.7), kind=kOutput, calls=%fused_computation.11 | convolution fusion | flops 17184063488 | bytes 25165824 | tf_op jit(solution)/shard_map/dot_general | solution.py:408
  571.2 10.0 %add_convert_fusion.3 = bf16[512,2048]{1,0:T(8,128)(2,1)} fusion(f32[512,2048]{1,0:T(8,128)S(1)} %fusion.50, bf16[2048,2048]{1,0:T(8,128)(2,1)} %all-gather.8.cloned.1.call-done, bf16[2048,2048]{1,0:T(8,128)(2,1)} %hidden_back.7), kind=kOutput, calls=%fused_computation.75 | convolution fusion | flops 4297064448 | bytes 16777216 | tf_op jit(solution)/shard_map/dot_general | solution.py:414
  602.5 11.3 %fusion.46 = f32[1024,2048]{1,0:T(8,128)} fusion(bf16[2048,1536]{1,0:T(8,128)(2,1)} %columns_sorted.1, bf16[2048,1536]{1,0:T(8,128)(2,1)S(1)} %bitcast.74), kind=kOutput, calls=%fused_computation.88 | convolution fusion | flops 6442450944 | bytes 17825792 | tf_op jit(solution)/shard_map/dot_general | solution.py:414
  613.8 16.2 %add_convert_fusion = bf16[1024,2048]{1,0:T(8,128)(2,1)} fusion(f32[1024,2048]{1,0:T(8,128)} %fusion.46, bf16[2048,2048]{1,0:T(8,128)(2,1)} %all-gather.8.cloned.1.call-done, bf16[2048,2048]{1,0:T(8,128)(2,1)S(1)} %bitcast.72), kind=kOutput, calls=%fused_computation.5 | convolution fusion | flops 8594128896 | bytes 25165824 | tf_op jit(solution)/shard_map/dot_general | solution.py:414
  648.4 26.0 %reduce-scatter.11.cloned.1.call-done = bf16[256,2048]{1,0:T(8,128)(2,1)} async-done(((bf16[2048,2048]{1,0:T(8,128)(2,1)}), bf16[256,2048]{1,0:T(8,128)(2,1)}) %reduce-scatter.11.cloned.1.call-update) | async-done | bytes 1048592 | tf_op jit(solution)/shard_map/reduce_scatter | solution.py:497
  (288 shorter events, 306.3 us)
Async XLA Ops:
  7.2 58.5 %all-gather.6.cloned.1.call-start = ((), (), s32[]{:S(2)}) async-start(), calls=%async_computation.5 | async-start | bytes 7077888 | tf_op jit(solution)/shard_map/all_gather | solution.py:527
  8.0 113.9 %all-gather.8.cloned.1.call-start = ((), (), s32[]{:S(2)}) async-start(), calls=%async_computation.6 | async-start | bytes 9437184 | tf_op jit(solution)/shard_map/all_gather | solution.py:531
  12.6 165.0 %all-gather.10.cloned.1.call-start = ((), (), s32[]{:S(2)}) async-start(), calls=%async_computation.7 | async-start | bytes 9437184 | tf_op jit(solution)/shard_map/all_gather | solution.py:532
  13.3 279.1 %all-gather.12.cloned.1.call-start = ((), (), s32[]{:S(2)}) async-start(), calls=%async_computation.8 | async-start | bytes 2359296 | tf_op jit(solution)/shard_map/all_gather | solution.py:533
  13.3 51.0 %collective-permute-start = (bf16[512,2048]{1,0:T(8,128)(2,1)}, bf16[512,2048]{1,0:T(8,128)(2,1)}, u32[]{:S(2)}, u32[]{:S(2)}) collective-permute-start(bf16[512,2048]{1,0:T(8,128)(2,1)} %normalize.1), channel_id=1, source_target_pairs={{0,1},{1,2},{2,3},{3,0},{4,5},{5,6},{6,7},{7,4},{8,9},{9,10},{10,1... | collective-permute-start | bytes 6291464 | tf_op jit(solution)/shard_map/ppermute | solution.py:420
  65.7 48.9 %collective-permute-start.1 = (bf16[512,2048]{1,0:T(8,128)(2,1)}, bf16[512,2048]{1,0:T(8,128)(2,1)}, u32[]{:S(2)}, u32[]{:S(2)}) collective-permute-start(bf16[512,2048]{1,0:T(8,128)(2,1)} %collective-permute-done), channel_id=1, source_target_pairs={{0,1},{1,2},{2,3},{3,0},{4,5},{5,6},{6,7},{7,4},{8,9},{9,10},{10,1... | collective-permute-start | bytes 6291464 | tf_op jit(solution)/shard_map/ppermute | solution.py:420
  114.6 48.5 %collective-permute-start.2 = (bf16[512,2048]{1,0:T(8,128)(2,1)}, bf16[512,2048]{1,0:T(8,128)(2,1)}, u32[]{:S(2)}, u32[]{:S(2)}) collective-permute-start(bf16[512,2048]{1,0:T(8,128)(2,1)} %collective-permute-done.1), channel_id=1, source_target_pairs={{0,1},{1,2},{2,3},{3,0},{4,5},{5,6},{6,7},{7,4},{8,9},{9,10},{10,1... | collective-permute-start | bytes 6291464 | tf_op jit(solution)/shard_map/ppermute | solution.py:420
  163.1 49.0 %collective-permute-start.3 = (bf16[512,2048]{1,0:T(8,128)(2,1)S(1)}, bf16[512,2048]{1,0:T(8,128)(2,1)}, u32[]{:S(2)}, u32[]{:S(2)}) collective-permute-start(bf16[512,2048]{1,0:T(8,128)(2,1)S(1)} %copy-done), channel_id=1, source_target_pairs={{0,1},{1,2},{2,3},{4,5},{5,6},{6,7},{8,9},{9,10},{10,11},{12,13},{... | collective-permute-start | bytes 6291464 | tf_op jit(solution)/shard_map/ppermute | solution.py:420
  165.7 47.0 %collective-permute-start.4 = (bf16[512,2048]{1,0:T(8,128)(2,1)S(1)}, bf16[512,2048]{1,0:T(8,128)(2,1)}, u32[]{:S(2)}, u32[]{:S(2)}) collective-permute-start(bf16[512,2048]{1,0:T(8,128)(2,1)S(1)} %copy-done), channel_id=1, source_target_pairs={{1,0},{2,1},{3,2},{5,4},{6,5},{7,6},{9,8},{10,9},{11,10},{13,12},{... | collective-permute-start | bytes 6291464 | tf_op jit(solution)/shard_map/ppermute | solution.py:420
  212.7 52.3 %collective-permute-start.5 = (bf16[512,2048]{1,0:T(8,128)(2,1)}, bf16[512,2048]{1,0:T(8,128)(2,1)}, u32[]{:S(2)}, u32[]{:S(2)}) collective-permute-start(bf16[512,2048]{1,0:T(8,128)(2,1)} %collective-permute-done.3), channel_id=1, source_target_pairs={{1,2},{2,3},{5,6},{6,7},{9,10},{10,11},{13,14},{14,15},{17,18},{18... | collective-permute-start | bytes 6291464 | tf_op jit(solution)/shard_map/ppermute | solution.py:420
  214.6 50.4 %collective-permute-start.6 = (bf16[512,2048]{1,0:T(8,128)(2,1)}, bf16[512,2048]{1,0:T(8,128)(2,1)}, u32[]{:S(2)}, u32[]{:S(2)}) collective-permute-start(bf16[512,2048]{1,0:T(8,128)(2,1)} %collective-permute-done.4), channel_id=1, source_target_pairs={{1,0},{2,1},{5,4},{6,5},{9,8},{10,9},{13,12},{14,13},{17,16},{18,1... | collective-permute-start | bytes 6291464 | tf_op jit(solution)/shard_map/ppermute | solution.py:420
  215.9 49.1 %collective-permute-start.7 = (bf16[512,2048]{1,0:T(8,128)(2,1)}, bf16[512,2048]{1,0:T(8,128)(2,1)}, u32[]{:S(2)}, u32[]{:S(2)}) collective-permute-start(bf16[512,2048]{1,0:T(8,128)(2,1)} %convolution_convert_fusion.8), channel_id=1, source_target_pairs={{0,1},{4,5},{8,9},{12,13},{16,17},{20,21},{24,25},{28,29}} | collective-permute-start | bytes 6291464 | tf_op jit(solution)/shard_map/ppermute | solution.py:420
  224.5 265.4 %reduce-scatter.5.cloned.1.call-start = ((), (), s32[]{:S(2)}) async-start(), calls=%async_computation.9 | async-start | bytes 9437184 | tf_op jit(solution)/shard_map/reduce_scatter | solution.py:497
  271.0 53.2 %collective-permute-start.11 = (bf16[512,2048]{1,0:T(8,128)(2,1)}, bf16[512,2048]{1,0:T(8,128)(2,1)}, u32[]{:S(2)}, u32[]{:S(2)}) collective-permute-start(bf16[512,2048]{1,0:T(8,128)(2,1)} %get-tuple-element.412), channel_id=1, source_target_pairs={{0,1},{1,2},{4,5},{5,6},{8,9},{9,10},{12,13},{13,14},{16,17},{17,1... | collective-permute-start | bytes 6291464 | tf_op jit(solution)/shard_map/ppermute | solution.py:420
  275.4 48.8 %collective-permute-start.12 = (bf16[512,2048]{1,0:T(8,128)(2,1)}, bf16[512,2048]{1,0:T(8,128)(2,1)}, u32[]{:S(2)}, u32[]{:S(2)}) collective-permute-start(bf16[512,2048]{1,0:T(8,128)(2,1)} %get-tuple-element.411), channel_id=1, source_target_pairs={{2,1},{3,2},{6,5},{7,6},{10,9},{11,10},{14,13},{15,14},{18,17},{19... | collective-permute-start | bytes 6291464 | tf_op jit(solution)/shard_map/ppermute | solution.py:420
  277.3 46.9 %collective-permute-start.10 = (bf16[512,2048]{1,0:T(8,128)(2,1)}, bf16[512,2048]{1,0:T(8,128)(2,1)}, u32[]{:S(2)}, u32[]{:S(2)}) collective-permute-start(bf16[512,2048]{1,0:T(8,128)(2,1)} %collective-permute-done.6), channel_id=1, source_target_pairs={{1,0},{5,4},{9,8},{13,12},{17,16},{21,20},{25,24},{29,28}} | collective-permute-start | bytes 6291464 | tf_op jit(solution)/shard_map/ppermute | solution.py:420
  328.7 48.1 %collective-permute-start.14 = (bf16[512,2048]{1,0:T(8,128)(2,1)}, bf16[512,2048]{1,0:T(8,128)(2,1)}, u32[]{:S(2)}, u32[]{:S(2)}) collective-permute-start(bf16[512,2048]{1,0:T(8,128)(2,1)} %add_convert_fusion.7), channel_id=1, source_target_pairs={{1,0},{2,1},{3,2},{5,4},{6,5},{7,6},{9,8},{10,9},{11,10},{13,12},{... | collective-permute-start | bytes 6291464 | tf_op jit(solution)/shard_map/ppermute | solution.py:420
  334.4 49.3 %collective-permute-start.13 = (bf16[512,2048]{1,0:T(8,128)(2,1)}, bf16[512,2048]{1,0:T(8,128)(2,1)}, u32[]{:S(2)}, u32[]{:S(2)}) collective-permute-start(bf16[512,2048]{1,0:T(8,128)(2,1)} %add_convert_fusion.8), channel_id=1, source_target_pairs={{0,1},{1,2},{2,3},{4,5},{5,6},{6,7},{8,9},{9,10},{10,11},{12,13},{... | collective-permute-start | bytes 6291464 | tf_op jit(solution)/shard_map/ppermute | solution.py:420
  383.7 197.6 %reduce-scatter.7.cloned.1.call-start = ((), (), s32[]{:S(2)}) async-start(), calls=%async_computation.10 | async-start | bytes 2359296 | tf_op jit(solution)/shard_map/reduce_scatter | solution.py:497
  383.7 48.9 %collective-permute-start.15 = (bf16[512,2048]{1,0:T(8,128)(2,1)}, bf16[512,2048]{1,0:T(8,128)(2,1)S(1)}, u32[]{:S(2)}, u32[]{:S(2)}) collective-permute-start(bf16[512,2048]{1,0:T(8,128)(2,1)} %convolution_convert_fusion.5), channel_id=1, source_target_pairs={{0,1},{1,2},{2,3},{3,0},{4,5},{5,6},{6,7},{7,4},{8,9},{9,10},{10,1... | collective-permute-start | bytes 6291464 | tf_op jit(solution)/shard_map/ppermute | solution.py:420
  436.4 53.4 %collective-permute-start.16 = (bf16[512,2048]{1,0:T(8,128)(2,1)}, bf16[512,2048]{1,0:T(8,128)(2,1)}, u32[]{:S(2)}, u32[]{:S(2)}) collective-permute-start(bf16[512,2048]{1,0:T(8,128)(2,1)} %add_convert_fusion.6), channel_id=1, source_target_pairs={{0,1},{1,2},{2,3},{3,0},{4,5},{5,6},{6,7},{7,4},{8,9},{9,10},{10,1... | collective-permute-start | bytes 6291464 | tf_op jit(solution)/shard_map/ppermute | solution.py:420
  495.0 135.1 %reduce-scatter.9.cloned.1.call-start = ((), (), s32[]{:S(2)}) async-start(), calls=%async_computation.11 | async-start | bytes 7077888 | tf_op jit(solution)/shard_map/reduce_scatter | solution.py:497
  538.5 135.9 %reduce-scatter.11.cloned.1.call-start = ((), (), s32[]{:S(2)}) async-start(), calls=%async_computation.12 | async-start | bytes 9437184 | tf_op jit(solution)/shard_map/reduce_scatter | solution.py:497
  584.3 45.8 %collective-permute-start.19 = (bf16[512,2048]{1,0:T(8,128)(2,1)S(1)}, bf16[512,2048]{1,0:T(8,128)(2,1)S(1)}, u32[]{:S(2)}, u32[]{:S(2)}) collective-permute-start(bf16[512,2048]{1,0:T(8,128)(2,1)S(1)} %add_convert_fusion.2), channel_id=1, source_target_pairs={{0,1},{1,2},{2,3},{3,0},{4,5},{5,6},{6,7},{7,4},{8,9},{9,10},{10,1... | collective-permute-start | bytes 6291464 | tf_op jit(solution)/shard_map/ppermute | solution.py:420
  (65 other events, 910.6 us)
Sparse Core Ops, SparseCore 0:
  10.0 48.4 all-gather.5
  60.4 54.3 all-gather.7
  116.7 55.9 all-gather.9
  224.6 29.8 all-gather.11
  383.8 77.7 reduce-scatter.4
  495.1 38.8 reduce-scatter.6
  538.6 60.5 reduce-scatter.8
  603.1 71.2 reduce-scatter.10

commit v9 on v7

--- a/solution.py
+++ b/solution.py
@@ -360,28 +360,6 @@
     )(x, gain[None, :], shift_in[None, :])
 
 
-def add_pair_kernel(a_ref, b_ref, c_ref, d_ref, ab_ref, cd_ref):
-    ab_ref[...] = (a_ref[...].astype(jnp.float32) + b_ref[...].astype(jnp.float32)).astype(
-        jnp.bfloat16
-    )
-    cd_ref[...] = (c_ref[...].astype(jnp.float32) + d_ref[...].astype(jnp.float32)).astype(
-        jnp.bfloat16
-    )
-
-
-def add_pair(a, b, c, d):
-    rows, width = a.shape
-    block = pl.BlockSpec((128, width), lambda i: (i, 0))
-    return pl.pallas_call(
-        add_pair_kernel,
-        grid=(rows // 128,),
-        in_specs=[block] * 4,
-        out_specs=[block] * 2,
-        out_shape=[jax.ShapeDtypeStruct((rows, width), jnp.bfloat16)] * 2,
-        name="add_pair",
-    )(a, b, c, d)
-
-
 def columns_sorted_kernel(weight_ref, out_ref):
     for c in range(3):
         out_ref[:, c * PAIR : (c + 1) * PAIR] = weight_ref[c]
@@ -486,9 +464,10 @@
         n, k = lax.axis_size("tensor"), self.k
         mine_up, mine_down = self.parts[k], self.parts[n - k]
         if k > 1:
-            mine_up, mine_down = add_pair(mine_up, self.up, mine_down, self.down)
-        self.up = shift(mine_up, [(i, i + 1) for i in range(k)])
-        self.down = shift(mine_down, [(i, i - 1) for i in range(n - k, n)])
+            mine_up = mine_up.astype(jnp.float32) + self.up.astype(jnp.float32)
+            mine_down = mine_down.astype(jnp.float32) + self.down.astype(jnp.float32)
+        self.up = shift(mine_up.astype(jnp.bfloat16), [(i, i + 1) for i in range(k)])
+        self.down = shift(mine_down.astype(jnp.bfloat16), [(i, i - 1) for i in range(n - k, n)])
         self.k = k + 1
 
     def total(self):

time: 788 us -> 735 us (0.933)
  starting transfers between devices: 93.2 us -> 61.6 us
  waiting for transfers between devices: 117 us -> 101 us
  other arithmetic: 90.9 us -> 104 us
  Pallas kernels: 164 us -> 151 us
    ppermute x21, starting transfers between devices: 88.1 us -> 56.7 us  [shift(): return lax.ppermute(x, 'tensor', pairs)]
    ppermute x21, waiting for transfers between devices: 74.3 us -> 54.8 us  [shift(): return lax.ppermute(x, 'tensor', pairs)]
    convert_element_type x0 -> x3, other arithmetic: none -> 14.9 us  [the longest x2 10.4 us: step(): mine_down.astype(jnp.bfloat16)]
    pallas_call x2 -> x0, Pallas kernels: 12.1 us -> none  [add_pair(): pl.pallas_call(add_pair_kernel, grid=(rows // 128,), in_specs=[block] * 4...]
    unnamed x141 -> x137, local copies, waits for them, and re-layouts: 17.6 us -> 14.6 us
  transfers between devices with their start and end apart: 30 -> 30, of which waited for: 10 -> 10; matrix products, arithmetic and copies ran while one was open for 44% -> 48% of each run, Pallas kernels for 20% -> 21%
where the time goes in v9:
time: 735 us; the launch traced here: 725 us
  matrix products  246 us (33%)
  Pallas kernels  151 us (21%)
  other arithmetic  104 us (14%)
  waiting for transfers between devices  101 us (14%)
  starting transfers between devices  61.6 us (8%)
  local copies, waits for them, and re-layouts  29.6 us (4%)
  between operations  16.6 us (2%)
  blocking collectives  14.7 us (2%)
    dot_general x4, matrix products, contract_rows(): lax.dot_general(left, right, (((0,), (0,)), ((), ())), preferred_element_...  72.5 us
    dot_general x10, matrix products, contract_cols(): lax.dot_general(left, right, (((1,), (1,)), ((), ())), preferred_element_...  67.5 us
    pallas_call x2, Pallas kernels, attention_backward(): pl.pallas_call(kernel, grid_spec=pltpu.PrefetchScalarGridSpec(num_scalar_...  61 us
    ppermute x21, starting transfers between devices, shift(): return lax.ppermute(x, 'tensor', pairs)  56.7 us
    ppermute x21, waiting for transfers between devices, shift(): return lax.ppermute(x, 'tensor', pairs)  54.8 us
    dot_general x4, matrix products, widen(): jnp.dot(ring[k], full_up, preferred_element_type=jnp.float32) + full_ubias  43 us
    reduce_scatter x4, waiting for transfers between devices, scatter_low(): lax.psum_scatter(part.astype(jnp.bfloat16), axis, scatter_dimension=dim,...  42.2 us
    pallas_call x1, Pallas kernels, attention_forward(): pl.pallas_call(kernel, grid_spec=pltpu.PrefetchScalarGridSpec(num_scalar_...  36.8 us
  transfers between devices with their start and end apart: 30, of which 10 were waited for; matrix products, arithmetic and copies ran while one was open for 48% of the time, Pallas kernels for 21%

profile of v9, /device:TPU:0, one launch (start us, length us, event | category | flops | bytes accessed | tf_op | source)
XLA Modules:
  0.0 724.8 jit_solution(13049461997438693976)
XLA Ops:
  19.9 14.7 %all-reduce = bf16[3584]{0:T(1024)(128)(2,1)S(1)} all-reduce(bf16[3584]{0:T(1024)(128)(2,1)S(1)} %dynamic-update-slice), channel_id=2, replica_groups=mesh['dp'=8,'tensor'=4] {'dp'}, use_global_device_ids=true, to_apply=%add | all-reduce | flops 3584 | bytes 14336
  65.7 11.9 %columns_sorted.1 = bf16[2048,1536]{1,0:T(8,128)(2,1)} custom-call(bf16[3,2048,512]{2,1,0:T(8,128)(2,1)} %all-gather.6.cloned.1.call-done.weight_ref), custom_call_target="tpu_custom_call" | custom-call | tf_op jit(solution)/shard_map/columns_sorted/pallas_call | solution.py:371
  77.6 8.6 %fusion.64.refs_2_ = f32[512,1536]{1,0:T(8,128)} fusion(bf16[512,2048]{1,0:T(8,128)(2,1)} %collective-permute-done, bf16[2048,1536]{1,0:T(8,128)(2,1)} %columns_sorted.1), kind=kOutput, calls=%fused_computation.153 | convolution fusion | flops 3221225472 | bytes 11534336 | tf_op jit(solution)/shard_map/dot_general | solution.py:571
  91.3 23.3 %collective-permute-done.1 = bf16[512,2048]{1,0:T(8,128)(2,1)} collective-permute-done((bf16[512,2048]{1,0:T(8,128)(2,1)}, bf16[512,2048]{1,0:T(8,128)(2,1)}, u32[]{:S(2)}, u32[]{:S(2)}) %collective-permute-start.1) | collective-permute-done | bytes 2097184 | tf_op jit(solution)/shard_map/ppermute | solution.py:420
  121.8 8.4 %fusion.66 = f32[512,2048]{1,0:T(8,128)S(1)} fusion(bf16[512,2048]{1,0:T(8,128)(2,1)} %normalize.1, bf16[2048,2048]{1,0:T(8,128)(2,1)} %all-gather.8.cloned.1.call-done), kind=kOutput, calls=%fused_computation.155 | convolution fusion | flops 4294967296 | bytes 14680064 | tf_op jit(solution)/shard_map/dot_general | solution.py:574
  138.0 16.4 %multiply_convert_fusion.1 = (bf16[512,2048]{1,0:T(8,128)(2,1)}, f32[512,2048]{1,0:T(8,128)}, f32[512,2048]{1,0:T(8,128)}, bf16[512,2048]{1,0:T(8,128)(2,1)}, f32[512,2048]{1,0:T(8,128)}, /*index=5*/bf16[512,2048]{1,0:T(8,128)(2,1)}) fusion(f32[2048]{0:T(1024)S(1)} %bitcast.86, f32[512,2048]{1,0:T(8,128)} %fusion.67, f32[512,2048]{1,0:T(8,128)S(1)} %fusion.66, ...), kind=kOutput, calls=%fused_computation.82 | convolution fusion | flops 4357881856 | bytes 37756928 | tf_op jit(solution)/shard_map/dot_general | solution.py:574
  154.3 8.7 %collective-permute-done.2 = bf16[512,2048]{1,0:T(8,128)(2,1)} collective-permute-done((bf16[512,2048]{1,0:T(8,128)(2,1)}, bf16[512,2048]{1,0:T(8,128)(2,1)}, u32[]{:S(2)}, u32[]{:S(2)}) %collective-permute-start.2) | collective-permute-done | bytes 2097184 | tf_op jit(solution)/shard_map/ppermute | solution.py:420
  167.2 10.5 %multiply_convert_fusion = (bf16[512,2048]{1,0:T(8,128)(2,1)}, f32[512,2048]{1,0:T(8,128)}) fusion(f32[2048]{0:T(1024)S(1)} %bitcast.87, bf16[512,2048]{1,0:T(8,128)(2,1)} %collective-permute-done.2, bf16[2048,2048]{1,0:T(8,128)(2,1)S(1)} %copy-done.53), kind=kOutput, calls=%fused_computation.81 | convolution fusion | flops 4315938816 | bytes 16785408 | tf_op jit(solution)/shard_map/dot_general | solution.py:574
  177.7 10.0 %convolution_convert_fusion.6 = bf16[512,2048]{1,0:T(8,128)(2,1)} fusion(bf16[512,2048]{1,0:T(8,128)(2,1)} %get-tuple-element.278, bf16[2048,2048]{1,0:T(8,128)(2,1)} %all-gather.10.cloned.1.call-done.weight_ref), kind=kOutput, calls=%fused_computation.92 | convolution fusion | flops 4296015872 | bytes 12582912 | tf_op jit(solution)/shard_map/dot_general | solution.py:579
  227.6 36.8 %attend.1 = (bf16[2048,512]{1,0:T(8,128)(2,1)}, bf16[2048,512]{1,0:T(8,128)(2,1)}, bf16[2048,512]{1,0:T(8,128)(2,1)}, bf16[2048,512]{1,0:T(8,128)(2,1)}, f32[4,2,2048]{2,1,0:T(2,128)S(1)}) custom-call(s32[8]{0:T(128)S(1)} %get-tuple-element.240.refs_0_, s32[8]{0:T(128)S(1)} %get-tuple-element.241.refs_1_, f32[512,1536]{1,0:T(8,128)} %fusion.64.refs_2_, ...), custom_call_target="tpu_custom_call" | custom-call | tf_op jit(solution)/shard_map/attend/pallas_call | solution.py:157
  280.9 8.7 %hidden_back.4.refs_0_ = bf16[2048,2048]{1,0:T(8,128)(2,1)} custom-call(bf16[512,2048]{1,0:T(8,128)(2,1)S(1)} %copy-done, bf16[2048,2048]{1,0:T(8,128)(2,1)} %all-gather.10.cloned.1.call-done.weight_ref, f32[512,2048]{1,0:T(8,128)S(1)} %copy-done.16), custom_call_target="tpu_custom_call" | custom-call | flops 4294967296 | bytes 8388608 | tf_op jit(solution)/shard_map/hidden_back/pallas_call | solution.py:320
  355.7 19.8 %convolution_convert_fusion.1 = bf16[2048,2048]{1,0:T(8,128)(2,1)} fusion(bf16[2048,2048]{1,0:T(8,128)(2,1)S(1)} %pad_maximum_fusion, bf16[512,2048]{1,0:T(8,128)(2,1)S(1)} %copy-done, bf16[512,2048]{1,0:T(8,128)(2,1)S(1)} %broadcast_select_fusion.block_ref, bf16[512,2048]{1,0:T(8,128)(2,1)S(1)} %copy-done.6, ...), kind=kOutput, calls=%fused_computation.12 | convolution fusion | flops 17217617920 | bytes 25165824 | tf_op jit(solution)/shard_map/dot_general | solution.py:408
  392.6 30.3 %attend_back.2 = (bf16[2048,1536]{1,0:T(8,128)(2,1)}, f32[3,1,512]{2,1,0:T(1,128)S(1)}) custom-call(s32[8]{0:T(128)S(1)} %get-tuple-element.240.refs_0_, s32[8]{0:T(128)S(1)} %get-tuple-element.241.refs_1_, bf16[512,512]{1,0:T(8,128)(2,1)S(1)} %copy-done.23, bf16[512,512]{1,0:T(8,128)(2,1)S(1)} %copy-done.19, bf16[512,512]{1,0:T(8,128)(2,1)S(1)} %copy-done.21, ...), custom_call_target="tpu_custom_call" | custom-call | tf_op jit(solution)/shard_map/attend_back/pallas_call | solution.py:279
  422.9 9.4 %convolution_convert_fusion.4 = bf16[512,2048]{1,0:T(8,128)(2,1)} fusion(bf16[2048,512]{1,0:T(8,128)(2,1)S(1)} %copy-done.55, bf16[2048,2048]{1,0:T(8,128)(2,1)} %pad_maximum_fusion.2), kind=kOutput, calls=%fused_computation.90 | convolution fusion | flops 4296015872 | bytes 12582912 | tf_op jit(solution)/shard_map/dot_general | solution.py:408
  447.8 30.7 %attend_back.3 = (bf16[2048,1536]{1,0:T(8,128)(2,1)}, f32[3,1,512]{2,1,0:T(1,128)S(1)}) custom-call(s32[8]{0:T(128)S(1)} %get-tuple-element.240.refs_0_, s32[8]{0:T(128)S(1)} %get-tuple-element.241.refs_1_, bf16[512,512]{1,0:T(8,128)(2,1)S(1)} %copy-done.24, bf16[512,512]{1,0:T(8,128)(2,1)S(1)} %copy-done.20, ...), custom_call_target="tpu_custom_call", output_to_operand_aliasing={{0}: (14, {}), {1}: (15, {})} | custom-call | tf_op jit(solution)/shard_map/attend_back/pallas_call | solution.py:279
  478.5 8.4 %hidden_back.6.refs_0_ = bf16[2048,2048]{1,0:T(8,128)(2,1)} custom-call(bf16[512,2048]{1,0:T(8,128)(2,1)S(1)} %copy-done.5, bf16[2048,2048]{1,0:T(8,128)(2,1)} %all-gather.10.cloned.1.call-done.weight_ref, f32[512,2048]{1,0:T(8,128)S(1)} %copy-done.13, bf16[2048,2048]{1,0:T(8,128)(2,1)} %hidden_back.5.refs_0_), custom_call_target="tpu_custom_call", output_to_operand_aliasing={{}: (3, {})} | custom-call | flops 4294967296 | bytes 8388608 | tf_op jit(solution)/shard_map/hidden_back/pallas_call | solution.py:320
  487.0 8.3 %hidden_back.7 = bf16[2048,2048]{1,0:T(8,128)(2,1)} custom-call(bf16[512,2048]{1,0:T(8,128)(2,1)S(1)} %copy-done.3, bf16[2048,2048]{1,0:T(8,128)(2,1)} %all-gather.10.cloned.1.call-done.weight_ref, f32[512,2048]{1,0:T(8,128)S(1)} %copy-done.14, bf16[2048,2048]{1,0:T(8,128)(2,1)} %hidden_back.6.refs_0_), custom_call_target="tpu_custom_call", output_to_operand_aliasing={{}: (3, {})} | custom-call | flops 4294967296 | bytes 8388608 | tf_op jit(solution)/shard_map/hidden_back/pallas_call | solution.py:320
  500.4 23.9 %convolution_convert_fusion = bf16[2048,2048]{1,0:T(8,128)(2,1)} fusion(bf16[2048,2048]{1,0:T(8,128)(2,1)} %pad_maximum_fusion.1, bf16[2048,2048]{1,0:T(8,128)(2,1)} %hidden_back.7), kind=kOutput, calls=%fused_computation.11 | convolution fusion | flops 17184063488 | bytes 25165824 | tf_op jit(solution)/shard_map/dot_general | solution.py:408
  530.3 10.0 %add_convert_fusion.4 = bf16[512,2048]{1,0:T(8,128)(2,1)} fusion(f32[512,2048]{1,0:T(8,128)S(1)} %fusion.52, bf16[2048,2048]{1,0:T(8,128)(2,1)} %all-gather.8.cloned.1.call-done, bf16[2048,2048]{1,0:T(8,128)(2,1)} %hidden_back.7), kind=kOutput, calls=%fused_computation.76 | convolution fusion | flops 4297064448 | bytes 16777216 | tf_op jit(solution)/shard_map/dot_general | solution.py:414
  543.7 19.4 %convolution_convert_fusion.3 = bf16[2048,1536]{1,0:T(8,128)(2,1)} fusion(bf16[2048,2048]{1,0:T(8,128)(2,1)} %pad_maximum_fusion.1, bf16[2048,1536]{1,0:T(8,128)(2,1)} %get-tuple-element.365), kind=kOutput, calls=%fused_computation.14 | convolution fusion | flops 12888047616 | bytes 20971520 | tf_op jit(solution)/shard_map/dot_general | solution.py:408
  569.1 9.9 %add_convert_fusion.3 = bf16[512,2048]{1,0:T(8,128)(2,1)} fusion(f32[512,2048]{1,0:T(8,128)S(1)} %fusion.50, bf16[2048,2048]{1,0:T(8,128)(2,1)} %all-gather.8.cloned.1.call-done, bf16[2048,2048]{1,0:T(8,128)(2,1)} %hidden_back.7), kind=kOutput, calls=%fused_computation.75 | convolution fusion | flops 4297064448 | bytes 16777216 | tf_op jit(solution)/shard_map/dot_general | solution.py:414
  605.5 10.9 %fusion.46 = f32[1024,2048]{1,0:T(8,128)} fusion(bf16[2048,1536]{1,0:T(8,128)(2,1)} %columns_sorted.1, bf16[2048,1536]{1,0:T(8,128)(2,1)S(1)} %bitcast.74), kind=kOutput, calls=%fused_computation.88 | convolution fusion | flops 6442450944 | bytes 17825792 | tf_op jit(solution)/shard_map/dot_general | solution.py:414
  616.4 14.6 %add_convert_fusion = bf16[1024,2048]{1,0:T(8,128)(2,1)} fusion(f32[1024,2048]{1,0:T(8,128)} %fusion.46, bf16[2048,2048]{1,0:T(8,128)(2,1)} %all-gather.8.cloned.1.call-done, bf16[2048,2048]{1,0:T(8,128)(2,1)S(1)} %bitcast.72), kind=kOutput, calls=%fused_computation.5 | convolution fusion | flops 8594128896 | bytes 25165824 | tf_op jit(solution)/shard_map/dot_general | solution.py:414
  637.1 42.2 %reduce-scatter.11.cloned.1.call-done.part_ref = bf16[256,1536]{1,0:T(8,128)(2,1)} async-done(((bf16[2048,1536]{1,0:T(8,128)(2,1)}), bf16[256,1536]{1,0:T(8,128)(2,1)}) %reduce-scatter.11.cloned.1.call-update) | async-done | bytes 786448 | tf_op jit(solution)/shard_map/reduce_scatter | solution.py:497
  (302 shorter events, 312.4 us)
Async XLA Ops:
  7.2 58.5 %all-gather.6.cloned.1.call-start = ((), (), s32[]{:S(2)}) async-start(), calls=%async_computation.5 | async-start | bytes 7077888 | tf_op jit(solution)/shard_map/all_gather | solution.py:527
  8.0 113.9 %all-gather.8.cloned.1.call-start = ((), (), s32[]{:S(2)}) async-start(), calls=%async_computation.6 | async-start | bytes 9437184 | tf_op jit(solution)/shard_map/all_gather | solution.py:531
  12.6 165.1 %all-gather.10.cloned.1.call-start = ((), (), s32[]{:S(2)}) async-start(), calls=%async_computation.7 | async-start | bytes 9437184 | tf_op jit(solution)/shard_map/all_gather | solution.py:532
  13.3 279.4 %all-gather.12.cloned.1.call-start = ((), (), s32[]{:S(2)}) async-start(), calls=%async_computation.8 | async-start | bytes 2359296 | tf_op jit(solution)/shard_map/all_gather | solution.py:533
  13.3 51.0 %collective-permute-start = (bf16[512,2048]{1,0:T(8,128)(2,1)}, bf16[512,2048]{1,0:T(8,128)(2,1)}, u32[]{:S(2)}, u32[]{:S(2)}) collective-permute-start(bf16[512,2048]{1,0:T(8,128)(2,1)} %normalize.1), channel_id=1, source_target_pairs={{0,1},{1,2},{2,3},{3,0},{4,5},{5,6},{6,7},{7,4},{8,9},{9,10},{10,1... | collective-permute-start | bytes 6291464 | tf_op jit(solution)/shard_map/ppermute | solution.py:420
  65.7 48.9 %collective-permute-start.1 = (bf16[512,2048]{1,0:T(8,128)(2,1)}, bf16[512,2048]{1,0:T(8,128)(2,1)}, u32[]{:S(2)}, u32[]{:S(2)}) collective-permute-start(bf16[512,2048]{1,0:T(8,128)(2,1)} %collective-permute-done), channel_id=1, source_target_pairs={{0,1},{1,2},{2,3},{3,0},{4,5},{5,6},{6,7},{7,4},{8,9},{9,10},{10,1... | collective-permute-start | bytes 6291464 | tf_op jit(solution)/shard_map/ppermute | solution.py:420
  114.6 48.5 %collective-permute-start.2 = (bf16[512,2048]{1,0:T(8,128)(2,1)}, bf16[512,2048]{1,0:T(8,128)(2,1)}, u32[]{:S(2)}, u32[]{:S(2)}) collective-permute-start(bf16[512,2048]{1,0:T(8,128)(2,1)} %collective-permute-done.1), channel_id=1, source_target_pairs={{0,1},{1,2},{2,3},{3,0},{4,5},{5,6},{6,7},{7,4},{8,9},{9,10},{10,1... | collective-permute-start | bytes 6291464 | tf_op jit(solution)/shard_map/ppermute | solution.py:420
  163.1 49.1 %collective-permute-start.3 = (bf16[512,2048]{1,0:T(8,128)(2,1)S(1)}, bf16[512,2048]{1,0:T(8,128)(2,1)}, u32[]{:S(2)}, u32[]{:S(2)}) collective-permute-start(bf16[512,2048]{1,0:T(8,128)(2,1)S(1)} %copy-done), channel_id=1, source_target_pairs={{0,1},{1,2},{2,3},{4,5},{5,6},{6,7},{8,9},{9,10},{10,11},{12,13},{... | collective-permute-start | bytes 6291464 | tf_op jit(solution)/shard_map/ppermute | solution.py:420
  165.7 47.0 %collective-permute-start.4 = (bf16[512,2048]{1,0:T(8,128)(2,1)S(1)}, bf16[512,2048]{1,0:T(8,128)(2,1)}, u32[]{:S(2)}, u32[]{:S(2)}) collective-permute-start(bf16[512,2048]{1,0:T(8,128)(2,1)S(1)} %copy-done), channel_id=1, source_target_pairs={{1,0},{2,1},{3,2},{5,4},{6,5},{7,6},{9,8},{10,9},{11,10},{13,12},{... | collective-permute-start | bytes 6291464 | tf_op jit(solution)/shard_map/ppermute | solution.py:420
  212.7 51.6 %collective-permute-start.5 = (bf16[512,2048]{1,0:T(8,128)(2,1)}, bf16[512,2048]{1,0:T(8,128)(2,1)}, u32[]{:S(2)}, u32[]{:S(2)}) collective-permute-start(bf16[512,2048]{1,0:T(8,128)(2,1)} %collective-permute-done.3), channel_id=1, source_target_pairs={{1,2},{2,3},{5,6},{6,7},{9,10},{10,11},{13,14},{14,15},{17,18},{18... | collective-permute-start | bytes 6291464 | tf_op jit(solution)/shard_map/ppermute | solution.py:420
  214.7 49.6 %collective-permute-start.6 = (bf16[512,2048]{1,0:T(8,128)(2,1)}, bf16[512,2048]{1,0:T(8,128)(2,1)}, u32[]{:S(2)}, u32[]{:S(2)}) collective-permute-start(bf16[512,2048]{1,0:T(8,128)(2,1)} %collective-permute-done.4), channel_id=1, source_target_pairs={{1,0},{2,1},{5,4},{6,5},{9,8},{10,9},{13,12},{14,13},{17,16},{18,1... | collective-permute-start | bytes 6291464 | tf_op jit(solution)/shard_map/ppermute | solution.py:420
  216.0 48.3 %collective-permute-start.7 = (bf16[512,2048]{1,0:T(8,128)(2,1)}, bf16[512,2048]{1,0:T(8,128)(2,1)}, u32[]{:S(2)}, u32[]{:S(2)}) collective-permute-start(bf16[512,2048]{1,0:T(8,128)(2,1)} %convolution_convert_fusion.8), channel_id=1, source_target_pairs={{0,1},{4,5},{8,9},{12,13},{16,17},{20,21},{24,25},{28,29}} | collective-permute-start | bytes 6291464 | tf_op jit(solution)/shard_map/ppermute | solution.py:420
  224.7 270.6 %reduce-scatter.5.cloned.1.call-start = ((), (), s32[]{:S(2)}) async-start(), calls=%async_computation.9 | async-start | bytes 9437184 | tf_op jit(solution)/shard_map/reduce_scatter | solution.py:497
  270.3 54.2 %collective-permute-start.11 = (bf16[512,2048]{1,0:T(8,128)(2,1)}, bf16[512,2048]{1,0:T(8,128)(2,1)}, u32[]{:S(2)}, u32[]{:S(2)}) collective-permute-start(bf16[512,2048]{1,0:T(8,128)(2,1)} %get-tuple-element.416), channel_id=1, source_target_pairs={{0,1},{1,2},{4,5},{5,6},{8,9},{9,10},{12,13},{13,14},{16,17},{17,1... | collective-permute-start | bytes 6291464 | tf_op jit(solution)/shard_map/ppermute | solution.py:420
  275.6 48.8 %collective-permute-start.12 = (bf16[512,2048]{1,0:T(8,128)(2,1)}, bf16[512,2048]{1,0:T(8,128)(2,1)}, u32[]{:S(2)}, u32[]{:S(2)}) collective-permute-start(bf16[512,2048]{1,0:T(8,128)(2,1)} %get-tuple-element.415), channel_id=1, source_target_pairs={{2,1},{3,2},{6,5},{7,6},{10,9},{11,10},{14,13},{15,14},{18,17},{19... | collective-permute-start | bytes 6291464 | tf_op jit(solution)/shard_map/ppermute | solution.py:420
  277.6 46.9 %collective-permute-start.10 = (bf16[512,2048]{1,0:T(8,128)(2,1)}, bf16[512,2048]{1,0:T(8,128)(2,1)}, u32[]{:S(2)}, u32[]{:S(2)}) collective-permute-start(bf16[512,2048]{1,0:T(8,128)(2,1)} %collective-permute-done.6), channel_id=1, source_target_pairs={{1,0},{5,4},{9,8},{13,12},{17,16},{21,20},{25,24},{29,28}} | collective-permute-start | bytes 6291464 | tf_op jit(solution)/shard_map/ppermute | solution.py:420
  329.0 47.8 %collective-permute-start.14 = (bf16[512,2048]{1,0:T(8,128)(2,1)}, bf16[512,2048]{1,0:T(8,128)(2,1)}, u32[]{:S(2)}, u32[]{:S(2)}) collective-permute-start(bf16[512,2048]{1,0:T(8,128)(2,1)} %add_convert_fusion.7), channel_id=1, source_target_pairs={{1,0},{2,1},{3,2},{5,4},{6,5},{7,6},{9,8},{10,9},{11,10},{13,12},{... | collective-permute-start | bytes 6291464 | tf_op jit(solution)/shard_map/ppermute | solution.py:420
  334.8 48.9 %collective-permute-start.13 = (bf16[512,2048]{1,0:T(8,128)(2,1)}, bf16[512,2048]{1,0:T(8,128)(2,1)}, u32[]{:S(2)}, u32[]{:S(2)}) collective-permute-start(bf16[512,2048]{1,0:T(8,128)(2,1)} %add_convert_fusion.8), channel_id=1, source_target_pairs={{0,1},{1,2},{2,3},{4,5},{5,6},{6,7},{8,9},{9,10},{10,11},{12,13},{... | collective-permute-start | bytes 6291464 | tf_op jit(solution)/shard_map/ppermute | solution.py:420
  383.7 156.6 %reduce-scatter.7.cloned.1.call-start = ((), (), s32[]{:S(2)}) async-start(), calls=%async_computation.10 | async-start | bytes 2359296 | tf_op jit(solution)/shard_map/reduce_scatter | solution.py:497
  383.8 48.5 %collective-permute-start.15 = (bf16[512,2048]{1,0:T(8,128)(2,1)}, bf16[512,2048]{1,0:T(8,128)(2,1)}, u32[]{:S(2)}, u32[]{:S(2)}) collective-permute-start(bf16[512,2048]{1,0:T(8,128)(2,1)} %convolution_convert_fusion.5), channel_id=1, source_target_pairs={{0,1},{1,2},{2,3},{3,0},{4,5},{5,6},{6,7},{7,4},{8,9},{9,10},{10,1... | collective-permute-start | bytes 6291464 | tf_op jit(solution)/shard_map/ppermute | solution.py:420
  436.8 58.5 %collective-permute-start.16 = (bf16[512,2048]{1,0:T(8,128)(2,1)}, bf16[512,2048]{1,0:T(8,128)(2,1)}, u32[]{:S(2)}, u32[]{:S(2)}) collective-permute-start(bf16[512,2048]{1,0:T(8,128)(2,1)} %add_convert_fusion.6), channel_id=1, source_target_pairs={{0,1},{1,2},{2,3},{3,0},{4,5},{5,6},{6,7},{7,4},{8,9},{9,10},{10,1... | collective-permute-start | bytes 6291464 | tf_op jit(solution)/shard_map/ppermute | solution.py:420
  440.9 190.1 %reduce-scatter.9.cloned.1.call-start = ((), (), s32[]{:S(2)}) async-start(), calls=%async_computation.11 | async-start | bytes 9437184 | tf_op jit(solution)/shard_map/reduce_scatter | solution.py:497
  541.0 138.3 %reduce-scatter.11.cloned.1.call-start = ((), (), s32[]{:S(2)}) async-start(), calls=%async_computation.12 | async-start | bytes 7077888 | tf_op jit(solution)/shard_map/reduce_scatter | solution.py:497
  634.9 59.4 %collective-permute-start.20 = (bf16[512,2048]{1,0:T(8,128)(2,1)}, bf16[512,2048]{1,0:T(8,128)(2,1)}, u32[]{:S(2)}, u32[]{:S(2)}) collective-permute-start(bf16[512,2048]{1,0:T(8,128)(2,1)} %add_convert_fusion.1), channel_id=1, source_target_pairs={{0,1},{1,2},{2,3},{3,0},{4,5},{5,6},{6,7},{7,4},{8,9},{9,10},{10,1... | collective-permute-start | bytes 6291464 | tf_op jit(solution)/shard_map/ppermute | solution.py:420
  (72 other events, 915.4 us)
Sparse Core Ops, SparseCore 0:
  10.0 48.4 all-gather.5
  60.4 54.3 all-gather.7
  116.7 55.9 all-gather.9
  224.8 29.6 all-gather.11
  383.8 77.7 reduce-scatter.4
  465.7 41.2 reduce-scatter.6
  541.1 72.5 reduce-scatter.8
  617.5 61.7 reduce-scatter.10
